TPU v7x, 32 devices: a whole 2x2x4 slice. The times are simulated.
32 devices in a mesh: slot: 4 (over y, x), seq: 8 (over z, core).
Axes of the slice: x: 2, y: 2, z: 4, core: 2. Of those that a mesh axis runs over, the one named last changes fastest.
Arguments:
- rows_in: bfloat16 [4, 2048, 2048], P('slot', 'seq'), may hold values from -6 to 6
- lengths: int32 [4], P('slot'), may hold values from 64 to 2048, as said below
- norm1_gain: bfloat16 [2048], P('seq'), may hold values from 0.5 to 1.5
- w_query: bfloat16 [2048, 2048], P('seq'), may hold values from -0.125 to 0.125
- w_key: bfloat16 [2048, 128], P('seq'), may hold values from -0.125 to 0.125
- w_value: bfloat16 [2048, 128], P('seq'), may hold values from -0.125 to 0.125
- w_out: bfloat16 [2048, 2048], P('seq'), may hold values from -0.5 to 0.5
- norm2_gain: bfloat16 [2048], P('seq'), may hold values from 0.5 to 1.5
- w_gate: bfloat16 [2048, 5632], P('seq'), may hold values from -0.125 to 0.125
- w_up: bfloat16 [2048, 5632], P('seq'), may hold values from -0.125 to 0.125
- w_down: bfloat16 [5632, 2048], P('seq'), may hold values from -0.078125 to 0.078125
- rows_cot: bfloat16 [4, 2048, 2048], P('slot', 'seq'), may hold values from -6 to 6
- kv_cot: bfloat16 [4, 2048, 256], P('slot', 'seq'), may hold values from -6 to 6
Outputs:
- rows: bfloat16 [4, 2048, 2048], P('slot', 'seq')
- shared_kv: bfloat16 [4, 2048, 256], P('slot', 'seq')
- input_grad: bfloat16 [4, 2048, 2048], P('slot', 'seq')
- norm1_gain_grad: float32 [2048], P('seq')
- w_query_grad: float32 [2048, 2048], P('seq')
- w_key_grad: float32 [2048, 128], P('seq')
- w_value_grad: float32 [2048, 128], P('seq')
- w_out_grad: float32 [2048, 2048], P('seq')
- norm2_gain_grad: float32 [2048], P('seq')
- w_gate_grad: float32 [2048, 5632], P('seq')
- w_up_grad: float32 [2048, 5632], P('seq')
- w_down_grad: float32 [5632, 2048], P('seq')
Inputs may be any that keep to these rules, and one draw needn't show every extreme that they name: `lengths`: one slot, drawn from the seed, has length 2048; the others lie between 64 and 2048.
All inputs are finite; a program needn't handle non-finite values.
Results may differ from a plain program's by a relative error of at most 0.02.
Values may be sent and summed in bfloat16 or wider, within the bound.
No kernel may reach another device: no remote copies, remote signals or barrier semaphores. Data moves between devices by JAX's collectives and lax.ppermute only.
A program may use at most 384 MiB of HBM per device.

v0:
```python
import jax
import jax.numpy as jnp
from jax import lax
from jax.sharding import PartitionSpec as P

WINDOW = 512


EPSILON = 1e-05
THETA = 10000.0
NEGATIVE = -1e30


def shifted(block, axis, distance):
    devices = range(lax.axis_size(axis))
    route = [(i - distance, i) for i in devices if i - distance in devices]
    return lax.ppermute(block, axis, route)


def rope_tables(positions, head_width):
    half_width = head_width // 2
    exponent = jnp.arange(half_width, dtype=jnp.float32) * (2.0 / head_width)
    frequency = THETA ** (-exponent)
    angles = positions.astype(jnp.float32)[:, None] * frequency[None, :]
    return (jnp.cos(angles), jnp.sin(angles))


def rotate(values, cosine_table, sine_table):
    half_width = values.shape[-1] // 2
    first_half = values[..., :half_width]
    second_half = values[..., half_width:]
    return jnp.concatenate(
        [
            first_half * cosine_table - second_half * sine_table,
            second_half * cosine_table + first_half * sine_table,
        ],
        axis=-1,
    )


def rms_scale(values):
    return lax.rsqrt(jnp.mean(values * values, axis=-1, keepdims=True) + EPSILON)


def window_mask(query_pos, key_pos, length):
    distance = query_pos[:, None] - key_pos[None, :]
    return (
        (key_pos[None, :] >= 0)
        & (key_pos[None, :] < length)
        & (distance >= 0)
        & (distance < WINDOW)
        & (query_pos[:, None] < length)
    )


def norm_back(grad_normed, unit_rows, scale_rows, gain_row):
    scaled = grad_normed * gain_row.astype(jnp.float32)
    return scale_rows * (scaled - unit_rows * jnp.mean(scaled * unit_rows, axis=-1, keepdims=True))


def shards(
    rows_in,
    lengths,
    norm1_gain,
    w_query,
    w_key,
    w_value,
    w_out,
    norm2_gain,
    w_gate,
    w_up,
    w_down,
    rows_cot,
    kv_cot,
):
    tok_count = rows_in.shape[1]
    head_width = w_key.shape[1]
    head_count = w_query.shape[1] // head_width
    hop_count = WINDOW // tok_count
    key_count = WINDOW + tok_count
    scaling = head_width ** (-0.5)
    gathered = (
        lax.all_gather(norm1_gain, "seq", axis=0, tiled=True),
        lax.all_gather(w_query, "seq", axis=0, tiled=True),
        lax.all_gather(w_key, "seq", axis=0, tiled=True),
        lax.all_gather(w_value, "seq", axis=0, tiled=True),
        lax.all_gather(w_out, "seq", axis=0, tiled=True),
        lax.all_gather(norm2_gain, "seq", axis=0, tiled=True),
        lax.all_gather(w_gate, "seq", axis=0, tiled=True),
        lax.all_gather(w_up, "seq", axis=0, tiled=True),
        lax.all_gather(w_down, "seq", axis=0, tiled=True),
    )
    gain_one, query_w, key_w, value_w, out_w, gain_two, gate_w, up_w, down_w = gathered
    first_row = lax.axis_index("seq") * tok_count
    query_pos = first_row + jnp.arange(tok_count, dtype=jnp.int32)
    seq_length = lengths[0]
    row_valid = (query_pos < seq_length).astype(jnp.float32)[:, None]
    query_valid = (query_pos < seq_length)[:, None, None]
    inputs = rows_in[0].astype(jnp.float32)
    scale_one = rms_scale(inputs)
    normed = (inputs * scale_one * gain_one.astype(jnp.float32)).astype(jnp.bfloat16)
    query_pre = jnp.dot(normed, query_w, preferred_element_type=jnp.float32)
    key_pre = jnp.dot(normed, key_w, preferred_element_type=jnp.float32)
    value_rows = jnp.dot(normed, value_w, preferred_element_type=jnp.float32).astype(jnp.bfloat16)
    cosine_table, sine_table = rope_tables(query_pos, head_width)
    queries = rotate(
        query_pre.reshape(tok_count, head_count, head_width),
        cosine_table[:, None, :],
        sine_table[:, None, :],
    ).astype(jnp.bfloat16)
    key_rows = rotate(key_pre, cosine_table, sine_table).astype(jnp.bfloat16)
    shared = jnp.concatenate([key_rows, value_rows], axis=1) * row_valid.astype(jnp.bfloat16)
    rim_list = []
    for hop_index in range(hop_count, 0, -1):
        rim_list.append(shifted(shared, "seq", hop_index))
    key_table = jnp.concatenate(rim_list + [shared], axis=0)
    key_part = key_table[:, :head_width]
    value_part = key_table[:, head_width:]
    key_pos = first_row - WINDOW + jnp.arange(key_count, dtype=jnp.int32)
    allowed = window_mask(query_pos, key_pos, seq_length)[:, None, :]
    allowed_float = allowed.astype(jnp.float32)
    flat_queries = queries.reshape(tok_count * head_count, head_width)

    def score_rows():
        raw_scores = jnp.dot(flat_queries, key_part.T, preferred_element_type=jnp.float32)
        raw_scores = raw_scores.reshape(tok_count, head_count, key_count) * scaling
        return jnp.where(allowed, raw_scores, NEGATIVE)

    masked = score_rows()
    row_max = jnp.max(masked, axis=-1, keepdims=True)
    exponent_rows = jnp.exp(masked - row_max) * allowed_float
    row_sum = jnp.sum(exponent_rows, axis=-1, keepdims=True)
    row_denom = jnp.where(query_valid, row_sum, 1.0)
    prob_rows = (exponent_rows / row_denom).astype(jnp.bfloat16)
    log_total = row_max + jnp.log(row_denom)
    flat_probs = prob_rows.reshape(tok_count * head_count, key_count)
    attended = jnp.dot(flat_probs, value_part, preferred_element_type=jnp.float32)
    attended = attended.reshape(tok_count, head_count * head_width).astype(jnp.bfloat16)
    middle = inputs + jnp.dot(attended, out_w, preferred_element_type=jnp.float32)
    scale_two = rms_scale(middle)
    normed_two = (middle * scale_two * gain_two.astype(jnp.float32)).astype(jnp.bfloat16)
    gate_out = jnp.dot(normed_two, gate_w, preferred_element_type=jnp.float32)
    up_out = jnp.dot(normed_two, up_w, preferred_element_type=jnp.float32)
    hidden = (jax.nn.silu(gate_out) * up_out).astype(jnp.bfloat16)
    result = middle + jnp.dot(hidden, down_w, preferred_element_type=jnp.float32) * row_valid
    back_set = (
        lax.all_gather(norm1_gain, "seq", axis=0, tiled=True),
        lax.all_gather(w_query, "seq", axis=0, tiled=True),
        lax.all_gather(w_key, "seq", axis=0, tiled=True),
        lax.all_gather(w_value, "seq", axis=0, tiled=True),
        lax.all_gather(w_out, "seq", axis=0, tiled=True),
        lax.all_gather(norm2_gain, "seq", axis=0, tiled=True),
        lax.all_gather(w_gate, "seq", axis=0, tiled=True),
        lax.all_gather(w_up, "seq", axis=0, tiled=True),
        lax.all_gather(w_down, "seq", axis=0, tiled=True),
    )
    gain_one, query_w, key_w, value_w, out_w, gain_two, gate_w, up_w, down_w = back_set
    out_grad = rows_cot[0].astype(jnp.float32)
    down_in = rows_cot[0] * row_valid.astype(jnp.bfloat16)
    grad_down = jnp.dot(hidden.T, down_in, preferred_element_type=jnp.float32)
    grad_hidden = jnp.dot(down_in, down_w.T, preferred_element_type=jnp.float32)
    sig_gate = jax.nn.sigmoid(gate_out)
    grad_gate = (grad_hidden * up_out * sig_gate * (1.0 + gate_out * (1.0 - sig_gate))).astype(
        jnp.bfloat16
    )
    grad_up = (grad_hidden * gate_out * sig_gate).astype(jnp.bfloat16)
    grad_gate_w = jnp.dot(normed_two.T, grad_gate, preferred_element_type=jnp.float32)
    grad_up_w = jnp.dot(normed_two.T, grad_up, preferred_element_type=jnp.float32)
    grad_normed_two = jnp.dot(grad_gate, gate_w.T, preferred_element_type=jnp.float32) + jnp.dot(
        grad_up, up_w.T, preferred_element_type=jnp.float32
    )
    unit_two = middle * scale_two
    grad_gain_two = jnp.sum(grad_normed_two * unit_two, axis=0)
    grad_middle = out_grad + norm_back(grad_normed_two, unit_two, scale_two, gain_two)
    branch_grad = grad_middle.astype(jnp.bfloat16)
    grad_out_w = jnp.dot(attended.T, branch_grad, preferred_element_type=jnp.float32)
    grad_attended = jnp.dot(branch_grad, out_w.T, preferred_element_type=jnp.float32).astype(
        jnp.bfloat16
    )
    flat_grad = grad_attended.reshape(tok_count * head_count, head_width)
    probs_float = jnp.exp(score_rows() - log_total) * allowed_float
    grad_probs = jnp.dot(flat_grad, value_part.T, preferred_element_type=jnp.float32)
    grad_probs = grad_probs.reshape(tok_count, head_count, key_count)
    grad_scores = probs_float * (
        grad_probs - jnp.sum(probs_float * grad_probs, axis=-1, keepdims=True)
    )
    flat_scores = grad_scores.astype(jnp.bfloat16).reshape(tok_count * head_count, key_count)
    grad_queries = jnp.dot(flat_scores, key_part, preferred_element_type=jnp.float32) * scaling
    grad_keys = jnp.dot(flat_scores.T, flat_queries, preferred_element_type=jnp.float32) * scaling
    grad_values = jnp.dot(flat_probs.T, flat_grad, preferred_element_type=jnp.float32)
    grad_table = jnp.concatenate([grad_keys, grad_values], axis=1)
    own_grad = grad_table[WINDOW:] + kv_cot[0].astype(jnp.float32)
    for hop_index in range(1, hop_count + 1):
        lower = (hop_count - hop_index) * tok_count
        own_grad = own_grad + shifted(
            grad_table[lower : lower + tok_count].astype(jnp.bfloat16), "seq", -hop_index
        ).astype(jnp.float32)
    own_grad = own_grad * row_valid
    grad_key_pre = rotate(own_grad[:, :head_width], cosine_table, -sine_table).astype(jnp.bfloat16)
    grad_value = own_grad[:, head_width:].astype(jnp.bfloat16)
    grad_query_pre = rotate(
        grad_queries.reshape(tok_count, head_count, head_width),
        cosine_table[:, None, :],
        -sine_table[:, None, :],
    )
    grad_query_pre = grad_query_pre.reshape(tok_count, head_count * head_width).astype(jnp.bfloat16)
    grad_query_w = jnp.dot(normed.T, grad_query_pre, preferred_element_type=jnp.float32)
    grad_key_w = jnp.dot(normed.T, grad_key_pre, preferred_element_type=jnp.float32)
    grad_value_w = jnp.dot(normed.T, grad_value, preferred_element_type=jnp.float32)
    grad_normed = (
        jnp.dot(grad_query_pre, query_w.T, preferred_element_type=jnp.float32)
        + jnp.dot(grad_key_pre, key_w.T, preferred_element_type=jnp.float32)
        + jnp.dot(grad_value, value_w.T, preferred_element_type=jnp.float32)
    )
    unit_one = inputs * scale_one
    grad_gain_one = jnp.sum(grad_normed * unit_one, axis=0)
    grad_inputs = grad_middle + norm_back(grad_normed, unit_one, scale_one, gain_one)
    shares = (
        lax.psum_scatter(
            grad_gain_one.astype(jnp.bfloat16), "seq", scatter_dimension=0, tiled=True
        ).astype(jnp.float32),
        lax.psum_scatter(
            grad_query_w.astype(jnp.bfloat16), "seq", scatter_dimension=0, tiled=True
        ).astype(jnp.float32),
        lax.psum_scatter(
            grad_key_w.astype(jnp.bfloat16), "seq", scatter_dimension=0, tiled=True
        ).astype(jnp.float32),
        lax.psum_scatter(
            grad_value_w.astype(jnp.bfloat16), "seq", scatter_dimension=0, tiled=True
        ).astype(jnp.float32),
        lax.psum_scatter(
            grad_out_w.astype(jnp.bfloat16), "seq", scatter_dimension=0, tiled=True
        ).astype(jnp.float32),
        lax.psum_scatter(
            grad_gain_two.astype(jnp.bfloat16), "seq", scatter_dimension=0, tiled=True
        ).astype(jnp.float32),
        lax.psum_scatter(
            grad_gate_w.astype(jnp.bfloat16), "seq", scatter_dimension=0, tiled=True
        ).astype(jnp.float32),
        lax.psum_scatter(
            grad_up_w.astype(jnp.bfloat16), "seq", scatter_dimension=0, tiled=True
        ).astype(jnp.float32),
        lax.psum_scatter(
            grad_down.astype(jnp.bfloat16), "seq", scatter_dimension=0, tiled=True
        ).astype(jnp.float32),
    )
    part_a, part_b, part_c, part_d, part_e, part_f, part_g, part_h, part_i = shares
    totals = (
        lax.psum(part_a.astype(jnp.bfloat16), "slot").astype(jnp.float32),
        lax.psum(part_b.astype(jnp.bfloat16), "slot").astype(jnp.float32),
        lax.psum(part_c.astype(jnp.bfloat16), "slot").astype(jnp.float32),
        lax.psum(part_d.astype(jnp.bfloat16), "slot").astype(jnp.float32),
        lax.psum(part_e.astype(jnp.bfloat16), "slot").astype(jnp.float32),
        lax.psum(part_f.astype(jnp.bfloat16), "slot").astype(jnp.float32),
        lax.psum(part_g.astype(jnp.bfloat16), "slot").astype(jnp.float32),
        lax.psum(part_h.astype(jnp.bfloat16), "slot").astype(jnp.float32),
        lax.psum(part_i.astype(jnp.bfloat16), "slot").astype(jnp.float32),
    )
    return (
        result.astype(jnp.bfloat16)[None],
        shared[None],
        grad_inputs.astype(jnp.bfloat16)[None],
        totals[0],
        totals[1],
        totals[2],
        totals[3],
        totals[4],
        totals[5],
        totals[6],
        totals[7],
        totals[8],
    )


def solution(mesh):
    placed = (
        P("slot", "seq", None),
        P("slot"),
        P("seq"),
        P("seq", None),
        P("seq", None),
        P("seq", None),
        P("seq", None),
        P("seq"),
        P("seq", None),
        P("seq", None),
        P("seq", None),
        P("slot", "seq", None),
        P("slot", "seq", None),
    )
    return jax.shard_map(
        shards,
        mesh=mesh,
        in_specs=placed,
        out_specs=(
            P("slot", "seq", None),
            P("slot", "seq", None),
            P("slot", "seq", None),
            P("seq"),
            P("seq", None),
            P("seq", None),
            P("seq", None),
            P("seq", None),
            P("seq"),
            P("seq", None),
            P("seq", None),
            P("seq", None),
        ),
        check_vma=False,
    )
```

profile of v0, /device:TPU:10, one launch (start us, length us, event | category | flops | bytes accessed | tf_op | source)
XLA Modules:
  0.0 2052.4 jit_solution(15873460140432739912)
XLA Ops:
  11.3 9.1 all-gather
  21.3 17.2 all_gather.39
  38.5 19.5 all_gather.38
  59.6 2.3 collective-permute-start.1
  61.9 3.1 collective-permute-start
  65.1 10.9 all-gather.1
  76.5 26.4 %all-gather.8.cloned.1.call-done = bf16[2048,2048]{1,0:T(8,128)(2,1)} async-done(((bf16[256,2048]{1,0:T(8,128)(2,1)}), bf16[2048,2048]{1,0:T(8,128)(2,1)}) %all-gather.8.cloned.1.call-update) | async-done | bytes 8388624 | tf_op jit(solution)/shard_map/all_gather | solution.py:84
  103.0 12.4 copy.43
  115.3 5.9 fusion.27
  121.6 2.3 fusion.1
  124.0 3.7 fusion
  128.6 3.7 divide_convert_fusion
  132.3 3.6 copy.46
  135.8 2.6 copy-done.1
  138.4 1.8 convolution_convert_fusion.5
  141.5 43.4 %all-gather.10.cloned.1.call-done = bf16[2048,2048]{1,0:T(8,128)(2,1)} async-done(((bf16[256,2048]{1,0:T(8,128)(2,1)}), bf16[2048,2048]{1,0:T(8,128)(2,1)}) %all-gather.10.cloned.1.call-update) | async-done | bytes 8388624 | tf_op jit(solution)/shard_map/all_gather | solution.py:87
  184.9 6.2 multiply_reduce_fusion.3
  191.4 196.1 %all-gather.12.cloned.1.call-done = bf16[2048,5632]{1,0:T(8,128)(2,1)} async-done(((bf16[256,5632]{1,0:T(8,128)(2,1)}), bf16[2048,5632]{1,0:T(8,128)(2,1)}) %all-gather.12.cloned.1.call-update) | async-done | bytes 23068688 | tf_op jit(solution)/shard_map/all_gather | solution.py:89
  387.5 13.8 fusion.84
  401.3 188.6 %all-gather.14.cloned.1.call-done = bf16[2048,5632]{1,0:T(8,128)(2,1)} async-done(((bf16[256,5632]{1,0:T(8,128)(2,1)}), bf16[2048,5632]{1,0:T(8,128)(2,1)}) %all-gather.14.cloned.1.call-update) | async-done | bytes 23068688 | tf_op jit(solution)/shard_map/all_gather | solution.py:90
  589.9 13.9 fusion.85
  603.8 188.4 %all-gather.16.cloned.1.call-done = bf16[5632,2048]{1,0:T(8,128)(2,1)} async-done(((bf16[704,2048]{1,0:T(8,128)(2,1)}), bf16[5632,2048]{1,0:T(8,128)(2,1)}) %all-gather.16.cloned.1.call-update) | async-done | bytes 23068688 | tf_op jit(solution)/shard_map/all_gather | solution.py:91
  792.3 18.6 multiply_convert_fusion.1
  810.9 12.5 fusion.86
  823.4 14.2 multiply_reduce_fusion.1
  837.6 2.2 multiply_add_fusion
  841.1 5.7 convolution_convert_fusion.6
  848.2 8.0 multiply_reduce_fusion
  857.0 5.8 multiply_convert_fusion
  863.9 1.7 copy-done.2
  865.6 3.9 fusion.88
  869.6 5.3 collective-permute-start.3
  875.0 1.9 collective-permute-start.2
  878.1 1.4 collective-permute-done.2
  879.6 1.8 fusion.65
  882.9 1.4 convolution_convert_fusion.7
  884.4 6.9 convolution_convert_fusion.3
  891.5 6.3 copy.49
  897.9 1.8 convolution_multiply_fusion
  899.7 2.7 fusion.82
  902.3 3.5 copy.60
  905.8 3.5 copy.59
  909.3 1.9 multiply_subtract_fusion
  912.3 5.8 convolution_convert_fusion.4
  918.3 12.8 convolution_convert_fusion.2
  931.2 12.7 convolution_convert_fusion.1
  944.0 13.4 convolution_convert_fusion
  957.8 75.5 %reduce-scatter.14.cloned.1.call-done = bf16[256,2048]{1,0:T(8,128)(2,1)} async-done(((bf16[2048,2048]{1,0:T(8,128)(2,1)}), bf16[256,2048]{1,0:T(8,128)(2,1)}) %reduce-scatter.14.cloned.1.call-update) | async-done | bytes 1048592 | tf_op jit(solution)/shard_map/reduce_scatter | solution.py:231
  1033.2 90.3 %reduce-scatter.8.cloned.1.call-done = bf16[256,2048]{1,0:T(8,128)(2,1)} async-done(((bf16[2048,2048]{1,0:T(8,128)(2,1)}), bf16[256,2048]{1,0:T(8,128)(2,1)}) %reduce-scatter.8.cloned.1.call-update) | async-done | bytes 1048592 | tf_op jit(solution)/shard_map/reduce_scatter | solution.py:222
  1123.5 228.0 %reduce-scatter.16.cloned.1.call-done = bf16[256,5632]{1,0:T(8,128)(2,1)} async-done(((bf16[2048,5632]{1,0:T(8,128)(2,1)}), bf16[256,5632]{1,0:T(8,128)(2,1)}) %reduce-scatter.16.cloned.1.call-update) | async-done | bytes 2883600 | tf_op jit(solution)/shard_map/reduce_scatter | solution.py:237
  1351.5 228.2 %reduce-scatter.18.cloned.1.call-done = bf16[256,5632]{1,0:T(8,128)(2,1)} async-done(((bf16[2048,5632]{1,0:T(8,128)(2,1)}), bf16[256,5632]{1,0:T(8,128)(2,1)}) %reduce-scatter.18.cloned.1.call-update) | async-done | bytes 2883600 | tf_op jit(solution)/shard_map/reduce_scatter | solution.py:240
  1579.7 228.0 %reduce-scatter.20.cloned.1.call-done = bf16[704,2048]{1,0:T(8,128)(2,1)} async-done(((bf16[5632,2048]{1,0:T(8,128)(2,1)}), bf16[704,2048]{1,0:T(8,128)(2,1)}) %reduce-scatter.20.cloned.1.call-update) | async-done | bytes 2883600 | tf_op jit(solution)/shard_map/reduce_scatter | solution.py:243
  1810.7 13.1 fusion.11
  1823.8 5.9 fusion.87
  1830.9 2.2 fusion.18
  1833.0 14.5 all-reduce.2
  1847.7 8.2 all-reduce.3
  1857.0 3.5 fusion.23
  1860.5 169.3 %all-reduce.7.cloned.1.call-done = (bf16[256,2048]{1,0:T(8,128)(2,1)}, bf16[256,128]{1,0:T(8,128)(2,1)}, bf16[256,128]{1,0:T(8,128)(2,1)}, bf16[256,2048]{1,0:T(...) async-done(((bf16[256,2048]{1,0:T(8,128)(2,1)}, bf16[256,128]{1,0:T(8,128)(2,1)}, bf16[256,128]{1,0:T(8,128)(2,1)}, ...) | async-done | bytes 10878992 | tf_op jit(solution)/shard_map/psum | solution.py:250
  2029.9 2.9 convert_element_type.249
  2034.2 1.6 convert_element_type.255
  2035.7 3.2 convert_element_type.259
  2038.9 3.2 convert_element_type.261
  2042.1 3.3 convert_element_type.263
  (195 shorter events, 24.3 us)
Async XLA Ops:
  7.2 95.8 %all-gather.8.cloned.1.call-start = ((), (), s32[]{:S(2)}) async-start(), calls=%async_computation.7 | async-start | bytes 9437184 | tf_op jit(solution)/shard_map/all_gather | solution.py:84
  7.9 177.0 %all-gather.10.cloned.1.call-start = ((), (), s32[]{:S(2)}) async-start(), calls=%async_computation.8 | async-start | bytes 9437184 | tf_op jit(solution)/shard_map/all_gather | solution.py:87
  8.7 378.8 %all-gather.12.cloned.1.call-start = ((), (), s32[]{:S(2)}) async-start(), calls=%async_computation.9 | async-start | bytes 25952256 | tf_op jit(solution)/shard_map/all_gather | solution.py:89
  9.4 11.6 copy-start.3
  9.4 11.9 copy-start.45
  9.4 580.5 %all-gather.14.cloned.1.call-start = ((), (), s32[]{:S(2)}) async-start(), calls=%async_computation.10 | async-start | bytes 25952256 | tf_op jit(solution)/shard_map/all_gather | solution.py:90
  10.0 28.5 %copy-start.46 = (bf16[256,128]{1,0:T(8,128)(2,1)S(1)}, bf16[256,128]{1,0:T(8,128)(2,1)}, u32[]{:S(2)}) copy-start(bf16[256,128]{1,0:T(8,128)(2,1)} %param.17) | copy-start | bytes 196612
  10.0 782.3 %all-gather.16.cloned.1.call-start = ((), (), s32[]{:S(2)}) async-start(), calls=%async_computation.11 | async-start | bytes 25952256 | tf_op jit(solution)/shard_map/all_gather | solution.py:91
  10.6 947.1 %reduce-scatter.10.cloned.1.call-start = ((), (), s32[]{:S(2)}) async-start(), calls=%async_computation.13 | async-start | bytes 589824 | tf_op jit(solution)/shard_map/reduce_scatter | solution.py:225
  20.4 39.1 %copy-start.53 = (f32[64]{0:T(128)}, f32[64]{0:T(128)S(1)}, u32[]{:S(2)}) copy-start(f32[64]{0:T(128)S(1)} %negate_power_fusion) | copy-start | bytes 772
  20.4 39.1 %copy-start.49 = (f32[256]{0:T(256)}, f32[256]{0:T(256)S(1)}, u32[]{:S(2)}) copy-start(f32[256]{0:T(256)S(1)} %fusion.68) | copy-start | bytes 3076
  38.5 20.4 copy-start.19
  38.5 26.5 %copy-start.55 = (bf16[256]{0:T(256)(128)(2,1)S(1)}, bf16[256]{0:T(256)(128)(2,1)}, u32[]{:S(2)}) copy-start(bf16[256]{0:T(256)(128)(2,1)} %param.20) | copy-start | bytes 1540
  58.9 17.1 copy-start.33
  59.0 17.1 copy-start.35
  59.0 62.3 %copy-start.27 = (f32[256,64]{0,1:T(8,128)}, f32[256,64]{0,1:T(8,128)S(1)}, u32[]{:S(2)}) copy-start(f32[256,64]{0,1:T(8,128)S(1)} %get-tuple-element.86) | copy-start | bytes 196612
  59.6 16.5 copy-start.38
  59.6 16.8 collective-permute-start.1
  61.9 14.6 collective-permute-start
  76.4 51.3 %copy-start.5 = (f32[256,768]{1,0:T(8,128)}, f32[256,768]{1,0:T(8,128)S(1)}, u32[]{:S(2)}) copy-start(f32[256,768]{1,0:T(8,128)S(1)} %get-tuple-element.82) | copy-start | bytes 2359300
  76.5 59.3 %copy-start.17 = (bf16[768,256]{0,1:T(8,128)(2,1)}, bf16[768,256]{0,1:T(8,128)(2,1)S(1)}, u32[]{:S(2)}) copy-start(bf16[768,256]{0,1:T(8,128)(2,1)S(1)} %pad_maximum_fusion.4) | copy-start | bytes 1179652
  121.6 2.3 copy-start.29
  124.0 4.6 copy-start
  135.8 2.6 copy-start.1
  191.1 646.5 %copy-start.9 = (f32[256,2048]{1,0:T(8,128)}, f32[256,2048]{1,0:T(8,128)S(1)}, u32[]{:S(2)}) copy-start(f32[256,2048]{1,0:T(8,128)S(1)} %get-tuple-element.90) | copy-start | bytes 6291460
  191.4 398.5 %copy-start.8 = (bf16[256,2048]{1,0:T(8,128)(2,1)}, bf16[256,2048]{1,0:T(8,128)(2,1)S(1)}, u32[]{:S(2)}) copy-start(bf16[256,2048]{1,0:T(8,128)(2,1)S(1)} %multiply_convert_fusion.4) | copy-start | bytes 3145732
  823.4 14.2 copy-start.10
  848.2 8.0 slice-start
  848.2 8.0 slice-start.1
  848.2 8.8 slice-start.2
  857.0 5.9 copy-start.30
  857.0 5.9 copy-start.32
  862.9 2.7 copy-start.2
  862.9 2.7 copy-start.26
  865.6 11.3 copy-start.44
  865.6 13.9 copy-start.50
  869.5 11.9 copy-start.4
  869.6 8.5 collective-permute-start.3
  875.0 4.6 collective-permute-start.2
  879.6 11.7 copy-start.24
  879.6 4.7 copy-start.7
  881.4 9.9 copy-start.40
  881.4 9.9 copy-start.42
  882.8 74.9 %reduce-scatter.12.cloned.1.call-start = ((), (), s32[]{:S(2)}) async-start(), calls=%async_computation.14 | async-start | bytes 589824 | tf_op jit(solution)/shard_map/reduce_scatter | solution.py:228
  884.3 148.9 %reduce-scatter.14.cloned.1.call-start = ((), (), s32[]{:S(2)}) async-start(), calls=%async_computation.15 | async-start | bytes 9437184 | tf_op jit(solution)/shard_map/reduce_scatter | solution.py:231
  891.3 6.5 copy-start.18
  891.3 232.2 %reduce-scatter.8.cloned.1.call-start = ((), (), s32[]{:S(2)}) async-start(), calls=%async_computation.12 | async-start | bytes 9437184 | tf_op jit(solution)/shard_map/reduce_scatter | solution.py:222
  902.3 7.0 copy-start.28
  902.3 7.0 copy-start.37
  918.0 433.5 %reduce-scatter.16.cloned.1.call-start = ((), (), s32[]{:S(2)}) async-start(), calls=%async_computation.16 | async-start | bytes 25952256 | tf_op jit(solution)/shard_map/reduce_scatter | solution.py:237
  931.1 648.6 %reduce-scatter.18.cloned.1.call-start = ((), (), s32[]{:S(2)}) async-start(), calls=%async_computation.17 | async-start | bytes 25952256 | tf_op jit(solution)/shard_map/reduce_scatter | solution.py:240
  943.9 863.9 %reduce-scatter.20.cloned.1.call-start = ((), (), s32[]{:S(2)}) async-start(), calls=%async_computation.18 | async-start | bytes 25952256 | tf_op jit(solution)/shard_map/reduce_scatter | solution.py:243
  957.4 1072.5 %all-reduce.7.cloned.1.call-start = ((), (), s32[]{:S(2)}) async-start(), calls=%async_computation.19 | async-start | bytes 21757952 | tf_op jit(solution)/shard_map/psum | solution.py:250
  1807.8 2.9 copy-start.51
  1810.7 13.1 copy-start.12
  1823.8 5.9 copy-start.22
  1823.8 5.9 copy-start.41
  1823.8 5.9 copy-start.43
  2029.9 2.9 copy-start.48
  2029.9 3.6 copy-start.47
  2029.9 4.3 copy-start.23
  2029.9 5.8 copy-start.16
  2035.7 3.2 copy-start.15
  2038.9 3.2 copy-start.14
  (13 other events, 17.8 us)
Sparse Core Ops, SparseCore 0:
  9.6 93.3 all-gather.7
  104.6 80.2 all-gather.9
  186.5 200.8 all-gather.11
  389.0 200.8 all-gather.13
  591.4 200.8 all-gather.15
  883.0 27.7 reduce-scatter.9
  913.1 29.0 reduce-scatter.11
  944.5 88.6 reduce-scatter.13
  1035.5 87.9 reduce-scatter.7
  1125.7 225.7 reduce-scatter.15
  1353.9 225.7 reduce-scatter.17
  1581.9 225.7 reduce-scatter.19
  1812.5 217.2 all-reduce.6
where the time goes:
time: 2060 us; the launch traced here: 2050 us
  waiting for transfers between devices  1670 us (81%)
  matrix products  187 us (9%)
  blocking collectives  79.4 us (4%)
  local copies, waits for them, and re-layouts  46 us (2%)
  other arithmetic  41.7 us (2%)
    reduce_scatter x1, waiting for transfers between devices, shards(): lax.psum_scatter(grad_up_w.astype(jnp.bfloat16), 'seq', scatter_dimension...  228 us
    reduce_scatter x1, waiting for transfers between devices, shards(): lax.psum_scatter(grad_down.astype(jnp.bfloat16), 'seq', scatter_dimension...  228 us
    reduce_scatter x1, waiting for transfers between devices, shards(): lax.psum_scatter(grad_gate_w.astype(jnp.bfloat16), 'seq', scatter_dimensi...  228 us
    all_gather x1, waiting for transfers between devices, shards(): lax.all_gather(w_gate, 'seq', axis=0, tiled=True)  196 us
    all_gather x1, waiting for transfers between devices, shards(): lax.all_gather(w_up, 'seq', axis=0, tiled=True)  189 us
    all_gather x1, waiting for transfers between devices, shards(): lax.all_gather(w_down, 'seq', axis=0, tiled=True)  188 us
    psum x1, waiting for transfers between devices, shards(): lax.psum(part_b.astype(jnp.bfloat16), 'slot').astype(jnp.float32)  169 us
    reduce_scatter x1, waiting for transfers between devices, shards(): lax.psum_scatter(grad_query_w.astype(jnp.bfloat16), 'seq', scatter_dimens...  90.3 us
  transfers between devices with their start and end apart: 17, of which 13 were waited for; matrix products, arithmetic and copies ran while one was open for 8% of the time, Pallas kernels for 0%

commit v1 on v0

v1 whole, which is shorter than its diff:
```python
import jax
import jax.numpy as jnp
from jax import lax
from jax.sharding import PartitionSpec as P

WINDOW = 512


EPSILON = 1e-05
THETA = 10000.0
NEGATIVE = -1e30
BF = jnp.bfloat16
F32 = jnp.float32


def swap(block, axis, mask):
    return lax.ppermute(block, axis, [(i, i ^ mask) for i in range(lax.axis_size(axis))])


def gather_slot(block):
    count = lax.axis_size("slot")
    if count != 4:
        return [block] + [swap(block, "slot", j) for j in range(1, count)]
    half = block.shape[0] // 2
    one = swap(block, "slot", 1)
    two = swap(block, "slot", 2)
    low = swap(one[:half], "slot", 2)
    high = swap(two[half:], "slot", 1)
    return [block, one, two, jnp.concatenate([low, high], axis=0)]


def scatter_slot(blocks):
    count = lax.axis_size("slot")
    own = blocks[0].astype(F32)
    if count != 4:
        for j in range(1, count):
            own = own + swap(blocks[j], "slot", j).astype(F32)
        return own
    half = blocks[0].shape[0] // 2
    low = swap(blocks[3][:half], "slot", 2)
    high = swap(blocks[3][half:], "slot", 1)
    one_high = swap(blocks[1][half:], "slot", 1)
    two_low = swap(blocks[2][:half], "slot", 2)
    one_low = swap((blocks[1][:half].astype(F32) + low.astype(F32)).astype(BF), "slot", 1)
    two_high = swap((blocks[2][half:].astype(F32) + high.astype(F32)).astype(BF), "slot", 2)
    first = jnp.concatenate([one_low, one_high], axis=0).astype(F32)
    second = jnp.concatenate([two_low, two_high], axis=0).astype(F32)
    return own + first + second


def trade_slot(blocks):
    return [blocks[0]] + [swap(blocks[j], "slot", j) for j in range(1, len(blocks))]


def gather_line(block):
    count = lax.axis_size("seq")
    if count != 8:
        return [block] + [swap(block, "seq", j) for j in range(2, count, 2)]
    one = swap(block, "seq", 2)
    three = swap(block, "seq", 6)
    two = swap(three, "seq", 2)
    return [block, one, two, three]


def both_cores(blocks):
    out = []
    for block in blocks:
        out += [block, swap(block, "seq", 1)]
    return out


def scatter_seq(blocks):
    count = lax.axis_size("seq")
    line = []
    for j in range(0, count, 2):
        line.append(blocks[j].astype(F32) + swap(blocks[j + 1], "seq", 1).astype(F32))
    if count != 8:
        own = line[0]
        for k in range(1, count // 2):
            own = own + swap(line[k].astype(BF), "seq", 2 * k).astype(F32)
        return own
    own, one, two, three = line
    passed = swap(two.astype(BF), "seq", 2)
    near = swap(one.astype(BF), "seq", 2)
    far = swap((three + passed.astype(F32)).astype(BF), "seq", 6)
    return own + near.astype(F32) + far.astype(F32)


def xor_blocks(values, index, count, axis):
    width = values.shape[axis] // count
    return jnp.concatenate(
        [lax.dynamic_slice_in_dim(values, (index ^ j) * width, width, axis) for j in range(count)],
        axis=axis,
    )


def shifted(block, axis, distance):
    devices = range(lax.axis_size(axis))
    route = [(i - distance, i) for i in devices if i - distance in devices]
    return lax.ppermute(block, axis, route)


def rope_tables(positions, head_width):
    half_width = head_width // 2
    exponent = jnp.arange(half_width, dtype=jnp.float32) * (2.0 / head_width)
    frequency = THETA ** (-exponent)
    angles = positions.astype(jnp.float32)[:, None] * frequency[None, :]
    return (jnp.cos(angles), jnp.sin(angles))


def rotate(values, cosine_table, sine_table):
    half_width = values.shape[-1] // 2
    first_half = values[..., :half_width]
    second_half = values[..., half_width:]
    return jnp.concatenate(
        [
            first_half * cosine_table - second_half * sine_table,
            second_half * cosine_table + first_half * sine_table,
        ],
        axis=-1,
    )


def rms_scale(values):
    return lax.rsqrt(jnp.mean(values * values, axis=-1, keepdims=True) + EPSILON)


def window_mask(query_pos, key_pos, length):
    distance = query_pos[:, None] - key_pos[None, :]
    return (
        (key_pos[None, :] >= 0)
        & (key_pos[None, :] < length)
        & (distance >= 0)
        & (distance < WINDOW)
        & (query_pos[:, None] < length)
    )


def norm_back(grad_normed, unit_rows, scale_rows, gain_row):
    scaled = grad_normed * gain_row.astype(jnp.float32)
    return scale_rows * (scaled - unit_rows * jnp.mean(scaled * unit_rows, axis=-1, keepdims=True))


def dot(left, right):
    return jnp.dot(left, right, preferred_element_type=F32)


def dot_nt(left, right):
    return lax.dot_general(left, right, (((1,), (1,)), ((), ())), preferred_element_type=F32)


def dot_tn(left, right):
    return lax.dot_general(left, right, (((0,), (0,)), ((), ())), preferred_element_type=F32)


def shards(
    rows_in,
    lengths,
    norm1_gain,
    w_query,
    w_key,
    w_value,
    w_out,
    norm2_gain,
    w_gate,
    w_up,
    w_down,
    rows_cot,
    kv_cot,
):
    slots = lax.axis_size("slot")
    seqs = lax.axis_size("seq")
    slot = lax.axis_index("slot")
    seq = lax.axis_index("seq")
    tok_count = rows_in.shape[1]
    model = rows_in.shape[2]
    head_width = w_key.shape[1]
    head_count = w_query.shape[1] // head_width
    hop_count = WINDOW // tok_count
    key_count = WINDOW + tok_count
    scaling = head_width ** (-0.5)
    rows_dev = w_query.shape[0]
    cols_slot = w_query.shape[1] // slots
    out_slot = w_out.shape[1] // slots
    hidden_all = w_gate.shape[1]
    piece = hidden_all // (slots * seqs)
    hidden_slot = piece * seqs
    kv_width = 2 * head_width

    gains = jnp.stack([norm1_gain, norm2_gain], axis=0)
    pack = jnp.concatenate(
        [lax.dynamic_slice_in_dim(w_query, slot * cols_slot, cols_slot, 1), w_key, w_value], axis=1
    )
    gains = jnp.pad(gains, ((0, 14), (0, pack.shape[1] - rows_dev)))
    pack_line = gather_line(jnp.concatenate([pack, gains], axis=0))
    out_line = gather_line(lax.dynamic_slice_in_dim(w_out, slot * out_slot, out_slot, 1))

    def spread(line):
        cut = len(line) // 2
        parts = []
        for group in (line[:cut], line[cut:]):
            got = gather_slot(jnp.concatenate(group, axis=0))
            parts.append(jnp.concatenate(got, axis=1))
        whole = jnp.concatenate(parts, axis=0)
        other = swap(whole, "seq", 1)
        mine = whole.reshape(len(line), rows_dev, -1)
        theirs = other.reshape(len(line), rows_dev, -1)
        return jnp.stack([mine, theirs], axis=1).reshape(2 * len(line) * rows_dev, -1)

    query_w = spread([block[:rows_dev, :cols_slot] for block in pack_line])
    rest = both_cores([block[:, cols_slot:] for block in pack_line])
    kv_w = jnp.concatenate([block[:rows_dev] for block in rest], axis=0)
    gain_rows = both_cores([block[rows_dev:, :rows_dev] for block in pack_line])
    gain_x = jnp.concatenate([block[:2] for block in gain_rows], axis=1)
    gain_both = xor_blocks(gain_x, seq, seqs, 1)
    gain_one, gain_two = gain_both[0], gain_both[1]
    out_w = spread(out_line)

    def share(weight):
        cut = weight.reshape(rows_dev, seqs, slots, piece)
        return lax.dynamic_index_in_dim(cut, slot, 2, keepdims=False).reshape(rows_dev, hidden_slot)

    gu_line = gather_line(jnp.concatenate([share(w_gate), share(w_up)], axis=1))
    down_line = gather_line(lax.dynamic_slice_in_dim(w_down, slot * piece, piece, 0))
    gu_w = jnp.concatenate(both_cores(gu_line), axis=0)
    down_w = jnp.zeros((hidden_slot, model), BF)
    for j, block in enumerate(both_cores(down_line)):
        down_w = lax.dynamic_update_slice_in_dim(down_w, block, (seq ^ j) * piece, 0)

    first_row = seq * tok_count
    query_pos = first_row + jnp.arange(tok_count, dtype=jnp.int32)
    seq_length = lengths[0]
    row_valid = (query_pos < seq_length).astype(jnp.float32)[:, None]
    query_valid = (query_pos < seq_length)[:, None, None]
    inputs = rows_in[0].astype(jnp.float32)
    scale_one = rms_scale(inputs)
    normed = (inputs * scale_one * gain_one.astype(jnp.float32)).astype(BF)
    normed_x = xor_blocks(normed, seq, seqs, 1)
    query_pre = xor_blocks(dot(normed_x, query_w), slot, slots, 1)
    kv_pre = dot(normed_x, kv_w)
    key_pre = kv_pre[:, :head_width]
    value_rows = kv_pre[:, head_width:].astype(BF)
    cosine_table, sine_table = rope_tables(query_pos, head_width)
    queries = rotate(
        query_pre.reshape(tok_count, head_count, head_width),
        cosine_table[:, None, :],
        sine_table[:, None, :],
    ).astype(BF)
    key_rows = rotate(key_pre, cosine_table, sine_table).astype(BF)
    shared = jnp.concatenate([key_rows, value_rows], axis=1) * row_valid.astype(BF)
    rim_list = []
    for hop_index in range(hop_count, 0, -1):
        rim_list.append(shifted(shared, "seq", hop_index))
    key_table = jnp.concatenate(rim_list + [shared], axis=0)
    key_part = key_table[:, :head_width]
    value_part = key_table[:, head_width:]
    key_pos = first_row - WINDOW + jnp.arange(key_count, dtype=jnp.int32)
    allowed = window_mask(query_pos, key_pos, seq_length)[:, None, :]
    allowed_float = allowed.astype(jnp.float32)
    flat_queries = queries.reshape(tok_count * head_count, head_width)

    def score_rows():
        raw_scores = dot(flat_queries, key_part.T)
        raw_scores = raw_scores.reshape(tok_count, head_count, key_count) * scaling
        return jnp.where(allowed, raw_scores, NEGATIVE)

    masked = score_rows()
    row_max = jnp.max(masked, axis=-1, keepdims=True)
    exponent_rows = jnp.exp(masked - row_max) * allowed_float
    row_sum = jnp.sum(exponent_rows, axis=-1, keepdims=True)
    row_denom = jnp.where(query_valid, row_sum, 1.0)
    prob_rows = (exponent_rows / row_denom).astype(BF)
    log_total = row_max + jnp.log(row_denom)
    flat_probs = prob_rows.reshape(tok_count * head_count, key_count)
    attended = dot(flat_probs, value_part)
    attended = attended.reshape(tok_count, head_count * head_width).astype(BF)
    attended_x = xor_blocks(attended, seq, seqs, 1)
    middle = inputs + xor_blocks(dot(attended_x, out_w), slot, slots, 1)
    scale_two = rms_scale(middle)
    normed_two = (middle * scale_two * gain_two.astype(jnp.float32)).astype(BF)

    normed_two_all = jnp.concatenate(
        gather_slot(xor_blocks(normed_two, seq, seqs, 1)), axis=0
    )
    down_in = rows_cot[0] * row_valid.astype(BF)
    down_in_all = jnp.concatenate(gather_slot(down_in), axis=0)
    gu_out = dot(normed_two_all, gu_w)
    gate_out = gu_out[:, :hidden_slot]
    up_out = gu_out[:, hidden_slot:]
    sig_gate = jax.nn.sigmoid(gate_out)
    hidden = (gate_out * sig_gate * up_out).astype(BF)
    down_part = dot(hidden, down_w).astype(BF)

    def token_blocks(values):
        return [values[j * tok_count : (j + 1) * tok_count] for j in range(slots)]

    result = middle + scatter_slot(token_blocks(down_part)) * row_valid

    grad_down = dot_tn(hidden, down_in_all).astype(BF)
    grad_hidden = dot_nt(down_in_all, down_w)
    grad_gate = grad_hidden * up_out * sig_gate * (1.0 + gate_out * (1.0 - sig_gate))
    grad_up = grad_hidden * gate_out * sig_gate
    grad_gu = jnp.concatenate([grad_gate.astype(BF), grad_up.astype(BF)], axis=1)
    grad_normed_two = dot_nt(grad_gu, gu_w).astype(BF)
    grad_gu_w = dot_tn(normed_two_all, grad_gu).astype(BF)
    grad_normed_two = xor_blocks(scatter_slot(token_blocks(grad_normed_two)), seq, seqs, 1)

    def row_blocks(values):
        return [values[j * rows_dev : (j + 1) * rows_dev] for j in range(seqs)]

    own_down = scatter_seq(
        [lax.dynamic_slice_in_dim(grad_down, (seq ^ j) * piece, piece, 0) for j in range(seqs)]
    ).astype(BF)
    own_gu = scatter_seq(row_blocks(grad_gu_w)).astype(BF)

    unit_two = middle * scale_two
    grad_gain_two = jnp.sum(grad_normed_two * unit_two, axis=0)
    grad_middle = rows_cot[0].astype(F32) + norm_back(
        grad_normed_two, unit_two, scale_two, gain_two
    )
    branch_grad = grad_middle.astype(BF)
    branch_x = xor_blocks(branch_grad, slot, slots, 1)

    def col_blocks(values):
        width = values.shape[1] // slots
        return [values[:, j * width : (j + 1) * width] for j in range(slots)]

    attended_all = jnp.concatenate(gather_slot(attended_x), axis=0)
    branch_all = jnp.concatenate(trade_slot(col_blocks(branch_x)), axis=0)
    own_out = scatter_seq(row_blocks(dot_tn(attended_all, branch_all).astype(BF))).astype(BF)

    grad_attended = xor_blocks(dot_nt(branch_x, out_w).astype(BF), seq, seqs, 1)
    flat_grad = grad_attended.reshape(tok_count * head_count, head_width)
    probs_float = jnp.exp(score_rows() - log_total) * allowed_float
    grad_probs = dot(flat_grad, value_part.T)
    grad_probs = grad_probs.reshape(tok_count, head_count, key_count)
    grad_scores = probs_float * (
        grad_probs - jnp.sum(probs_float * grad_probs, axis=-1, keepdims=True)
    )
    flat_scores = grad_scores.astype(BF).reshape(tok_count * head_count, key_count)
    grad_queries = dot(flat_scores, key_part) * scaling
    grad_keys = dot(flat_scores.T, flat_queries) * scaling
    grad_values = dot(flat_probs.T, flat_grad)
    grad_table = jnp.concatenate([grad_keys, grad_values], axis=1)
    own_grad = grad_table[WINDOW:] + kv_cot[0].astype(jnp.float32)
    for hop_index in range(1, hop_count + 1):
        lower = (hop_count - hop_index) * tok_count
        own_grad = own_grad + shifted(
            grad_table[lower : lower + tok_count].astype(BF), "seq", -hop_index
        ).astype(jnp.float32)
    own_grad = own_grad * row_valid
    grad_key_pre = rotate(own_grad[:, :head_width], cosine_table, -sine_table).astype(BF)
    grad_value = own_grad[:, head_width:].astype(BF)
    grad_kv_pre = jnp.concatenate([grad_key_pre, grad_value], axis=1)
    grad_query_pre = rotate(
        grad_queries.reshape(tok_count, head_count, head_width),
        cosine_table[:, None, :],
        -sine_table[:, None, :],
    )
    grad_query_pre = grad_query_pre.reshape(tok_count, head_count * head_width).astype(BF)
    grad_query_x = xor_blocks(grad_query_pre, slot, slots, 1)
    grad_normed = xor_blocks(
        dot_nt(grad_query_x, query_w) + dot_nt(grad_kv_pre, kv_w), seq, seqs, 1
    )
    unit_one = inputs * scale_one
    grad_gain_one = jnp.sum(grad_normed * unit_one, axis=0)
    grad_inputs = grad_middle + norm_back(grad_normed, unit_one, scale_one, gain_one)

    normed_all = jnp.concatenate(gather_slot(normed_x), axis=0)
    traded = trade_slot(
        [jnp.concatenate([block, grad_kv_pre], axis=1) for block in col_blocks(grad_query_x)]
    )
    grad_qkv_w = dot_tn(normed_all, jnp.concatenate(traded, axis=0)).astype(BF)
    gain_grads = jnp.stack([grad_gain_one, grad_gain_two], axis=0)
    gain_grads = xor_blocks(gain_grads, seq, seqs, 1).astype(BF)
    qkv_blocks = []
    for j, block in enumerate(row_blocks(grad_qkv_w)):
        extra = gain_grads[:, j * rows_dev : (j + 1) * rows_dev]
        extra = jnp.pad(extra, ((0, 14), (0, block.shape[1] - rows_dev)))
        qkv_blocks.append(jnp.concatenate([block, extra], axis=0))
    own_qkv = scatter_seq(qkv_blocks)
    own_query = jnp.concatenate([own_qkv[:, :cols_slot], ], axis=1).astype(BF)

    def slot_columns(blocks):
        return xor_blocks(jnp.concatenate(blocks, axis=1), slot, slots, 1).astype(F32)

    query_blocks = gather_slot(own_query)
    query_grad = slot_columns([block[:rows_dev] for block in query_blocks])
    gain_total = sum(block[rows_dev : rows_dev + 2, :rows_dev].astype(F32) for block in query_blocks)
    out_grad_w = slot_columns(gather_slot(own_out))
    down_grad = xor_blocks(
        jnp.concatenate(gather_slot(own_down), axis=0), slot, slots, 0
    ).astype(F32)
    gu_all = jnp.stack(gather_slot(own_gu), axis=0)
    gu_all = xor_blocks(gu_all, slot, slots, 0)

    def whole(part):
        cut = part.reshape(slots, rows_dev, seqs, piece).transpose(1, 2, 0, 3)
        return cut.reshape(rows_dev, hidden_all).astype(F32)

    gate_grad = whole(gu_all[:, :, :hidden_slot])
    up_grad = whole(gu_all[:, :, hidden_slot:])
    return (
        result.astype(BF)[None],
        shared[None],
        grad_inputs.astype(BF)[None],
        gain_total[0],
        query_grad,
        own_qkv[:rows_dev, cols_slot : cols_slot + head_width],
        own_qkv[:rows_dev, cols_slot + head_width : cols_slot + kv_width],
        out_grad_w,
        gain_total[1],
        gate_grad,
        up_grad,
        down_grad,
    )


def solution(mesh):
    placed = (
        P("slot", "seq", None),
        P("slot"),
        P("seq"),
        P("seq", None),
        P("seq", None),
        P("seq", None),
        P("seq", None),
        P("seq"),
        P("seq", None),
        P("seq", None),
        P("seq", None),
        P("slot", "seq", None),
        P("slot", "seq", None),
    )
    return jax.shard_map(
        shards,
        mesh=mesh,
        in_specs=placed,
        out_specs=(
            P("slot", "seq", None),
            P("slot", "seq", None),
            P("slot", "seq", None),
            P("seq"),
            P("seq", None),
            P("seq", None),
            P("seq", None),
            P("seq", None),
            P("seq"),
            P("seq", None),
            P("seq", None),
            P("seq", None),
        ),
        check_vma=False,
    )
```

time: 2060 us -> 1020 us (0.50)
  waiting for transfers between devices: 1670 us -> 356 us
  local copies, waits for them, and re-layouts: 46 us -> 192 us
  starting transfers between devices: 13.8 us -> 151 us
  other arithmetic: 41.7 us -> 163 us
  blocking collectives: 79.4 us -> 0 us
  matrix products: 187 us -> 136 us
    reduce_scatter x7 -> x0, waiting for transfers between devices: 850 us -> none  [the longest x1 228 us: shards(): lax.psum_scatter(grad_up_w.astype(jnp.bfloat16), 'seq', scatter_dimension...]
    all_gather x5 -> x0, waiting for transfers between devices: 643 us -> none  [the longest x1 196 us: shards(): lax.all_gather(w_gate, 'seq', axis=0, tiled=True)]
    ppermute x0 -> x124, waiting for transfers between devices: none -> 354 us  [swap(): lax.ppermute(block, axis, [(i, i ^ mask) for i in range(lax.axis_size(axi...]
    psum x1 -> x0, waiting for transfers between devices: 169 us -> none  [shards(): lax.psum(part_b.astype(jnp.bfloat16), 'slot').astype(jnp.float32)]
    ppermute x0 -> x124, starting transfers between devices: none -> 141 us  [swap(): lax.ppermute(block, axis, [(i, i ^ mask) for i in range(lax.axis_size(axi...]
    concatenate x1 -> x17, other arithmetic: 0.01 us -> 80.6 us  [the longest x2 73 us: spread(): whole = jnp.concatenate(parts, axis=0)]
    unnamed x129 -> x362, local copies, waits for them, and re-layouts: 18.5 us -> 97 us
    all_gather x4 -> x0, blocking collectives: 56.7 us -> none  [the longest x1 19.5 us: shards(): lax.all_gather(w_key, 'seq', axis=0, tiled=True)]
  transfers between devices with their start and end apart: 17 -> 128, of which waited for: 13 -> 51; matrix products, arithmetic and copies ran while one was open for 8% -> 43% of each run, Pallas kernels for 0% -> 0%
where the time goes in v1:
time: 1020 us; the launch traced here: 1000 us
  waiting for transfers between devices  356 us (35%)
  local copies, waits for them, and re-layouts  192 us (19%)
  other arithmetic  163 us (16%)
  starting transfers between devices  151 us (15%)
  matrix products  136 us (13%)
    ppermute x124, waiting for transfers between devices, swap(): lax.ppermute(block, axis, [(i, i ^ mask) for i in range(lax.axis_size(axi...  354 us
    ppermute x124, starting transfers between devices, swap(): lax.ppermute(block, axis, [(i, i ^ mask) for i in range(lax.axis_size(axi...  141 us
    unnamed x362, local copies, waits for them, and re-layouts  97 us
    concatenate x2, other arithmetic, spread(): whole = jnp.concatenate(parts, axis=0)  73 us
    dot_general x11, matrix products, dot(): return jnp.dot(left, right, preferred_element_type=F32)  58 us
    dot_general x5, matrix products, dot_nt(): lax.dot_general(left, right, (((1,), (1,)), ((), ())), preferred_element_...  41.5 us
    dot_general x4, matrix products, dot_tn(): lax.dot_general(left, right, (((0,), (0,)), ((), ())), preferred_element_...  36.2 us
    convert_element_type x4, local copies, waits for them, and re-layouts, whole(): return cut.reshape(rows_dev, hidden_all).astype(F32)  23.8 us
  transfers between devices with their start and end apart: 128, of which 51 were waited for; matrix products, arithmetic and copies ran while one was open for 43% of the time, Pallas kernels for 0%

profile of v1, /device:TPU:10, one launch (start us, length us, event | category | flops | bytes accessed | tf_op | source)
XLA Modules:
  0.0 1002.2 jit_solution(9623437372608313971)
XLA Ops:
  15.7 4.5 copy.57
  20.2 4.6 copy.58
  53.0 11.6 %collective-permute-done.28 = bf16[256,512]{1,0:T(8,128)(2,1)S(1)} collective-permute-done((bf16[256,512]{1,0:T(8,128)(2,1)}, bf16[256,512]{1,0:T(8,128)(2,1)S(1)}, u32[]{:S(2)}, u32[]{:S(2)}) %collective-permute-start.28) | collective-permute-done | bytes 262176 | tf_op jit(solution)/shard_map/ppermute | solution.py:17
  71.0 13.1 %collective-permute-done.24 = bf16[512,512]{1,0:T(8,128)(2,1)S(1)} collective-permute-done((bf16[512,512]{1,0:T(8,128)(2,1)S(1)}, bf16[512,512]{1,0:T(8,128)(2,1)S(1)}, u32[]{:S(2)}, u32[]{:S(2)}) %collective-permute-start.24) | collective-permute-done | bytes 524320 | tf_op jit(solution)/shard_map/ppermute | solution.py:17
  100.4 13.3 %collective-permute-done.7 = bf16[512,512]{1,0:T(8,128)(2,1)S(1)} collective-permute-done((bf16[512,512]{1,0:T(8,128)(2,1)S(1)}, bf16[512,512]{1,0:T(8,128)(2,1)S(1)}, u32[]{:S(2)}, u32[]{:S(2)}) %collective-permute-start.7) | collective-permute-done | bytes 524320 | tf_op jit(solution)/shard_map/ppermute | solution.py:17
  119.9 9.0 collective-permute-done.30
  146.7 4.2 collective-permute-start.20
  157.8 5.4 collective-permute-done.32
  166.4 22.2 %maximum_maximum_fusion.1 = bf16[1024,2048]{1,0:T(8,128)(2,1)S(1)} fusion(bf16[256,512]{1,0:T(8,128)(2,1)S(1)} %collective-permute-done.32, bf16[256,512]{1,0:T(8,128)(2,1)S(1)} %collective-permute-done.31, bf16[512,512]{1,0:T(8,128)(2,1)} %collective-permute-done.30, bf16[512,512]{1,0:T(8,128)(2,1)} %collective-permute-done.29, ...), kind=kLoop, calls=%fused_computation.22 | loop fusion | flops 46137344 | bytes 8388608 | tf_op jit(solution)/shard_map/concatenate | solution.py:204
  193.5 4.2 collective-permute-done.39
  202.0 41.1 %collective-permute-done.49 = bf16[176,2048]{1,0:T(8,128)(2,1)S(1)} collective-permute-done((bf16[176,2048]{1,0:T(8,128)(2,1)}, bf16[176,2048]{1,0:T(8,128)(2,1)S(1)}, u32[]{:S(2)}, u32[]{:S(2)}) %collective-permute-start.49) | collective-permute-done | bytes 720928 | tf_op jit(solution)/shard_map/ppermute | solution.py:17
  245.9 50.8 %maximum_maximum_fusion = bf16[1024,2048]{1,0:T(8,128)(2,1)} fusion(bf16[256,512]{1,0:T(8,128)(2,1)} %copy-done.87, bf16[256,512]{1,0:T(8,128)(2,1)} %collective-permute-done.13, bf16[512,512]{1,0:T(8,128)(2,1)S(1)} %collective-permute-done.12, bf16[512,512]{1,0:T(8,128)(2,1)S(1)} %collective-permute-done.11, bf16[256,512]{1,0:T(8,128)(2,1)S(1)} %copy-done.38, ...), kind=kLoop, calls=%fused_computation.21 | loop fusion | flops 50331648 | bytes 8388608 | tf_op jit(solution)/shard_map/concatenate | solution.py:204
  307.4 8.0 collective-permute-done.72
  318.0 14.3 %collective-permute-done.42 = bf16[256,2816]{0,1:T(8,128)(2,1)S(1)} collective-permute-done((bf16[256,2816]{0,1:T(8,128)(2,1)}, bf16[256,2816]{0,1:T(8,128)(2,1)S(1)}, u32[]{:S(2)}, u32[]{:S(2)}) %collective-permute-start.42) | collective-permute-done | bytes 1441824 | tf_op jit(solution)/shard_map/ppermute | solution.py:17
  344.0 7.4 pad_maximum_fusion.1
  351.4 7.5 pad_maximum_fusion
  359.0 5.7 fusion.157
  370.5 3.8 fusion
  375.0 3.7 divide_convert_fusion
  378.7 3.6 copy.56
  397.6 5.9 fusion.159
  416.3 5.4 collective-permute-done.89
  423.9 20.3 %collective-permute-done.35 = bf16[256,2048]{1,0:T(8,128)(2,1)S(1)} collective-permute-done((bf16[256,2048]{1,0:T(8,128)(2,1)S(1)}, bf16[256,2048]{1,0:T(8,128)(2,1)S(1)}, u32[]{:S(2)}, u32[]{:S(2)}) %collective-permute-start.35) | collective-permute-done | bytes 1048608 | tf_op jit(solution)/shard_map/ppermute | solution.py:17
  449.2 16.4 %collective-permute-done.36 = bf16[128,2048]{1,0:T(8,128)(2,1)S(1)} collective-permute-done((bf16[128,2048]{1,0:T(8,128)(2,1)S(1)}, bf16[128,2048]{1,0:T(8,128)(2,1)S(1)}, u32[]{:S(2)}, u32[]{:S(2)}) %collective-permute-start.36) | collective-permute-done | bytes 524320 | tf_op jit(solution)/shard_map/ppermute | solution.py:17
  467.6 16.5 %fusion.160 = f32[1024,2816]{1,0:T(8,128)} fusion(bf16[1024,2048]{1,0:T(8,128)(2,1)} %constant_dynamic-update-slice_fusion.50, bf16[2048,2816]{0,1:T(8,128)(2,1)S(1)} %constant_dynamic-update-slice_fusion.62), kind=kOutput, calls=%fused_computation.494 | convolution fusion | flops 11811160064 | bytes 27262976 | tf_op jit(solution)/shard_map/dot_general | solution.py:145
  484.1 15.2 %multiply_convert_fusion.2 = (bf16[1024,1408]{1,0:T(8,128)(2,1)}, bf16[1024,1408]{1,0:T(8,128)(2,1)}, bf16[1024,1408]{1,0:T(8,128)(2,1)}) fusion(f32[1024,2816]{1,0:T(8,128)} %fusion.160, bf16[1024,2048]{1,0:T(8,128)(2,1)S(1)} %copy-done.88, bf16[1408,2048]{1,0:T(8,128)(2,1)} %constant_dynamic-update-slice_fusion.144), kind=kOutput, calls=%fused_computation.16 | convolution fusion | flops 5928648704 | bytes 30146560 | tf_op jit(solution)/shard_map/dot_general | solution.py:149
  499.3 16.6 %convolution_convert_fusion.3 = bf16[1024,2048]{1,0:T(8,128)(2,1)S(1)} fusion(bf16[2048,2816]{0,1:T(8,128)(2,1)} %copy-done.90, bf16[1024,1408]{1,0:T(8,128)(2,1)} %get-tuple-element.57, bf16[1024,1408]{1,0:T(8,128)(2,1)} %get-tuple-element.56), kind=kOutput, calls=%fused_computation.23 | convolution fusion | flops 11824791552 | bytes 21495808 | tf_op jit(solution)/shard_map/dot_general | solution.py:149
  515.9 18.5 %convolution_convert_fusion = bf16[2048,2816]{1,0:T(8,128)(2,1)} fusion(bf16[1024,2048]{1,0:T(8,128)(2,1)} %constant_dynamic-update-slice_fusion.50, bf16[1024,1408]{1,0:T(8,128)(2,1)} %get-tuple-element.57, bf16[1024,1408]{1,0:T(8,128)(2,1)} %get-tuple-element.56), kind=kOutput, calls=%fused_computation.6 | convolution fusion | flops 11828461568 | bytes 21495808 | tf_op jit(solution)/shard_map/dot_general | solution.py:153
  534.4 8.8 convolution_convert_fusion.4
  543.3 10.6 %convolution_convert_fusion.1 = bf16[1408,2048]{1,0:T(8,128)(2,1)S(1)} fusion(bf16[1024,1408]{1,0:T(8,128)(2,1)} %get-tuple-element.64, bf16[1024,2048]{1,0:T(8,128)(2,1)} %constant_dynamic-update-slice_fusion.70), kind=kOutput, calls=%fused_computation.10 | convolution fusion | flops 5908463616 | bytes 12845056 | tf_op jit(solution)/shard_map/dot_general | solution.py:153
  566.5 3.7 collective-permute-done.66
  571.8 7.6 collective-permute-done.56
  587.4 5.6 collective-permute-done.65
  594.5 9.7 collective-permute-done.67
  609.1 6.4 collective-permute-done.55
  616.7 7.8 collective-permute-done.57
  624.9 3.3 add_convert_fusion.5
  630.8 3.4 convolution_convert_fusion.7
  641.9 11.7 %multiply_reduce_fusion = (f32[256,16]{0,1:T(8,128)S(1)}, f32[256,16,768]{2,0,1:T(8,128)}) fusion(f32[256,16,768]{2,0,1:T(8,128)} %copy-done.2, f32[256,16]{0,1:T(8,128)S(1)} %get-tuple-element.44, f32[256,768]{1,0:T(8,128)S(1)} %get-tuple-element.198, pred[256,768]{1,0:T(8,128)(4,1)S(1)} %get-tuple-element.199, bf16[768,256]{0,1:T(8,128)(2,1)S(1)} %copy-done.31, ...), kind=kOutput, calls=%fused_computation.1 | convolution fusion | flops 824176640 | bytes 27426816 | tf_op jit(solution)/shard_map/dot_general | solution.py:145
  654.8 8.1 multiply_convert_fusion
  667.2 6.5 copy.61
  692.3 5.9 convolution_add_fusion
  706.1 3.4 convolution_convert_fusion.6
  712.5 4.6 add_convert_fusion.3
  717.1 6.5 collective-permute-done.122
  731.1 3.6 convolution_convert_fusion.5
  735.1 6.9 collective-permute-done.100
  747.1 7.3 collective-permute-done.101
  758.0 10.6 %collective-permute-done.119 = bf16[176,2048]{1,0:T(8,128)(2,1)S(1)} collective-permute-done((bf16[176,2048]{1,0:T(8,128)(2,1)S(1)}, bf16[176,2048]{1,0:T(8,128)(2,1)S(1)}, u32[]{:S(2)}, u32[]{:S(2)}) %collective-permute-start.119) | collective-permute-done | bytes 720928 | tf_op jit(solution)/shard_map/ppermute | solution.py:17
  770.9 43.0 %collective-permute-start.82 = (bf16[272,768]{1,0:T(8,128)(2,1)S(1)}, bf16[272,768]{1,0:T(8,128)(2,1)S(1)}, u32[]{:S(2)}, u32[]{:S(2)}) collective-permute-start(bf16[272,768]{1,0:T(8,128)(2,1)S(1)} %add_convert_fusion.17), channel_id=1, source_target_pairs={{0,2},{1,3},{2,0},{3,1},{4,6},{5,7},{6,4},{7,5},{8,10},{9,11},{10,... | collective-permute-start | bytes 1253384 | tf_op jit(solution)/shard_map/ppermute | solution.py:17
  833.4 12.3 %collective-permute-done.83 = bf16[272,768]{1,0:T(8,128)(2,1)S(1)} collective-permute-done((bf16[272,768]{1,0:T(8,128)(2,1)S(1)}, bf16[272,768]{1,0:T(8,128)(2,1)S(1)}, u32[]{:S(2)}, u32[]{:S(2)}) %collective-permute-start.83) | collective-permute-done | bytes 417824 | tf_op jit(solution)/shard_map/ppermute | solution.py:17
  851.2 10.9 %collective-permute-done.124 = bf16[176,2048]{1,0:T(8,128)(2,1)} collective-permute-done((bf16[176,2048]{1,0:T(8,128)(2,1)}, bf16[176,2048]{1,0:T(8,128)(2,1)}, u32[]{:S(2)}, u32[]{:S(2)}) %collective-permute-start.124) | collective-permute-done | bytes 720928 | tf_op jit(solution)/shard_map/ppermute | solution.py:17
  866.6 5.2 collective-permute-done.84
  874.0 32.1 %collective-permute-done.112 = bf16[256,2816]{1,0:T(8,128)(2,1)} collective-permute-done((bf16[256,2816]{1,0:T(8,128)(2,1)}, bf16[256,2816]{1,0:T(8,128)(2,1)}, u32[]{:S(2)}, u32[]{:S(2)}) %collective-permute-start.112) | collective-permute-done | bytes 1441824 | tf_op jit(solution)/shard_map/ppermute | solution.py:17
  906.1 3.4 add_convert_fusion
  913.6 28.1 %collective-permute-done.114 = bf16[256,2816]{1,0:T(8,128)(2,1)S(1)} collective-permute-done((bf16[256,2816]{1,0:T(8,128)(2,1)S(1)}, bf16[256,2816]{1,0:T(8,128)(2,1)S(1)}, u32[]{:S(2)}, u32[]{:S(2)}) %collective-permute-start.114) | collective-permute-done | bytes 1441824 | tf_op jit(solution)/shard_map/ppermute | solution.py:17
  946.8 10.9 %collective-permute-done.116 = bf16[128,2816]{1,0:T(8,128)(2,1)S(1)} collective-permute-done((bf16[128,2816]{1,0:T(8,128)(2,1)S(1)}, bf16[128,2816]{1,0:T(8,128)(2,1)S(1)}, u32[]{:S(2)}, u32[]{:S(2)}) %collective-permute-start.116) | collective-permute-done | bytes 720928 | tf_op jit(solution)/shard_map/ppermute | solution.py:17
  960.2 5.2 slice_convert_fusion
  965.4 6.3 copy.70
  971.7 5.6 copy.71
  977.3 6.2 copy.75
  983.6 6.3 copy.68
  989.9 5.6 copy.69
  995.5 6.3 copy.74
  (767 shorter events, 315.5 us)
Async XLA Ops:
  2.6 38.9 %collective-permute-start.27 = (bf16[256,512]{1,0:T(8,128)(2,1)}, bf16[256,512]{1,0:T(8,128)(2,1)}, u32[]{:S(2)}, u32[]{:S(2)}) collective-permute-start(bf16[256,512]{1,0:T(8,128)(2,1)} %constant_dynamic-slice_fusion.51), channel_id=1, source_target_pairs={{0,6},{1,7},{2,4},{3,5},{4,2},{5,3},{6,0},{7,1},{8,14},{9,15},{10,... | collective-permute-start | bytes 786440 | tf_op jit(solution)/shard_map/ppermute | solution.py:17
  4.2 37.5 %collective-permute-start.22 = (bf16[256,512]{1,0:T(8,128)(2,1)}, bf16[256,512]{1,0:T(8,128)(2,1)}, u32[]{:S(2)}, u32[]{:S(2)}) collective-permute-start(bf16[256,512]{1,0:T(8,128)(2,1)} %constant_dynamic-slice_fusion.51), channel_id=1, source_target_pairs={{0,2},{1,3},{2,0},{3,1},{4,6},{5,7},{6,4},{7,5},{8,10},{9,11},{10,... | collective-permute-start | bytes 786440 | tf_op jit(solution)/shard_map/ppermute | solution.py:17
  11.2 36.1 %collective-permute-start.3 = (bf16[272,768]{1,0:T(8,128)(2,1)}, bf16[272,768]{1,0:T(8,128)(2,1)}, u32[]{:S(2)}, u32[]{:S(2)}) collective-permute-start(bf16[272,768]{1,0:T(8,128)(2,1)} %pad_maximum_fusion.24), channel_id=1, source_target_pairs={{0,6},{1,7},{2,4},{3,5},{4,2},{5,3},{6,0},{7,1},{8,14},{9,15},{10,... | collective-permute-start | bytes 1253384 | tf_op jit(solution)/shard_map/ppermute | solution.py:17
  11.2 32.5 %collective-permute-start.1 = (bf16[272,768]{1,0:T(8,128)(2,1)}, bf16[272,768]{1,0:T(8,128)(2,1)}, u32[]{:S(2)}, u32[]{:S(2)}) collective-permute-start(bf16[272,768]{1,0:T(8,128)(2,1)} %pad_maximum_fusion.24), channel_id=1, source_target_pairs={{0,2},{1,3},{2,0},{3,1},{4,6},{5,7},{6,4},{7,5},{8,10},{9,11},{10,... | collective-permute-start | bytes 1253384 | tf_op jit(solution)/shard_map/ppermute | solution.py:17
  12.7 26.2 %collective-permute-start = (bf16[16,256]{1,0:T(8,128)(2,1)}, bf16[16,256]{1,0:T(8,128)(2,1)}, u32[]{:S(2)}, u32[]{:S(2)}) collective-permute-start(bf16[16,256]{1,0:T(8,128)(2,1)} %pad_slice_fusion.2), channel_id=1, source_target_pairs={{0,1},{1,0},{2,3},{3,2},{4,5},{5,4},{6,7},{7,6},{8,9},{9,8},{10,11... | collective-permute-start | bytes 24584 | tf_op jit(solution)/shard_map/ppermute | solution.py:17
  40.3 28.3 %collective-permute-start.46 = (bf16[176,2048]{1,0:T(8,128)(2,1)}, bf16[176,2048]{1,0:T(8,128)(2,1)S(1)}, u32[]{:S(2)}, u32[]{:S(2)}) collective-permute-start(bf16[176,2048]{1,0:T(8,128)(2,1)} %get-tuple-element.51), channel_id=1, source_target_pairs={{0,2},{1,3},{2,0},{3,1},{4,6},{5,7},{6,4},{7,5},{8,10},{9,11},{10,... | collective-permute-start | bytes 2162696 | tf_op jit(solution)/shard_map/ppermute | solution.py:17
  41.5 25.0 %collective-permute-start.45 = (bf16[176,2048]{1,0:T(8,128)(2,1)}, bf16[176,2048]{1,0:T(8,128)(2,1)S(1)}, u32[]{:S(2)}, u32[]{:S(2)}) collective-permute-start(bf16[176,2048]{1,0:T(8,128)(2,1)} %get-tuple-element.51), channel_id=1, source_target_pairs={{0,1},{1,0},{2,3},{3,2},{4,5},{5,4},{6,7},{7,6},{8,9},{9,8},{10,11... | collective-permute-start | bytes 2162696 | tf_op jit(solution)/shard_map/ppermute | solution.py:17
  41.6 22.9 %collective-permute-start.28 = (bf16[256,512]{1,0:T(8,128)(2,1)}, bf16[256,512]{1,0:T(8,128)(2,1)S(1)}, u32[]{:S(2)}, u32[]{:S(2)}) collective-permute-start(bf16[256,512]{1,0:T(8,128)(2,1)} %collective-permute-done.27), channel_id=1, source_target_pairs={{0,2},{1,3},{2,0},{3,1},{4,6},{5,7},{6,4},{7,5},{8,10},{9,11},{10,... | collective-permute-start | bytes 786440 | tf_op jit(solution)/shard_map/ppermute | solution.py:17
  47.2 84.4 %collective-permute-start.59 = (bf16[256,2048]{1,0:T(8,128)(2,1)}, bf16[256,2048]{1,0:T(8,128)(2,1)}, u32[]{:S(2)}, u32[]{:S(2)}) collective-permute-start(bf16[256,2048]{1,0:T(8,128)(2,1)} %get-tuple-element.47), channel_id=1, source_target_pairs={{0,16},{8,24},{16,0},{24,8},{1,17},{9,25},{17,1},{25,9},{2,18},{10... | collective-permute-start | bytes 3145736 | tf_op jit(solution)/shard_map/ppermute | solution.py:17
  52.4 31.7 %collective-permute-start.24 = (bf16[512,512]{1,0:T(8,128)(2,1)S(1)}, bf16[512,512]{1,0:T(8,128)(2,1)S(1)}, u32[]{:S(2)}, u32[]{:S(2)}) collective-permute-start(bf16[512,512]{1,0:T(8,128)(2,1)S(1)} %pad_maximum_fusion.23), channel_id=1, source_target_pairs={{0,16},{8,24},{16,0},{24,8},{1,17},{9,25},{17,1},{25,9},{2,18},{10... | collective-permute-start | bytes 1572872 | tf_op jit(solution)/shard_map/ppermute | solution.py:17
  68.6 72.1 %collective-permute-start.58 = (bf16[256,2048]{1,0:T(8,128)(2,1)}, bf16[256,2048]{1,0:T(8,128)(2,1)}, u32[]{:S(2)}, u32[]{:S(2)}) collective-permute-start(bf16[256,2048]{1,0:T(8,128)(2,1)} %get-tuple-element.47), channel_id=1, source_target_pairs={{0,8},{8,0},{16,24},{24,16},{1,9},{9,1},{17,25},{25,17},{2,10},{10... | collective-permute-start | bytes 3145736 | tf_op jit(solution)/shard_map/ppermute | solution.py:17
  86.4 27.3 %collective-permute-start.7 = (bf16[512,512]{1,0:T(8,128)(2,1)S(1)}, bf16[512,512]{1,0:T(8,128)(2,1)S(1)}, u32[]{:S(2)}, u32[]{:S(2)}) collective-permute-start(bf16[512,512]{1,0:T(8,128)(2,1)S(1)} %pad_maximum_fusion.21), channel_id=1, source_target_pairs={{0,8},{8,0},{16,24},{24,16},{1,9},{9,1},{17,25},{25,17},{2,10},{10... | collective-permute-start | bytes 1572872 | tf_op jit(solution)/shard_map/ppermute | solution.py:17
  90.0 24.4 %collective-permute-start.18 = (bf16[272,256]{1,0:T(8,128)(2,1)S(1)}, bf16[272,256]{1,0:T(8,128)(2,1)S(1)}, u32[]{:S(2)}, u32[]{:S(2)}) collective-permute-start(bf16[272,256]{1,0:T(8,128)(2,1)S(1)} %slice.585), channel_id=1, source_target_pairs={{0,1},{1,0},{2,3},{3,2},{4,5},{5,4},{6,7},{7,6},{8,9},{9,8},{10,11... | collective-permute-start | bytes 417800 | tf_op jit(solution)/shard_map/ppermute | solution.py:17
  97.6 45.5 %collective-permute-start.48 = (bf16[176,2048]{1,0:T(8,128)(2,1)}, bf16[176,2048]{1,0:T(8,128)(2,1)}, u32[]{:S(2)}, u32[]{:S(2)}) collective-permute-start(bf16[176,2048]{1,0:T(8,128)(2,1)} %get-tuple-element.51), channel_id=1, source_target_pairs={{0,6},{1,7},{2,4},{3,5},{4,2},{5,3},{6,0},{7,1},{8,14},{9,15},{10,... | collective-permute-start | bytes 2162696 | tf_op jit(solution)/shard_map/ppermute | solution.py:17
  131.6 23.1 %collective-permute-start.10 = (bf16[256,512]{1,0:T(8,128)(2,1)}, bf16[256,512]{1,0:T(8,128)(2,1)}, u32[]{:S(2)}, u32[]{:S(2)}) collective-permute-start(bf16[256,512]{1,0:T(8,128)(2,1)} %slice.572), channel_id=1, source_target_pairs={{0,8},{8,0},{16,24},{24,16},{1,9},{9,1},{17,25},{25,17},{2,10},{10... | collective-permute-start | bytes 786440 | tf_op jit(solution)/shard_map/ppermute | solution.py:17
  140.7 24.8 %collective-permute-start.12 = (bf16[512,512]{1,0:T(8,128)(2,1)}, bf16[512,512]{1,0:T(8,128)(2,1)S(1)}, u32[]{:S(2)}, u32[]{:S(2)}) collective-permute-start(bf16[512,512]{1,0:T(8,128)(2,1)} %pad_maximum_fusion.22), channel_id=1, source_target_pairs={{0,16},{8,24},{16,0},{24,8},{1,17},{9,25},{17,1},{25,9},{2,18},{10... | collective-permute-start | bytes 1572872 | tf_op jit(solution)/shard_map/ppermute | solution.py:17
  143.2 22.4 %collective-permute-start.11 = (bf16[512,512]{1,0:T(8,128)(2,1)S(1)}, bf16[512,512]{1,0:T(8,128)(2,1)S(1)}, u32[]{:S(2)}, u32[]{:S(2)}) collective-permute-start(bf16[512,512]{1,0:T(8,128)(2,1)S(1)} %copy-done.74), channel_id=1, source_target_pairs={{0,8},{8,0},{16,24},{24,16},{1,9},{9,1},{17,25},{25,17},{2,10},{10... | collective-permute-start | bytes 1572872 | tf_op jit(solution)/shard_map/ppermute | solution.py:17
  153.2 35.7 %collective-permute-start.38 = (bf16[256,2816]{0,1:T(8,128)(2,1)S(1)}, bf16[256,2816]{0,1:T(8,128)(2,1)S(1)}, u32[]{:S(2)}, u32[]{:S(2)}) collective-permute-start(bf16[256,2816]{0,1:T(8,128)(2,1)S(1)} %copy-done.44), channel_id=1, source_target_pairs={{0,1},{1,0},{2,3},{3,2},{4,5},{5,4},{6,7},{7,6},{8,9},{9,8},{10,11... | collective-permute-start | bytes 4325384 | tf_op jit(solution)/shard_map/ppermute | solution.py:17
  163.2 34.5 %collective-permute-start.39 = (bf16[256,2816]{0,1:T(8,128)(2,1)S(1)}, bf16[256,2816]{0,1:T(8,128)(2,1)S(1)}, u32[]{:S(2)}, u32[]{:S(2)}) collective-permute-start(bf16[256,2816]{0,1:T(8,128)(2,1)S(1)} %copy-done.44), channel_id=1, source_target_pairs={{0,2},{1,3},{2,0},{3,1},{4,6},{5,7},{6,4},{7,5},{8,10},{9,11},{10,... | collective-permute-start | bytes 4325384 | tf_op jit(solution)/shard_map/ppermute | solution.py:17
  163.5 80.1 %collective-permute-start.41 = (bf16[256,2816]{0,1:T(8,128)(2,1)S(1)}, bf16[256,2816]{0,1:T(8,128)(2,1)}, u32[]{:S(2)}, u32[]{:S(2)}) collective-permute-start(bf16[256,2816]{0,1:T(8,128)(2,1)S(1)} %copy-done.44), channel_id=1, source_target_pairs={{0,6},{1,7},{2,4},{3,5},{4,2},{5,3},{6,0},{7,1},{8,14},{9,15},{10,... | collective-permute-start | bytes 4325384 | tf_op jit(solution)/shard_map/ppermute | solution.py:17
  165.5 27.3 %collective-permute-start.47 = (bf16[176,2048]{1,0:T(8,128)(2,1)S(1)}, bf16[176,2048]{1,0:T(8,128)(2,1)S(1)}, u32[]{:S(2)}, u32[]{:S(2)}) collective-permute-start(bf16[176,2048]{1,0:T(8,128)(2,1)S(1)} %copy-done.71), channel_id=1, source_target_pairs={{0,1},{1,0},{2,3},{3,2},{4,5},{5,4},{6,7},{7,6},{8,9},{9,8},{10,11... | collective-permute-start | bytes 2162696 | tf_op jit(solution)/shard_map/ppermute | solution.py:17
  165.6 23.1 %collective-permute-start.9 = (bf16[256,512]{1,0:T(8,128)(2,1)S(1)}, bf16[256,512]{1,0:T(8,128)(2,1)S(1)}, u32[]{:S(2)}, u32[]{:S(2)}) collective-permute-start(bf16[256,512]{1,0:T(8,128)(2,1)S(1)} %copy-done.89), channel_id=1, source_target_pairs={{0,16},{8,24},{16,0},{24,8},{1,17},{9,25},{17,1},{25,9},{2,18},{10... | collective-permute-start | bytes 786440 | tf_op jit(solution)/shard_map/ppermute | solution.py:17
  188.9 54.2 %collective-permute-start.49 = (bf16[176,2048]{1,0:T(8,128)(2,1)}, bf16[176,2048]{1,0:T(8,128)(2,1)S(1)}, u32[]{:S(2)}, u32[]{:S(2)}) collective-permute-start(bf16[176,2048]{1,0:T(8,128)(2,1)} %collective-permute-done.48), channel_id=1, source_target_pairs={{0,2},{1,3},{2,0},{3,1},{4,6},{5,7},{6,4},{7,5},{8,10},{9,11},{10,... | collective-permute-start | bytes 2162696 | tf_op jit(solution)/shard_map/ppermute | solution.py:17
  192.8 52.3 %collective-permute-start.14 = (bf16[256,512]{1,0:T(8,128)(2,1)S(1)}, bf16[256,512]{1,0:T(8,128)(2,1)S(1)}, u32[]{:S(2)}, u32[]{:S(2)}) collective-permute-start(bf16[256,512]{1,0:T(8,128)(2,1)S(1)} %slice.576), channel_id=1, source_target_pairs={{0,8},{8,0},{16,24},{24,16},{1,9},{9,1},{17,25},{25,17},{2,10},{10... | collective-permute-start | bytes 786440 | tf_op jit(solution)/shard_map/ppermute | solution.py:17
  197.7 48.1 %collective-permute-start.13 = (bf16[256,512]{1,0:T(8,128)(2,1)S(1)}, bf16[256,512]{1,0:T(8,128)(2,1)}, u32[]{:S(2)}, u32[]{:S(2)}) collective-permute-start(bf16[256,512]{1,0:T(8,128)(2,1)S(1)} %slice.575), channel_id=1, source_target_pairs={{0,16},{8,24},{16,0},{24,8},{1,17},{9,25},{17,1},{25,9},{2,18},{10... | collective-permute-start | bytes 786440 | tf_op jit(solution)/shard_map/ppermute | solution.py:17
  200.6 100.6 %collective-permute-start.71 = (bf16[256,2048]{1,0:T(8,128)(2,1)S(1)}, bf16[256,2048]{1,0:T(8,128)(2,1)S(1)}, u32[]{:S(2)}, u32[]{:S(2)}) collective-permute-start(bf16[256,2048]{1,0:T(8,128)(2,1)S(1)} %copy-done.47), channel_id=1, source_target_pairs={{0,16},{8,24},{16,0},{24,8},{1,17},{9,25},{17,1},{25,9},{2,18},{10... | collective-permute-start | bytes 3145736 | tf_op jit(solution)/shard_map/ppermute | solution.py:17
  243.1 55.1 %collective-permute-start.70 = (bf16[256,2048]{1,0:T(8,128)(2,1)S(1)}, bf16[256,2048]{1,0:T(8,128)(2,1)S(1)}, u32[]{:S(2)}, u32[]{:S(2)}) collective-permute-start(bf16[256,2048]{1,0:T(8,128)(2,1)S(1)} %copy-done.47), channel_id=1, source_target_pairs={{0,8},{8,0},{16,24},{24,16},{1,9},{9,1},{17,25},{25,17},{2,10},{10... | collective-permute-start | bytes 3145736 | tf_op jit(solution)/shard_map/ppermute | solution.py:17
  243.6 53.1 %collective-permute-start.61 = (bf16[128,2048]{1,0:T(8,128)(2,1)S(1)}, bf16[128,2048]{1,0:T(8,128)(2,1)S(1)}, u32[]{:S(2)}, u32[]{:S(2)}) collective-permute-start(bf16[128,2048]{1,0:T(8,128)(2,1)S(1)} %slice.612), channel_id=1, source_target_pairs={{0,8},{8,0},{16,24},{24,16},{1,9},{9,1},{17,25},{25,17},{2,10},{10... | collective-permute-start | bytes 1572872 | tf_op jit(solution)/shard_map/ppermute | solution.py:17
  245.1 53.0 %collective-permute-start.60 = (bf16[128,2048]{1,0:T(8,128)(2,1)S(1)}, bf16[128,2048]{1,0:T(8,128)(2,1)}, u32[]{:S(2)}, u32[]{:S(2)}) collective-permute-start(bf16[128,2048]{1,0:T(8,128)(2,1)S(1)} %slice.611), channel_id=1, source_target_pairs={{0,16},{8,24},{16,0},{24,8},{1,17},{9,25},{17,1},{25,9},{2,18},{10... | collective-permute-start | bytes 1572872 | tf_op jit(solution)/shard_map/ppermute | solution.py:17
  245.8 96.1 %collective-permute-start.33 = (bf16[1024,2048]{1,0:T(8,128)(2,1)S(1)}, bf16[1024,2048]{1,0:T(8,128)(2,1)S(1)}, u32[]{:S(2)}, u32[]{:S(2)}) collective-permute-start(bf16[1024,2048]{1,0:T(8,128)(2,1)S(1)} %maximum_maximum_fusion.1), channel_id=1, source_target_pairs={{0,1},{1,0},{2,3},{3,2},{4,5},{5,4},{6,7},{7,6},{8,9},{9,8},{10,11... | collective-permute-start | bytes 12582920 | tf_op jit(solution)/shard_map/ppermute | solution.py:17
  296.7 54.7 %collective-permute-start.15 = (bf16[1024,2048]{1,0:T(8,128)(2,1)}, bf16[1024,2048]{1,0:T(8,128)(2,1)}, u32[]{:S(2)}, u32[]{:S(2)}) collective-permute-start(bf16[1024,2048]{1,0:T(8,128)(2,1)} %maximum_maximum_fusion), channel_id=1, source_target_pairs={{0,1},{1,0},{2,3},{3,2},{4,5},{5,4},{6,7},{7,6},{8,9},{9,8},{10,11... | collective-permute-start | bytes 12582920 | tf_op jit(solution)/shard_map/ppermute | solution.py:17
  298.2 34.2 %collective-permute-start.42 = (bf16[256,2816]{0,1:T(8,128)(2,1)}, bf16[256,2816]{0,1:T(8,128)(2,1)S(1)}, u32[]{:S(2)}, u32[]{:S(2)}) collective-permute-start(bf16[256,2816]{0,1:T(8,128)(2,1)} %collective-permute-done.41), channel_id=1, source_target_pairs={{0,2},{1,3},{2,0},{3,1},{4,6},{5,7},{6,4},{7,5},{8,10},{9,11},{10,... | collective-permute-start | bytes 4325384 | tf_op jit(solution)/shard_map/ppermute | solution.py:17
  305.1 30.4 %collective-permute-start.40 = (bf16[256,2816]{0,1:T(8,128)(2,1)S(1)}, bf16[256,2816]{0,1:T(8,128)(2,1)S(1)}, u32[]{:S(2)}, u32[]{:S(2)}) collective-permute-start(bf16[256,2816]{0,1:T(8,128)(2,1)S(1)} %collective-permute-done.39), channel_id=1, source_target_pairs={{0,1},{1,0},{2,3},{3,2},{4,5},{5,4},{6,7},{7,6},{8,9},{9,8},{10,11... | collective-permute-start | bytes 4325384 | tf_op jit(solution)/shard_map/ppermute | solution.py:17
  334.1 74.0 %collective-permute-start.44 = (bf16[256,2816]{0,1:T(8,128)(2,1)}, bf16[256,2816]{0,1:T(8,128)(2,1)}, u32[]{:S(2)}, u32[]{:S(2)}) collective-permute-start(bf16[256,2816]{0,1:T(8,128)(2,1)} %collective-permute-done.41), channel_id=1, source_target_pairs={{0,1},{1,0},{2,3},{3,2},{4,5},{5,4},{6,7},{7,6},{8,9},{9,8},{10,11... | collective-permute-start | bytes 4325384 | tf_op jit(solution)/shard_map/ppermute | solution.py:17
  395.6 26.1 %collective-permute-start.89 = (bf16[256,2048]{1,0:T(8,128)(2,1)S(1)}, bf16[256,2048]{1,0:T(8,128)(2,1)S(1)}, u32[]{:S(2)}, u32[]{:S(2)}) collective-permute-start(bf16[256,2048]{1,0:T(8,128)(2,1)S(1)} %get-tuple-element.132), channel_id=1, source_target_pairs={{0,16},{8,24},{16,0},{24,8},{1,17},{9,25},{17,1},{25,9},{2,18},{10... | collective-permute-start | bytes 3145736 | tf_op jit(solution)/shard_map/ppermute | solution.py:17
  397.0 26.1 %collective-permute-start.88 = (bf16[256,2048]{1,0:T(8,128)(2,1)S(1)}, bf16[256,2048]{1,0:T(8,128)(2,1)S(1)}, u32[]{:S(2)}, u32[]{:S(2)}) collective-permute-start(bf16[256,2048]{1,0:T(8,128)(2,1)S(1)} %get-tuple-element.132), channel_id=1, source_target_pairs={{0,8},{8,0},{16,24},{24,16},{1,9},{9,1},{17,25},{25,17},{2,10},{10... | collective-permute-start | bytes 3145736 | tf_op jit(solution)/shard_map/ppermute | solution.py:17
  405.9 38.2 %collective-permute-start.35 = (bf16[256,2048]{1,0:T(8,128)(2,1)S(1)}, bf16[256,2048]{1,0:T(8,128)(2,1)S(1)}, u32[]{:S(2)}, u32[]{:S(2)}) collective-permute-start(bf16[256,2048]{1,0:T(8,128)(2,1)S(1)} %get-tuple-element.175), channel_id=1, source_target_pairs={{0,16},{8,24},{16,0},{24,8},{1,17},{9,25},{17,1},{25,9},{2,18},{10... | collective-permute-start | bytes 3145736 | tf_op jit(solution)/shard_map/ppermute | solution.py:17
  406.7 38.9 %collective-permute-start.34 = (bf16[256,2048]{1,0:T(8,128)(2,1)S(1)}, bf16[256,2048]{1,0:T(8,128)(2,1)S(1)}, u32[]{:S(2)}, u32[]{:S(2)}) collective-permute-start(bf16[256,2048]{1,0:T(8,128)(2,1)S(1)} %get-tuple-element.175), channel_id=1, source_target_pairs={{0,8},{8,0},{16,24},{24,16},{1,9},{9,1},{17,25},{25,17},{2,10},{10... | collective-permute-start | bytes 3145736 | tf_op jit(solution)/shard_map/ppermute | solution.py:17
  421.7 143.9 %collective-permute-start.91 = (bf16[128,2048]{1,0:T(8,128)(2,1)S(1)}, bf16[128,2048]{1,0:T(8,128)(2,1)S(1)}, u32[]{:S(2)}, u32[]{:S(2)}) collective-permute-start(bf16[128,2048]{1,0:T(8,128)(2,1)S(1)} %slice.653), channel_id=1, source_target_pairs={{0,8},{8,0},{16,24},{24,16},{1,9},{9,1},{17,25},{25,17},{2,10},{10... | collective-permute-start | bytes 1572872 | tf_op jit(solution)/shard_map/ppermute | solution.py:17
  423.1 139.3 %collective-permute-start.90 = (bf16[128,2048]{1,0:T(8,128)(2,1)S(1)}, bf16[128,2048]{1,0:T(8,128)(2,1)S(1)}, u32[]{:S(2)}, u32[]{:S(2)}) collective-permute-start(bf16[128,2048]{1,0:T(8,128)(2,1)S(1)} %slice.652), channel_id=1, source_target_pairs={{0,16},{8,24},{16,0},{24,8},{1,17},{9,25},{17,1},{25,9},{2,18},{10... | collective-permute-start | bytes 1572872 | tf_op jit(solution)/shard_map/ppermute | solution.py:17
  444.2 22.6 %collective-permute-start.37 = (bf16[128,2048]{1,0:T(8,128)(2,1)S(1)}, bf16[128,2048]{1,0:T(8,128)(2,1)S(1)}, u32[]{:S(2)}, u32[]{:S(2)}) collective-permute-start(bf16[128,2048]{1,0:T(8,128)(2,1)S(1)} %slice.601), channel_id=1, source_target_pairs={{0,8},{8,0},{16,24},{24,16},{1,9},{9,1},{17,25},{25,17},{2,10},{10... | collective-permute-start | bytes 1572872 | tf_op jit(solution)/shard_map/ppermute | solution.py:17
  570.2 22.8 %collective-permute-start.65 = (bf16[128,2048]{1,0:T(8,128)(2,1)}, bf16[128,2048]{1,0:T(8,128)(2,1)S(1)}, u32[]{:S(2)}, u32[]{:S(2)}) collective-permute-start(bf16[128,2048]{1,0:T(8,128)(2,1)} %get-tuple-element.81), channel_id=1, source_target_pairs={{0,16},{8,24},{16,0},{24,8},{1,17},{9,25},{17,1},{25,9},{2,18},{10... | collective-permute-start | bytes 1572872 | tf_op jit(solution)/shard_map/ppermute | solution.py:17
  581.8 22.5 %collective-permute-start.67 = (bf16[128,2048]{1,0:T(8,128)(2,1)S(1)}, bf16[128,2048]{1,0:T(8,128)(2,1)S(1)}, u32[]{:S(2)}, u32[]{:S(2)}) collective-permute-start(bf16[128,2048]{1,0:T(8,128)(2,1)S(1)} %get-tuple-element.85), channel_id=1, source_target_pairs={{0,16},{8,24},{16,0},{24,8},{1,17},{9,25},{17,1},{25,9},{2,18},{10... | collective-permute-start | bytes 1572872 | tf_op jit(solution)/shard_map/ppermute | solution.py:17
  582.9 22.5 %collective-permute-start.63 = (bf16[128,2048]{1,0:T(8,128)(2,1)S(1)}, bf16[128,2048]{1,0:T(8,128)(2,1)S(1)}, u32[]{:S(2)}, u32[]{:S(2)}) collective-permute-start(bf16[128,2048]{1,0:T(8,128)(2,1)S(1)} %get-tuple-element.86), channel_id=1, source_target_pairs={{0,8},{8,0},{16,24},{24,16},{1,9},{9,1},{17,25},{25,17},{2,10},{10... | collective-permute-start | bytes 1572872 | tf_op jit(solution)/shard_map/ppermute | solution.py:17
  584.8 30.7 %collective-permute-start.55 = (bf16[128,2048]{1,0:T(8,128)(2,1)S(1)}, bf16[128,2048]{1,0:T(8,128)(2,1)S(1)}, u32[]{:S(2)}, u32[]{:S(2)}) collective-permute-start(bf16[128,2048]{1,0:T(8,128)(2,1)S(1)} %copy-done.77), channel_id=1, source_target_pairs={{0,16},{8,24},{16,0},{24,8},{1,17},{9,25},{17,1},{25,9},{2,18},{10... | collective-permute-start | bytes 1572872 | tf_op jit(solution)/shard_map/ppermute | solution.py:17
  593.0 23.6 %collective-permute-start.54 = (bf16[128,2048]{1,0:T(8,128)(2,1)S(1)}, bf16[128,2048]{1,0:T(8,128)(2,1)S(1)}, u32[]{:S(2)}, u32[]{:S(2)}) collective-permute-start(bf16[128,2048]{1,0:T(8,128)(2,1)S(1)} %copy-done.76), channel_id=1, source_target_pairs={{0,8},{8,0},{16,24},{24,16},{1,9},{9,1},{17,25},{25,17},{2,10},{10... | collective-permute-start | bytes 1572872 | tf_op jit(solution)/shard_map/ppermute | solution.py:17
  594.5 115.1 %collective-permute-start.110 = (bf16[256,2816]{1,0:T(8,128)(2,1)}, bf16[256,2816]{1,0:T(8,128)(2,1)}, u32[]{:S(2)}, u32[]{:S(2)}) collective-permute-start(bf16[256,2816]{1,0:T(8,128)(2,1)} %get-tuple-element.59), channel_id=1, source_target_pairs={{0,1},{1,0},{2,3},{3,2},{4,5},{5,4},{6,7},{7,6},{8,9},{9,8},{10,11... | collective-permute-start | bytes 4325384 | tf_op jit(solution)/shard_map/ppermute | solution.py:17
  615.5 94.9 %collective-permute-start.107 = (bf16[256,2816]{1,0:T(8,128)(2,1)}, bf16[256,2816]{1,0:T(8,128)(2,1)}, u32[]{:S(2)}, u32[]{:S(2)}) collective-permute-start(bf16[256,2816]{1,0:T(8,128)(2,1)} %get-tuple-element.61), channel_id=1, source_target_pairs={{0,1},{1,0},{2,3},{3,2},{4,5},{5,4},{6,7},{7,6},{8,9},{9,8},{10,11... | collective-permute-start | bytes 4325384 | tf_op jit(solution)/shard_map/ppermute | solution.py:17
  629.0 75.9 %collective-permute-start.94 = (bf16[256,512]{1,0:T(8,128)(2,1)}, bf16[256,512]{1,0:T(8,128)(2,1)}, u32[]{:S(2)}, u32[]{:S(2)}) collective-permute-start(bf16[256,512]{1,0:T(8,128)(2,1)} %get-tuple-element.172), channel_id=1, source_target_pairs={{0,24},{8,16},{16,8},{24,0},{1,25},{9,17},{17,9},{25,1},{2,26},{10... | collective-permute-start | bytes 786440 | tf_op jit(solution)/shard_map/ppermute | solution.py:17
  744.5 78.4 %collective-permute-start.109 = (bf16[256,2816]{1,0:T(8,128)(2,1)S(1)}, bf16[256,2816]{1,0:T(8,128)(2,1)S(1)}, u32[]{:S(2)}, u32[]{:S(2)}) collective-permute-start(bf16[256,2816]{1,0:T(8,128)(2,1)S(1)} %copy-done.45), channel_id=1, source_target_pairs={{0,1},{1,0},{2,3},{3,2},{4,5},{5,4},{6,7},{7,6},{8,9},{9,8},{10,11... | collective-permute-start | bytes 4325384 | tf_op jit(solution)/shard_map/ppermute | solution.py:17
  745.0 23.6 %collective-permute-start.119 = (bf16[176,2048]{1,0:T(8,128)(2,1)S(1)}, bf16[176,2048]{1,0:T(8,128)(2,1)S(1)}, u32[]{:S(2)}, u32[]{:S(2)}) collective-permute-start(bf16[176,2048]{1,0:T(8,128)(2,1)S(1)} %copy-done.66), channel_id=1, source_target_pairs={{0,2},{1,3},{2,0},{3,1},{4,6},{5,7},{6,4},{7,5},{8,10},{9,11},{10,... | collective-permute-start | bytes 2162696 | tf_op jit(solution)/shard_map/ppermute | solution.py:17
  747.0 77.1 %collective-permute-start.111 = (bf16[256,2816]{1,0:T(8,128)(2,1)S(1)}, bf16[256,2816]{1,0:T(8,128)(2,1)S(1)}, u32[]{:S(2)}, u32[]{:S(2)}) collective-permute-start(bf16[256,2816]{1,0:T(8,128)(2,1)S(1)} %get-tuple-element.63), channel_id=1, source_target_pairs={{0,2},{1,3},{2,0},{3,1},{4,6},{5,7},{6,4},{7,5},{8,10},{9,11},{10,... | collective-permute-start | bytes 4325384 | tf_op jit(solution)/shard_map/ppermute | solution.py:17
  756.3 57.5 %collective-permute-start.103 = (bf16[256,512]{0,1:T(8,128)(2,1)S(1)}, bf16[256,512]{0,1:T(8,128)(2,1)S(1)}, u32[]{:S(2)}, u32[]{:S(2)}) collective-permute-start(bf16[256,512]{0,1:T(8,128)(2,1)S(1)} %add_convert_fusion.19), channel_id=1, source_target_pairs={{0,16},{8,24},{16,0},{24,8},{1,17},{9,25},{17,1},{25,9},{2,18},{10... | collective-permute-start | bytes 786440 | tf_op jit(solution)/shard_map/ppermute | solution.py:17
  768.7 51.6 %collective-permute-start.80 = (bf16[272,768]{1,0:T(8,128)(2,1)S(1)}, bf16[272,768]{1,0:T(8,128)(2,1)S(1)}, u32[]{:S(2)}, u32[]{:S(2)}) collective-permute-start(bf16[272,768]{1,0:T(8,128)(2,1)S(1)} %fusion.79), channel_id=1, source_target_pairs={{0,1},{1,0},{2,3},{3,2},{4,5},{5,4},{6,7},{7,6},{8,9},{9,8},{10,11... | collective-permute-start | bytes 1253384 | tf_op jit(solution)/shard_map/ppermute | solution.py:17
  770.9 50.5 %collective-permute-start.82 = (bf16[272,768]{1,0:T(8,128)(2,1)S(1)}, bf16[272,768]{1,0:T(8,128)(2,1)S(1)}, u32[]{:S(2)}, u32[]{:S(2)}) collective-permute-start(bf16[272,768]{1,0:T(8,128)(2,1)S(1)} %add_convert_fusion.17), channel_id=1, source_target_pairs={{0,2},{1,3},{2,0},{3,1},{4,6},{5,7},{6,4},{7,5},{8,10},{9,11},{10,... | collective-permute-start | bytes 1253384 | tf_op jit(solution)/shard_map/ppermute | solution.py:17
  828.6 43.2 %collective-permute-start.106 = (bf16[256,2816]{1,0:T(8,128)(2,1)}, bf16[256,2816]{1,0:T(8,128)(2,1)}, u32[]{:S(2)}, u32[]{:S(2)}) collective-permute-start(bf16[256,2816]{1,0:T(8,128)(2,1)} %get-tuple-element.58), channel_id=1, source_target_pairs={{0,1},{1,0},{2,3},{3,2},{4,5},{5,4},{6,7},{7,6},{8,9},{9,8},{10,11... | collective-permute-start | bytes 4325384 | tf_op jit(solution)/shard_map/ppermute | solution.py:17
  828.6 44.2 %collective-permute-start.108 = (bf16[256,2816]{1,0:T(8,128)(2,1)}, bf16[256,2816]{1,0:T(8,128)(2,1)}, u32[]{:S(2)}, u32[]{:S(2)}) collective-permute-start(bf16[256,2816]{1,0:T(8,128)(2,1)} %get-tuple-element.62), channel_id=1, source_target_pairs={{0,2},{1,3},{2,0},{3,1},{4,6},{5,7},{6,4},{7,5},{8,10},{9,11},{10,... | collective-permute-start | bytes 4325384 | tf_op jit(solution)/shard_map/ppermute | solution.py:17
  831.6 74.5 %collective-permute-start.112 = (bf16[256,2816]{1,0:T(8,128)(2,1)}, bf16[256,2816]{1,0:T(8,128)(2,1)}, u32[]{:S(2)}, u32[]{:S(2)}) collective-permute-start(bf16[256,2816]{1,0:T(8,128)(2,1)} %add_convert_fusion.1), channel_id=1, source_target_pairs={{0,6},{1,7},{2,4},{3,5},{4,2},{5,3},{6,0},{7,1},{8,14},{9,15},{10,... | collective-permute-start | bytes 4325384 | tf_op jit(solution)/shard_map/ppermute | solution.py:17
  864.5 45.5 %collective-permute-start.127 = (bf16[88,2048]{1,0:T(8,128)(2,1)S(1)}, bf16[88,2048]{1,0:T(8,128)(2,1)S(1)}, u32[]{:S(2)}, u32[]{:S(2)}) collective-permute-start(bf16[88,2048]{1,0:T(8,128)(2,1)S(1)} %slice.678), channel_id=1, source_target_pairs={{0,8},{8,0},{16,24},{24,16},{1,9},{9,1},{17,25},{25,17},{2,10},{10... | collective-permute-start | bytes 1081352 | tf_op jit(solution)/shard_map/ppermute | solution.py:17
  871.8 38.2 %collective-permute-start.126 = (bf16[88,2048]{1,0:T(8,128)(2,1)S(1)}, bf16[88,2048]{1,0:T(8,128)(2,1)S(1)}, u32[]{:S(2)}, u32[]{:S(2)}) collective-permute-start(bf16[88,2048]{1,0:T(8,128)(2,1)S(1)} %slice.677), channel_id=1, source_target_pairs={{0,16},{8,24},{16,0},{24,8},{1,17},{9,25},{17,1},{25,9},{2,18},{10... | collective-permute-start | bytes 1081352 | tf_op jit(solution)/shard_map/ppermute | solution.py:17
  871.8 41.5 %collective-permute-start.86 = (bf16[136,512]{1,0:T(8,128)(2,1)S(1)}, bf16[136,512]{1,0:T(8,128)(2,1)S(1)}, u32[]{:S(2)}, u32[]{:S(2)}) collective-permute-start(bf16[136,512]{1,0:T(8,128)(2,1)S(1)} %slice.643), channel_id=1, source_target_pairs={{0,8},{8,0},{16,24},{24,16},{1,9},{9,1},{17,25},{25,17},{2,10},{10... | collective-permute-start | bytes 417800 | tf_op jit(solution)/shard_map/ppermute | solution.py:17
  872.8 40.6 %collective-permute-start.87 = (bf16[136,512]{1,0:T(8,128)(2,1)S(1)}, bf16[136,512]{1,0:T(8,128)(2,1)S(1)}, u32[]{:S(2)}, u32[]{:S(2)}) collective-permute-start(bf16[136,512]{1,0:T(8,128)(2,1)S(1)} %slice.649), channel_id=1, source_target_pairs={{0,16},{8,24},{16,0},{24,8},{1,17},{9,25},{17,1},{25,9},{2,18},{10... | collective-permute-start | bytes 417800 | tf_op jit(solution)/shard_map/ppermute | solution.py:17
  909.5 32.2 %collective-permute-start.114 = (bf16[256,2816]{1,0:T(8,128)(2,1)S(1)}, bf16[256,2816]{1,0:T(8,128)(2,1)S(1)}, u32[]{:S(2)}, u32[]{:S(2)}) collective-permute-start(bf16[256,2816]{1,0:T(8,128)(2,1)S(1)} %add_convert_fusion), channel_id=1, source_target_pairs={{0,16},{8,24},{16,0},{24,8},{1,17},{9,25},{17,1},{25,9},{2,18},{10... | collective-permute-start | bytes 4325384 | tf_op jit(solution)/shard_map/ppermute | solution.py:17
  910.0 31.9 %collective-permute-start.113 = (bf16[256,2816]{1,0:T(8,128)(2,1)S(1)}, bf16[256,2816]{1,0:T(8,128)(2,1)S(1)}, u32[]{:S(2)}, u32[]{:S(2)}) collective-permute-start(bf16[256,2816]{1,0:T(8,128)(2,1)S(1)} %add_convert_fusion), channel_id=1, source_target_pairs={{0,8},{8,0},{16,24},{24,16},{1,9},{9,1},{17,25},{25,17},{2,10},{10... | collective-permute-start | bytes 4325384 | tf_op jit(solution)/shard_map/ppermute | solution.py:17
  (190 other events, 3242.4 us)

commit v2 on v0

v2 whole, which is shorter than its diff:
```python
import functools

import jax
import jax.numpy as jnp
from jax import lax
from jax.experimental import pallas as pl
from jax.experimental.pallas import tpu as pltpu
from jax.sharding import PartitionSpec as P

WINDOW = 512


EPSILON = 1e-05
THETA = 10000.0
NEGATIVE = -1e30
BF = jnp.bfloat16
F32 = jnp.float32


def swap(block, axis, mask):
    return lax.ppermute(block, axis, [(i, i ^ mask) for i in range(lax.axis_size(axis))])


def gather_near(block):
    count = lax.axis_size("slot")
    if count != 4:
        return [block] + [swap(block, "slot", j) for j in range(1, count)]
    return [block, swap(block, "slot", 1), swap(block, "slot", 2)]


def gather_far(near):
    if lax.axis_size("slot") != 4:
        return []
    half = near[0].shape[0] // 2
    return [swap(near[1][:half], "slot", 2), swap(near[2][half:], "slot", 1)]


def scatter_pass(parts):
    if lax.axis_size("slot") != 4:
        return []
    return [swap(parts[5], "slot", 2), swap(parts[6], "slot", 1)]


def scatter_near(parts):
    if lax.axis_size("slot") != 4:
        return [swap(parts[j], "slot", j) for j in range(1, len(parts))]
    return [swap(parts[2], "slot", 1), swap(parts[3], "slot", 2)]


def scatter_far(parts, passed):
    if lax.axis_size("slot") != 4:
        return []
    low, high = passed
    return [
        swap((parts[1].astype(F32) + low.astype(F32)).astype(BF), "slot", 1),
        swap((parts[4].astype(F32) + high.astype(F32)).astype(BF), "slot", 2),
    ]


def scatter_total(parts, near, far):
    own = parts[0].astype(F32)
    if lax.axis_size("slot") != 4:
        for part in near:
            own = own + part.astype(F32)
        return own
    first = jnp.concatenate([far[0], near[0]], axis=0).astype(F32)
    second = jnp.concatenate([near[1], far[1]], axis=0).astype(F32)
    return own + first + second


def trade_slot(blocks):
    return [blocks[0]] + [swap(blocks[j], "slot", j) for j in range(1, len(blocks))]


def line_near(block):
    count = lax.axis_size("seq")
    if count != 8:
        return [block] + [swap(block, "seq", j) for j in range(2, count, 2)]
    return [block, swap(block, "seq", 2), swap(block, "seq", 6)]


def line_far(near):
    if lax.axis_size("seq") != 8:
        return []
    return [swap(near[2], "seq", 2)]


def line_all(near, far):
    return near[:2] + far + near[2:]


def shifted(block, axis, distance):
    devices = range(lax.axis_size(axis))
    route = [(i - distance, i) for i in devices if i - distance in devices]
    return lax.ppermute(block, axis, route)


def rope_tables(positions, head_width):
    half_width = head_width // 2
    exponent = jnp.arange(half_width, dtype=jnp.float32) * (2.0 / head_width)
    frequency = THETA ** (-exponent)
    angles = positions.astype(jnp.float32)[:, None] * frequency[None, :]
    return (jnp.cos(angles), jnp.sin(angles))


def dot(left, right):
    return jnp.dot(left, right, preferred_element_type=F32)


def dot_nt(left, right):
    return lax.dot_general(left, right, (((1,), (1,)), ((), ())), preferred_element_type=F32)


def dot_tn(left, right):
    return lax.dot_general(left, right, (((0,), (0,)), ((), ())), preferred_element_type=F32)


VMEM = pl.BlockSpec(memory_space=pltpu.VMEM)
SMEM = pl.BlockSpec(memory_space=pltpu.SMEM)
ANY = pl.BlockSpec(memory_space=pl.ANY)
BIG = pltpu.CompilerParams(vmem_limit_bytes=56 * 1024 * 1024)


def line_sums(mine, passed):
    count = lax.axis_size("seq") // 2
    rows = mine.shape[0] // count
    out = []
    for k in range(count):
        part = slice(k * rows, (k + 1) * rows)
        total = mine[part].astype(F32) + passed[part].astype(F32)
        out.append(total.astype(BF) if k else total)
    return out


def line_first(blocks):
    if len(blocks) != 4:
        return [swap(blocks[k], "seq", 2 * k) for k in range(1, len(blocks))]
    return [swap(blocks[1], "seq", 2), swap(blocks[2], "seq", 2)]


def line_second(blocks, first):
    if len(blocks) != 4:
        return []
    return [swap((blocks[3].astype(F32) + first[1].astype(F32)).astype(BF), "seq", 6)]


def line_total(blocks, first, second):
    parts = first[:1] + second if len(blocks) == 4 else first
    total = blocks[0]
    for part in parts:
        total = total + part.astype(F32)
    return total


def line_place(block, seq, count):
    away = block ^ seq
    return (away >> 1) + (away & 1) * (count // 2)


def line_block(place, seq, count):
    half = count // 2
    return seq ^ (2 * place if place < half else 2 * (place - half) + 1)


def line_block_at(spot, seq, count):
    half = count // 2
    return seq ^ (2 * (spot % half) + spot // half)


def line_order(values, seq, count):
    width = values.shape[1] // count
    return jnp.concatenate(
        [
            lax.dynamic_slice_in_dim(values, line_block(m, seq, count) * width, width, 1)
            for m in range(count)
        ],
        axis=1,
    )


def rms_of(values):
    return lax.rsqrt(jnp.mean(values * values, axis=-1, keepdims=True) + EPSILON)


def turn(values, cosine, sine):
    return values * cosine + pltpu.roll(values, values.shape[1] // 2, 1) * sine


def at(block, width):
    return pl.ds(pl.multiple_of(block * width, width), width)


def grouped(refs, counts):
    out, start = [], 0
    for count in counts:
        out.append(refs[start : start + count])
        start += count
    return out


def chunk_of(pieces, c, count):
    if len(pieces) == count:
        return pieces[c][...]
    rows = pieces[0].shape[0] // count
    return pieces[0][c * rows : (c + 1) * rows]


def piece_dot(left, pieces):
    total, row = None, 0
    for ref in pieces:
        rows = ref.shape[0]
        part = dot(left[:, row : row + rows], ref[...])
        total = part if total is None else total + part
        row += rows
    return total


def project_kernel(shape, *refs):
    counts, seqs = shape
    slots, count, chunks = len(counts), sum(counts), max(counts)
    place, rows_ref, gain_ref, valid_ref, cos_ref, sin_ref = refs[:6]
    mine = grouped(refs[6 : 6 + count], counts)
    theirs = grouped(refs[6 + count : 6 + 2 * count], counts)
    kv_mine, kv_theirs = refs[6 + 2 * count : 8 + 2 * count]
    normed_ref, query_ref, shared_ref, line_ref = refs[8 + 2 * count :]
    seq = place[0]
    model = rows_ref.shape[1]
    half = model // 2
    width = model // seqs
    scale = rms_of(rows_ref[...].astype(F32))
    for m in range(seqs):
        block = at(line_block(m, seq, seqs), width)
        to = slice(m * width, (m + 1) * width)
        part = rows_ref[:, block].astype(F32)
        part = (part * scale * gain_ref[:, to]).astype(BF)
        normed_ref[:, block] = part
        line_ref[:, to] = part
    cosine, sine = cos_ref[...], sin_ref[...]
    head = cosine.shape[1]
    left, right = line_ref[:, :half], line_ref[:, half:]
    col = 0
    for i in range(slots):
        total = piece_dot(left, mine[i]) + piece_dot(right, theirs[i])
        for h in range(total.shape[1] // head):
            turned = turn(total[:, h * head : (h + 1) * head], cosine, sine)
            query_ref[:, col : col + head] = turned.astype(BF)
            col += head
    kv = dot(left, kv_mine[...]) + dot(right, kv_theirs[...])
    valid = valid_ref[...]
    shared_ref[:, :head] = (turn(kv[:, :head], cosine, sine) * valid).astype(BF)
    shared_ref[:, head:] = (kv[:, head:] * valid).astype(BF)


def set_bias(place, bias_ref, step):
    @pl.when(step == 0)
    def _():
        toks, keys = bias_ref.shape
        first = place[0] * toks
        query = first + lax.broadcasted_iota(jnp.int32, (toks, keys), 0)
        key = first - WINDOW + lax.broadcasted_iota(jnp.int32, (toks, keys), 1)
        length = place[2]
        away = query - key
        good = (key >= 0) & (key < length) & (away >= 0) & (away < WINDOW) & (query < length)
        bias_ref[...] = jnp.where(good, 0.0, NEGATIVE)


def softmax_rows(place, query, keys, bias):
    head = query.shape[1]
    scores = dot_nt(query, keys) * (head**-0.5) + bias
    grown = jnp.exp(scores - jnp.max(scores, axis=-1, keepdims=True))
    toks = query.shape[0]
    pos = place[0] * toks + lax.broadcasted_iota(jnp.int32, (toks, 1), 0)
    total = jnp.sum(grown, axis=-1, keepdims=True)
    return grown * jnp.where(pos < place[2], 1.0 / total, 0.0)


def attend_kernel(rims, late, place, query_ref, *refs):
    table = refs[: rims + 1]
    out_ref, bias_ref = refs[rims + 1 + late :]
    set_bias(place, bias_ref, pl.program_id(0))
    head = query_ref.shape[1]
    keys = jnp.concatenate([ref[:, :head] for ref in table], axis=0)
    values = jnp.concatenate([ref[:, head:] for ref in table], axis=0)
    probs = softmax_rows(place, query_ref[...], keys, bias_ref[...])
    out_ref[...] = dot(probs.astype(BF), values).astype(BF)


def attend_back_kernel(rims, late, place, query_ref, grad_ref, *refs):
    table = refs[: rims + 1]
    cos_ref, sin_ref = refs[rims + 1 : rims + 3]
    gq_ref, gkv_ref, bias_ref = refs[rims + 3 + late :]
    step = pl.program_id(0)
    set_bias(place, bias_ref, step)

    @pl.when(step == 0)
    def _():
        gkv_ref[...] = jnp.zeros_like(gkv_ref)

    head = query_ref.shape[1]
    scaling = head**-0.5
    keys = jnp.concatenate([ref[:, :head] for ref in table], axis=0)
    values = jnp.concatenate([ref[:, head:] for ref in table], axis=0)
    query, grad = query_ref[...], grad_ref[...]
    probs = softmax_rows(place, query, keys, bias_ref[...])
    grad_probs = dot_nt(grad, values)
    both = probs * grad_probs
    grad_scores = (both - probs * jnp.sum(both, axis=-1, keepdims=True)).astype(BF)
    grad_query = dot(grad_scores, keys) * scaling
    gq_ref[...] = turn(grad_query, cos_ref[...], -sin_ref[...]).astype(BF)
    gkv_ref[:, :head] += dot_tn(grad_scores, query) * scaling
    gkv_ref[:, head:] += dot_tn(probs.astype(BF), grad)


def out_kernel(shape, *refs):
    counts, seqs = shape
    slots, count, chunks = len(counts), sum(counts), max(counts)
    place, att_ref, rows_ref, gain_ref = refs[:4]
    mine = grouped(refs[4 : 4 + count], counts)
    theirs = grouped(refs[4 + count : 4 + 2 * count], counts)
    middle_ref, normed_ref, plain_ref = refs[4 + 2 * count :]
    seq, slot = place[0], place[1]
    model = rows_ref.shape[1]
    half = model // 2
    width = model // seqs
    left, right = att_ref[:, :half], att_ref[:, half:]
    for i in range(slots):
        total = piece_dot(left, mine[i]) + piece_dot(right, theirs[i])
        to = at(slot ^ i, total.shape[1])
        middle_ref[:, to] = rows_ref[:, to].astype(F32) + total
    scale = rms_of(middle_ref[...])
    for m in range(seqs):
        to = at(line_block(m, seq, seqs), width)
        gain = gain_ref[:, m * width : (m + 1) * width]
        normed_ref[:, to] = (middle_ref[:, to] * scale * gain).astype(BF)
        plain_ref[:, to] = att_ref[:, m * width : (m + 1) * width]


def mid_back_kernel(shape, *refs):
    counts, seqs = shape
    slots, count, chunks = len(counts), sum(counts), max(counts)
    place, grad_ref, middle_ref, cot_ref, gain_ref = refs[:5]
    mine = grouped(refs[5 : 5 + count], counts)
    theirs = grouped(refs[5 + count : 5 + 2 * count], counts)
    gmid_ref, gatt_ref, ggain_ref = refs[5 + 2 * count : 8 + 2 * count]
    branch = refs[8 + 2 * count :]
    seq, slot = place[0], place[1]
    model = middle_ref.shape[1]
    half = model // 2
    width = model // seqs
    scale = rms_of(middle_ref[...])
    mean = 0.0
    for m in range(seqs):
        to = at(line_block(m, seq, seqs), width)
        here = slice(m * width, (m + 1) * width)
        grad = grad_ref[:, to]
        unit = middle_ref[:, to] * scale
        ggain_ref[:, to] = jnp.sum(grad * unit, axis=0, keepdims=True)
        scaled = grad * gain_ref[:, here]
        gmid_ref[:, to] = scaled
        mean = mean + jnp.sum(scaled * unit, axis=1, keepdims=True)
    mean = mean * (1.0 / model)
    gmid_ref[...] = cot_ref[...].astype(F32) + scale * (
        gmid_ref[...] - middle_ref[...] * (scale * mean)
    )
    out_cols = model // slots
    for i in range(slots):
        branch[i][...] = gmid_ref[:, at(slot ^ i, out_cols)].astype(BF)
    for pieces, start in ((mine, 0), (theirs, half)):
        row = start
        for c in range(chunks):
            rows = half // chunks
            total = dot_nt(branch[0][...], chunk_of(pieces[0], c, chunks))
            for i in range(1, slots):
                total = total + dot_nt(branch[i][...], chunk_of(pieces[i], c, chunks))
            gatt_ref[:, row : row + rows] = total.astype(BF)
            row += rows


def input_back_kernel(shape, *refs):
    counts, seqs = shape
    slots, count, chunks = len(counts), sum(counts), max(counts)
    place, gq_ref, gkv_ref, rows_ref, gmid_ref, gain_ref = refs[:6]
    mine = grouped(refs[6 : 6 + count], counts)
    theirs = grouped(refs[6 + count : 6 + 2 * count], counts)
    kv_mine, kv_theirs = refs[6 + 2 * count : 8 + 2 * count]
    out_ref, ggain_ref, scaled_ref = refs[8 + 2 * count :]
    seq = place[0]
    model = rows_ref.shape[1]
    half = model // 2
    width = model // seqs
    cols = model // slots
    rows_in = rows_ref[...].astype(F32)
    scale = rms_of(rows_in)
    mean = 0.0
    for pieces, kv_ref, start in ((mine, kv_mine, 0), (theirs, kv_theirs, half)):
        row = 0
        for c in range(chunks):
            rows = half // chunks
            total = dot_nt(gkv_ref[...], kv_ref[row : row + rows])
            for i in range(slots):
                total = total + dot_nt(
                    gq_ref[:, i * cols : (i + 1) * cols], chunk_of(pieces[i], c, chunks)
                )
            for b in range(rows // width):
                m = (start + row) // width + b
                here = slice(m * width, (m + 1) * width)
                to = at(line_block(m, seq, seqs), width)
                grad = total[:, b * width : (b + 1) * width]
                unit = rows_ref[:, to].astype(F32) * scale
                ggain_ref[:, to] = jnp.sum(grad * unit, axis=0, keepdims=True)
                scaled = grad * gain_ref[:, here]
                scaled_ref[:, to] = scaled
                mean = mean + jnp.sum(scaled * unit, axis=1, keepdims=True)
            row += rows
    mean = mean * (1.0 / model)
    out_ref[...] = (
        gmid_ref[...] + scale * (scaled_ref[...] - rows_in * (scale * mean))
    ).astype(BF)


def share_kernel(slots, seqs, place, gate_ref, up_ref, out_ref):
    piece = gate_ref.shape[1] // (slots * seqs)
    width = piece * seqs
    for s in range(slots):

        @pl.when(place[1] == s)
        def _():
            for n, ref in enumerate((gate_ref, up_ref)):
                parts = [
                    ref[:, (q * slots + s) * piece : (q * slots + s + 1) * piece]
                    for q in range(seqs)
                ]
                out_ref[:, n * width : (n + 1) * width] = jnp.concatenate(parts, axis=1)


def parts_product(left, right):
    total, block, row = None, 0, 0
    for ref in left:
        rows = ref.shape[0]
        part = dot_tn(ref[...], right[block][row : row + rows])
        total = part if total is None else total + part
        row += rows
        if row == right[block].shape[0]:
            block, row = block + 1, 0
    return total


def line_grads_kernel(count, slots, place, *refs):
    normed, attended = refs[:count], refs[count : 2 * count]
    traded, branch = refs[2 * count : 2 * count + slots], refs[2 * count + slots :][:slots]
    gain_ref, out_ref = refs[2 * count + 2 * slots], refs[-1]
    first = parts_product(normed, traded)
    second = parts_product(attended, branch)
    start = first.shape[1]
    end = start + second.shape[1]
    out_ref[:, :start] = first.astype(BF)
    out_ref[:, start:end] = second.astype(BF)
    out_ref[:, end:] = gain_ref[...]


def cut_store(total, outs):
    row = 0
    for ref in outs:
        rows = ref.shape[0]
        ref[...] = total[row : row + rows].astype(BF)
        row += rows


def gate_kernel(count, *refs):
    tokens = refs[:count]
    wgate_ref, wup_ref, all_ref, gate_ref, up_ref, hidden_ref = refs[count:]

    @pl.when(pl.program_id(0) == 0)
    def _():
        row = 0
        for ref in tokens:
            all_ref[row : row + ref.shape[0]] = ref[...]
            row += ref.shape[0]

    tile = wgate_ref.shape[1]
    both = dot(all_ref[...], jnp.concatenate([wgate_ref[...], wup_ref[...]], axis=1))
    gate, up = both[:, :tile], both[:, tile:]
    gate_ref[...] = gate.astype(BF)
    up_ref[...] = up.astype(BF)
    hidden_ref[...] = (gate * jax.nn.sigmoid(gate) * up).astype(BF)


def rows_kernel(transposed, late, left_ref, right_ref, *refs):
    right = right_ref[...]
    total = dot_nt(left_ref[...], right) if transposed else dot(left_ref[...], right)
    cut_store(total, refs[late:])


def unline_kernel(seqs, place, *refs):
    out_ref = refs[seqs]
    for m in range(seqs):
        rows = refs[m].shape[0]
        to = pl.ds(pl.multiple_of(line_block(m, place[0], seqs) * rows, rows), rows)
        out_ref[to] = refs[m][...]


def unshare_kernel(slots, seqs, place, part_ref, out_ref):
    piece = part_ref.shape[2] // seqs
    parts = []
    for q in range(seqs):
        for s in range(slots):
            part = part_ref[s, :, q * piece : (q + 1) * piece]
            parts.append(part.astype(F32))
    out_ref[...] = jnp.concatenate(parts, axis=1)


def tie(value, *after):
    return pl.pallas_call(
        lambda *refs: None,
        out_shape=jax.ShapeDtypeStruct(value.shape, value.dtype),
        in_specs=[ANY] * (1 + len(after)),
        out_specs=ANY,
        input_output_aliases={0: 0},
    )(value, *after)


def fence(values, after):
    count = len(values)
    return list(
        pl.pallas_call(
            lambda *refs: None,
            out_shape=[jax.ShapeDtypeStruct(value.shape, value.dtype) for value in values],
            in_specs=[ANY] * (count + len(after)),
            out_specs=[ANY] * count,
            input_output_aliases={k: k for k in range(count)},
        )(*values, *after)
    )


class Flow:
    def __init__(self):
        self.now = []

    def at(self, *values):
        self.now = list(values)

    def go(self, *values):
        kept = {id(value) for value in values}
        return fence(list(values), [value for value in self.now if id(value) not in kept])


def call(kernel, inputs, late, out_shape, in_specs=None, scratch=()):
    count = len(inputs)
    single = not isinstance(out_shape, (tuple, list))

    def run(*refs):
        kernel(*refs[:count], *refs[count + len(late) :])

    return pl.pallas_call(
        run,
        out_shape=out_shape,
        in_specs=[SMEM] + [VMEM] * (count - 1) + [ANY] * len(late),
        out_specs=VMEM if single else (VMEM,) * len(out_shape),
        scratch_shapes=list(scratch),
        compiler_params=BIG,
    )(*inputs, *late)


def shape_of(rows, cols, kind):
    return jax.ShapeDtypeStruct((rows, cols), kind)


def shards(
    rows_in,
    lengths,
    norm1_gain,
    w_query,
    w_key,
    w_value,
    w_out,
    norm2_gain,
    w_gate,
    w_up,
    w_down,
    rows_cot,
    kv_cot,
):
    slots = lax.axis_size("slot")
    seqs = lax.axis_size("seq")
    slot = lax.axis_index("slot")
    seq = lax.axis_index("seq")
    tok_count = rows_in.shape[1]
    model = rows_in.shape[2]
    head_width = w_key.shape[1]
    head_count = w_query.shape[1] // head_width
    hop_count = WINDOW // tok_count
    key_count = WINDOW + tok_count
    rows_dev = w_query.shape[0]
    cols_slot = w_query.shape[1] // slots
    out_slot = w_out.shape[1] // slots
    hidden_all = w_gate.shape[1]
    piece = hidden_all // (slots * seqs)
    hidden_slot = piece * seqs
    half = model // 2
    extra = 16
    place = jnp.stack([seq, slot, lengths[0]]).astype(jnp.int32)
    rows_own, cot_own = rows_in[0], rows_cot[0]

    first_row = seq * tok_count
    query_pos = first_row + jnp.arange(tok_count, dtype=jnp.int32)
    row_valid = (query_pos < lengths[0]).astype(F32)[:, None]
    flow = Flow()

    gains = jnp.stack([norm1_gain, norm2_gain], axis=0)
    pack = jnp.concatenate(
        [lax.dynamic_slice_in_dim(w_query, slot * cols_slot, cols_slot, 1), w_key, w_value], axis=1
    )
    gains = jnp.pad(gains, ((0, extra - 2), (cols_slot, pack.shape[1] - cols_slot - rows_dev)))
    pack = jnp.concatenate([pack, gains], axis=0)
    pack_near = line_near(pack)
    cot_near = gather_near(cot_own * row_valid.astype(BF))
    gu_share = call(
        functools.partial(share_kernel, slots, seqs),
        (place, w_gate, w_up),
        (),
        shape_of(rows_dev, 2 * hidden_slot, BF),
    )
    out_share = lax.dynamic_slice_in_dim(w_out, slot * out_slot, out_slot, 1)
    down_share = lax.dynamic_slice_in_dim(w_down, slot * piece, piece, 0)
    flow.at(*pack_near[1:], *cot_near[1:], gu_share)

    *pack_near[1:], out_share = flow.go(*pack_near[1:], out_share)
    *cot_near[1:], down_share = flow.go(*cot_near[1:], down_share)
    pack_far = line_far(pack_near)
    out_near = line_near(out_share)
    cot_far = gather_far(cot_near)
    flow.at(*pack_far, *out_near[1:], *cot_far)

    pack_line = line_all(pack_near, pack_far)
    query_line = jnp.concatenate([block[:rows_dev, :cols_slot] for block in pack_line], axis=0)
    kv_gain = jnp.concatenate([block[:, cols_slot:] for block in pack_line], axis=0)
    query_line, kv_gain, out_near[-1], gu_share = flow.go(
        query_line, kv_gain, out_near[-1], gu_share
    )
    gu_w = lax.all_gather(gu_share, "seq", axis=0, tiled=True)
    down_w = lax.all_gather(down_share, "seq", axis=0, tiled=True)
    query_near = gather_near(query_line)
    query_other = [swap(query_line, "seq", 1)]
    kv_other = swap(kv_gain, "seq", 1)
    out_far = line_far(out_near)
    flow.at(*query_near[1:], query_other[0], kv_other, *out_far)

    query_near[1:] = flow.go(*query_near[1:])
    query_far = gather_far(query_near)
    query_other += [swap(part, "seq", 1) for part in query_near[1:]]
    flow.at(*query_far, *query_other[1:])

    *query_far, out_line = flow.go(
        *query_far, jnp.concatenate(line_all(out_near, out_far), axis=0)
    )
    query_other += [swap(part, "seq", 1) for part in query_far]
    query_w = query_near + query_far + query_other
    out_near = gather_near(out_line)
    flow.at(*query_w[len(query_near) :])
    kv_w, gain_line = [], []
    for part in (kv_gain, kv_other):
        part = part.reshape(seqs // 2, rows_dev + extra, -1)
        kv_w.append(part[:, :rows_dev].reshape(half, -1))
        gain_line.append(part[:, rows_dev : rows_dev + 2, :rows_dev])
    gain_line = jnp.concatenate(gain_line, axis=0).transpose(1, 0, 2).reshape(2, 1, model)
    gain_line = gain_line.astype(F32)
    gain_one, gain_two = gain_line[0], gain_line[1]
    shape = ((1, 1, 1, 2) if slots == 4 else (1,) * slots, seqs)

    cosine, sine = rope_tables(query_pos, head_width)
    cosine = jnp.concatenate([cosine, cosine], axis=1)
    sine = jnp.concatenate([-sine, sine], axis=1)
    normed, queries, shared = call(
        functools.partial(project_kernel, shape),
        (place, rows_own, gain_one, row_valid, cosine, sine, *query_w, *kv_w),
        (),
        (
            shape_of(tok_count, model, BF),
            shape_of(tok_count, head_count * head_width, BF),
            shape_of(tok_count, 2 * head_width, BF),
        ),
        scratch=[pltpu.VMEM((tok_count, model), BF)],
    )
    out_other = [swap(out_near[0], "seq", 1)]
    table = [shifted(shared, "seq", hop) for hop in range(hop_count, 0, -1)] + [shared]
    flow.at(*table[:-1], out_other[0], *out_near[1:])

    slot_heads = head_count // slots
    block_heads = rows_dev // head_width

    def own_col(p, place):
        return (0, p)

    def line_col(p, place):
        head = (place[1] ^ (p // slot_heads)) * slot_heads + p % slot_heads
        spot = line_place(head // block_heads, place[0], seqs)
        return (0, spot * block_heads + head % block_heads)

    def fixed(p, place):
        return (0, 0)

    head_own = pl.BlockSpec((tok_count, head_width), own_col)
    head_line = pl.BlockSpec((tok_count, head_width), line_col)
    table_spec = [pl.BlockSpec((tok_count, 2 * head_width), fixed)] * (hop_count + 1)
    angle_spec = [pl.BlockSpec((tok_count, head_width), fixed)] * 2
    bias_scratch = [pltpu.VMEM((tok_count, key_count), F32)]
    out_near[1:] = flow.go(*out_near[1:])
    out_far = gather_far(out_near)
    out_other += [swap(part, "seq", 1) for part in out_near[1:]]
    late = out_near[1:]
    attended = pl.pallas_call(
        functools.partial(attend_kernel, hop_count, len(late)),
        out_shape=shape_of(tok_count, head_count * head_width, BF),
        grid_spec=pltpu.PrefetchScalarGridSpec(
            num_scalar_prefetch=1,
            grid=(head_count,),
            in_specs=[head_own] + table_spec + [ANY] * len(late),
            out_specs=head_line,
            scratch_shapes=bias_scratch,
        ),
        compiler_params=BIG,
    )(place, queries, *table, *late)
    flow.at(*out_far, *out_other[1:], attended)
    if out_far:
        out_far = flow.go(*out_far)
    out_other += [swap(part, "seq", 1) for part in out_far]
    out_w = out_near + out_far + out_other
    middle, normed_two, attended = call(
        functools.partial(out_kernel, shape),
        (place, attended, rows_own, gain_two, *out_w),
        (),
        (
            shape_of(tok_count, model, F32),
            shape_of(tok_count, model, BF),
            shape_of(tok_count, model, BF),
        ),
    )

    normed_two_near = gather_near(normed_two)
    cot_rows = jnp.concatenate(cot_near + cot_far, axis=0)
    flow.at(*normed_two_near[1:], cot_rows)
    normed_two_near[1:] = flow.go(*normed_two_near[1:])
    normed_two_parts = normed_two_near + gather_far(normed_two_near)
    flow.at(*normed_two_parts[len(normed_two_near) - 1 :])

    normed_near = gather_near(tie(normed, *normed_two_parts[slots - 1 :]))
    tokens = slots * tok_count
    tile = 128
    if hidden_slot % tile == 0:
        steps = hidden_slot // tile
        part_spec = pl.BlockSpec((tokens, tile), lambda j: (0, j))
        normed_two_all, gate_out, up_out, hidden = pl.pallas_call(
            functools.partial(gate_kernel, len(normed_two_parts)),
            out_shape=(shape_of(tokens, model, BF),) + (shape_of(tokens, hidden_slot, BF),) * 3,
            grid=(steps,),
            in_specs=[pl.BlockSpec(part.shape, lambda j: (0, 0)) for part in normed_two_parts]
            + [
                pl.BlockSpec((model, tile), lambda j: (0, j)),
                pl.BlockSpec((model, tile), lambda j: (0, steps + j)),
            ],
            out_specs=(pl.BlockSpec((tokens, model), lambda j: (0, 0)),) + (part_spec,) * 3,
            compiler_params=BIG,
        )(*normed_two_parts, gu_w, gu_w)
        gate_out, up_out = gate_out.astype(F32), up_out.astype(F32)
    else:
        normed_two_all = jnp.concatenate(normed_two_parts, axis=0)
        gu_out = dot(normed_two_all, gu_w)
        gate_out, up_out = gu_out[:, :hidden_slot], gu_out[:, hidden_slot:]
        hidden = (gate_out * jax.nn.sigmoid(gate_out) * up_out).astype(BF)
    sig_gate = jax.nn.sigmoid(gate_out)
    cot_rows = tie(cot_rows, *normed_near[1:], hidden)
    grad_down = dot_tn(hidden, cot_rows).astype(BF)
    own_down = lax.psum_scatter(grad_down, "seq", scatter_dimension=0, tiled=True)
    *normed_near[1:], attended = fence([*normed_near[1:], attended], [cot_rows])
    normed_all = normed_near + gather_far(normed_near)
    attended_near = gather_near(attended)

    grad_hidden = dot_nt(cot_rows, down_w)
    grad_gate = grad_hidden * up_out * sig_gate * (1.0 + gate_out * (1.0 - sig_gate))
    grad_up = grad_hidden * gate_out * sig_gate
    grad_gu = jnp.concatenate([grad_gate.astype(BF), grad_up.astype(BF)], axis=1)
    grad_gu = tie(grad_gu, *normed_all[slots - 1 :], *attended_near[1:])
    half_tok = tok_count // 2
    cut_rows = [tok_count] + [half_tok] * 6 if slots == 4 else [tok_count] * slots

    def cut_product(left, right, transposed, late):
        width = 256
        depth = left.shape[1]
        right_spec = (
            pl.BlockSpec((width, depth), lambda j: (j, 0))
            if transposed
            else pl.BlockSpec((depth, width), lambda j: (0, j))
        )
        return list(
            pl.pallas_call(
                functools.partial(rows_kernel, transposed, len(late)),
                out_shape=[shape_of(rows, model, BF) for rows in cut_rows],
                grid=(model // width,),
                in_specs=[pl.BlockSpec(left.shape, lambda j: (0, 0)), right_spec]
                + [ANY] * len(late),
                out_specs=[pl.BlockSpec((rows, width), lambda j: (0, j)) for rows in cut_rows],
                compiler_params=BIG,
            )(left, right, *late)
        )

    attended_near[1:] = fence(attended_near[1:], [grad_gu])
    attended_all = attended_near + gather_far(attended_near)
    grad_parts = cut_product(grad_gu, gu_w, True, ())
    if slots == 4:
        grad_parts[5:] = fence(
            grad_parts[5:], attended_all[slots - 1 :]
        )
    passed = scatter_pass(grad_parts)
    down_parts = cut_product(tie(hidden, grad_parts[0]), down_w, False, ())
    if slots == 4:
        *passed, grad_parts[2], grad_parts[3], grad_gu = fence(
            [*passed, grad_parts[2], grad_parts[3], grad_gu], [down_parts[0]]
        )
    near = scatter_near(grad_parts)
    far = scatter_far(grad_parts, passed)
    grad_gate_w = dot_tn(normed_two_all, grad_gu[:, :hidden_slot]).astype(BF)
    grad_normed_two = scatter_total(grad_parts, near, far)
    grad_gate_w, own_down, down_parts[-1] = fence(
        [grad_gate_w, own_down, down_parts[-1]], [grad_normed_two]
    )
    own_gate = lax.psum_scatter(grad_gate_w, "seq", scatter_dimension=0, tiled=True)
    down_passed = scatter_pass(
        [*down_parts[:-2], tie(down_parts[-2], down_parts[-1]), down_parts[-1]]
    )

    grad_middle, grad_attended, grad_gain_two, *branch = call(
        functools.partial(mid_back_kernel, shape),
        (place, grad_normed_two, middle, cot_own, gain_two, *out_w),
        (grad_gate_w,),
        (
            shape_of(tok_count, model, F32),
            shape_of(tok_count, head_count * head_width, BF),
            shape_of(1, model, F32),
        )
        + (shape_of(tok_count, out_slot, BF),) * slots,
    )
    branch_all = trade_slot(branch)

    grad_query, grad_table = pl.pallas_call(
        functools.partial(attend_back_kernel, hop_count, 0),
        out_shape=(
            shape_of(tok_count, head_count * head_width, BF),
            shape_of(key_count, 2 * head_width, F32),
        ),
        grid_spec=pltpu.PrefetchScalarGridSpec(
            num_scalar_prefetch=1,
            grid=(head_count,),
            in_specs=[head_own, head_line] + table_spec + angle_spec,
            out_specs=(head_own, pl.BlockSpec((key_count, 2 * head_width), fixed)),
            scratch_shapes=bias_scratch,
        ),
        compiler_params=BIG,
    )(place, queries, grad_attended, *table, cosine, sine)
    grad_table, down_parts[2], down_parts[3], *down_passed = fence(
        [grad_table, down_parts[2], down_parts[3], *down_passed],
        branch_all[1:],
    )
    down_near = scatter_near(down_parts)
    grad_up_w = dot_tn(normed_two_all, tie(grad_gu, grad_table)[:, hidden_slot:]).astype(BF)
    own_grad = grad_table[WINDOW:] + kv_cot[0].astype(F32)
    for hop in range(1, hop_count + 1):
        lower = (hop_count - hop) * tok_count
        own_grad = own_grad + shifted(
            grad_table[lower : lower + tok_count].astype(BF), "seq", -hop
        ).astype(F32)
    own_grad = own_grad * row_valid
    grad_key = own_grad[:, :head_width]
    grad_key = grad_key * cosine - jnp.roll(grad_key, head_width // 2, axis=1) * sine
    grad_kv = jnp.concatenate([grad_key, own_grad[:, head_width:]], axis=1).astype(BF)
    grad_kv, own_down = fence([grad_kv, own_down], [grad_up_w])

    traded = [
        jnp.concatenate([grad_query[:, j * cols_slot : (j + 1) * cols_slot], grad_kv], axis=1)
        for j in range(slots)
    ]
    late = traded
    traded = trade_slot(traded)
    grad_inputs, grad_gain_one = call(
        functools.partial(input_back_kernel, shape),
        (place, grad_query, grad_kv, rows_own, grad_middle, gain_one, *query_w, *kv_w),
        late,
        (shape_of(tok_count, model, BF), shape_of(1, model, F32)),
        scratch=[pltpu.VMEM((tok_count, model), F32)],
    )
    gain_grads = jnp.concatenate([grad_gain_one, grad_gain_two], axis=0).astype(BF)
    gain_grads = jnp.pad(gain_grads.T, ((0, 0), (0, head_width - 2)))
    gain_grads, down_parts[1], own_down = fence(
        [gain_grads, down_parts[1], own_down], [grad_inputs, *traded[1:], *down_near]
    )
    own_down_near = gather_near(own_down)
    width_all = traded[0].shape[1] + branch_all[0].shape[1] + head_width
    places = seqs // 2

    def line_grads(start, late):
        def columns(m, place):
            return (0, line_block_at(start + m, place[0], seqs))

        def rows(m, place):
            return (line_block_at(start + m, place[0], seqs), 0)

        return pl.pallas_call(
            functools.partial(line_grads_kernel, len(normed_all), slots),
            out_shape=shape_of(half, width_all, BF),
            grid_spec=pltpu.PrefetchScalarGridSpec(
                num_scalar_prefetch=1,
                grid=(places,),
                in_specs=[
                    pl.BlockSpec((part.shape[0], rows_dev), columns)
                    for part in normed_all + attended_all
                ]
                + [pl.BlockSpec(part.shape, fixed) for part in traded + branch_all]
                + [pl.BlockSpec((rows_dev, head_width), rows)]
                + [ANY] * len(late),
                out_specs=pl.BlockSpec((rows_dev, width_all), lambda m, place: (m, 0)),
            ),
            compiler_params=BIG,
        )(place, *normed_all, *attended_all, *traded, *branch_all, gain_grads, *late)

    theirs = line_grads(places, ())
    down_far = scatter_far(down_parts, down_passed)
    passed = swap(theirs, "seq", 1)
    mine = line_grads(0, (theirs,))
    grad_up_w = tie(grad_up_w, own_gate, grad_inputs)
    own_up = lax.psum_scatter(grad_up_w, "seq", scatter_dimension=0, tiled=True)
    passed = tie(passed, mine)
    own_down_near[1:] = fence(own_down_near[1:], [passed])
    own_down_all = own_down_near + gather_far(own_down_near)
    line = line_sums(mine, passed)
    first = line_first(line)
    down_total = scatter_total(down_parts, down_near, down_far)
    result = (middle + down_total * row_valid).astype(BF)
    second = line_second(line, first)
    own_gate = tie(own_gate.astype(BF), own_up, result)
    gate_all = lax.all_gather(own_gate, "slot", axis=0)
    up_all = lax.all_gather(own_up.astype(BF), "slot", axis=0)
    own = line_total(line, first, second)
    kv_end = cols_slot + 2 * head_width
    shared_out = jnp.concatenate([own[:, :cols_slot], own[:, kv_end:]], axis=1).astype(BF)
    shared_near = gather_near(shared_out)
    all_own = jnp.concatenate(shared_near + gather_far(shared_near), axis=0)
    all_own = all_own.reshape(slots, rows_dev, -1)
    all_own = jnp.stack(
        [lax.dynamic_index_in_dim(all_own, slot ^ j, 0, keepdims=False) for j in range(slots)]
    )

    def by_slot(parts):
        parts = jnp.concatenate(parts, axis=0).reshape(slots, -1, parts[0].shape[1])
        return jnp.stack(
            [lax.dynamic_index_in_dim(parts, slot ^ j, 0, keepdims=False) for j in range(slots)]
        )

    def slot_columns(parts):
        return parts.transpose(1, 0, 2).reshape(rows_dev, -1).astype(F32)

    query_grad = slot_columns(all_own[:, :, :cols_slot])
    out_grad_w = slot_columns(all_own[:, :, cols_slot : cols_slot + out_slot])
    gain_total = jnp.sum(all_own[:, :, cols_slot + out_slot :][:, :, :2].astype(F32), axis=0)
    down_grad = by_slot(own_down_all).reshape(slots * piece, model).astype(F32)
    row_tile = 32

    def whole_rows(parts):
        return pl.pallas_call(
            functools.partial(unshare_kernel, slots, seqs),
            out_shape=shape_of(rows_dev, hidden_all, F32),
            grid_spec=pltpu.PrefetchScalarGridSpec(
                num_scalar_prefetch=1,
                grid=(rows_dev // row_tile,),
                in_specs=[
                    pl.BlockSpec((slots, row_tile, hidden_slot), lambda r, place: (0, r, 0))
                ],
                out_specs=pl.BlockSpec((row_tile, hidden_all), lambda r, place: (r, 0)),
            ),
            compiler_params=BIG,
        )(place, parts)

    gate_grad = whole_rows(gate_all)
    up_grad = whole_rows(up_all)
    return (
        result[None],
        shared[None],
        grad_inputs[None],
        gain_total[:, 0],
        query_grad,
        own[:, cols_slot : cols_slot + head_width].astype(F32),
        own[:, cols_slot + head_width : kv_end].astype(F32),
        out_grad_w,
        gain_total[:, 1],
        gate_grad,
        up_grad,
        down_grad,
    )


def solution(mesh):
    placed = (
        P("slot", "seq", None),
        P("slot"),
        P("seq"),
        P("seq", None),
        P("seq", None),
        P("seq", None),
        P("seq", None),
        P("seq"),
        P("seq", None),
        P("seq", None),
        P("seq", None),
        P("slot", "seq", None),
        P("slot", "seq", None),
    )
    return jax.shard_map(
        shards,
        mesh=mesh,
        in_specs=placed,
        out_specs=(
            P("slot", "seq", None),
            P("slot", "seq", None),
            P("slot", "seq", None),
            P("seq"),
            P("seq", None),
            P("seq", None),
            P("seq", None),
            P("seq", None),
            P("seq"),
            P("seq", None),
            P("seq", None),
            P("seq", None),
        ),
        check_vma=False,
    )
```

time: 2060 us -> 660 us (0.32)
  waiting for transfers between devices: 1670 us -> 225 us
  Pallas kernels: 0 us -> 158 us
  matrix products: 187 us -> 43.7 us
  blocking collectives: 79.4 us -> 0 us
  starting transfers between devices: 13.8 us -> 86.3 us
  local copies, waits for them, and re-layouts: 46 us -> 81.1 us
    reduce_scatter x7 -> x3, waiting for transfers between devices: 850 us -> 14.9 us  [the longest x1 14.9 us: shards(): own_up = lax.psum_scatter(grad_up_w, 'seq', scatter_dimension=0, tiled=True)]
    all_gather x5 -> x4, waiting for transfers between devices: 643 us -> 0.01 us  [the longest x1 0.01 us: shards(): gu_w = lax.all_gather(gu_share, 'seq', axis=0, tiled=True)]
    ppermute x0 -> x71, waiting for transfers between devices: none -> 193 us  [swap(): lax.ppermute(block, axis, [(i, i ^ mask) for i in range(lax.axis_size(axi...]
    psum x1 -> x0, waiting for transfers between devices: 169 us -> none  [shards(): lax.psum(part_b.astype(jnp.bfloat16), 'slot').astype(jnp.float32)]
    pallas_call x0 -> x40, Pallas kernels: none -> 158 us  [the longest x5 40 us: call(): pl.pallas_call(run, out_shape=out_shape, in_specs=[SMEM] + [VMEM] * (coun...]
    dot_general x27 -> x4, matrix products: 187 us -> 43.7 us  [the longest x3 32.8 us: dot_tn(): lax.dot_general(left, right, (((0,), (0,)), ((), ())), preferred_element_...]
    ppermute x0 -> x71, starting transfers between devices: none -> 75.8 us  [swap(): lax.ppermute(block, axis, [(i, i ^ mask) for i in range(lax.axis_size(axi...]
    all_gather x4 -> x0, blocking collectives: 56.7 us -> none  [the longest x1 19.5 us: shards(): lax.all_gather(w_key, 'seq', axis=0, tiled=True)]
  transfers between devices with their start and end apart: 17 -> 82, of which waited for: 13 -> 35; matrix products, arithmetic and copies ran while one was open for 8% -> 20% of each run, Pallas kernels for 0% -> 23%
where the time goes in v2:
time: 660 us; the launch traced here: 650 us
  waiting for transfers between devices  225 us (34%)
  Pallas kernels  158 us (24%)
  starting transfers between devices  86.3 us (13%)
  local copies, waits for them, and re-layouts  81.1 us (12%)
  matrix products  43.7 us (7%)
  other arithmetic  38.9 us (6%)
  between operations  16.6 us (3%)
    ppermute x71, waiting for transfers between devices, swap(): lax.ppermute(block, axis, [(i, i ^ mask) for i in range(lax.axis_size(axi...  193 us
    ppermute x71, starting transfers between devices, swap(): lax.ppermute(block, axis, [(i, i ^ mask) for i in range(lax.axis_size(axi...  75.8 us
    unnamed x200, local copies, waits for them, and re-layouts  45.9 us
    pallas_call x5, Pallas kernels, call(): pl.pallas_call(run, out_shape=out_shape, in_specs=[SMEM] + [VMEM] * (coun...  40 us
    dot_general x3, matrix products, dot_tn(): lax.dot_general(left, right, (((0,), (0,)), ((), ())), preferred_element_...  32.8 us
    pallas_call x2, Pallas kernels, cut_product(): pl.pallas_call(functools.partial(rows_kernel, transposed, len(late)), out...  29.3 us
    pallas_call x1, Pallas kernels, shards(): pl.pallas_call(functools.partial(attend_back_kernel, hop_count, 0), out_s...  20.8 us
    pallas_call x1, Pallas kernels, shards(): pl.pallas_call(functools.partial(gate_kernel, len(normed_two_parts)), out...  19.2 us
  transfers between devices with their start and end apart: 82, of which 35 were waited for; matrix products, arithmetic and copies ran while one was open for 20% of the time, Pallas kernels for 23%

profile of v2, /device:TPU:10, one launch (start us, length us, event | category | flops | bytes accessed | tf_op | source)
XLA Modules:
  0.0 649.7 jit_solution(13485487389828776245)
XLA Ops:
  8.1 2.8 constant_dynamic-update-slice_fusion.4
  17.1 2.5 collective-permute-start
  20.2 4.5 shard_map.220.refs_5_.refs_3_
  27.3 8.8 %collective-permute-done.3.refs_4_ = bf16[256,2048]{1,0:T(8,128)(2,1)} collective-permute-done((bf16[256,2048]{1,0:T(8,128)(2,1)}, bf16[256,2048]{1,0:T(8,128)(2,1)}, u32[]{:S(2)}, u32[]{:S(2)}) %collective-permute-start.3) | collective-permute-done | bytes 1048608 | tf_op jit(solution)/shard_map/ppermute | solution.py:21
  36.2 2.3 copy.103.refs_1_
  38.5 2.3 copy.102.refs_0_
  48.8 2.5 collective-permute-start.5
  51.3 3.1 collective-permute-done.4.refs_4_
  56.4 3.7 collective-permute-done.6.refs_5_
  64.8 6.0 collective-permute-start.13
  70.8 8.1 %collective-permute-done.13.refs_4_ = bf16[256,512]{1,0:T(8,128)(2,1)S(1)} collective-permute-done((bf16[256,512]{1,0:T(8,128)(2,1)}, bf16[256,512]{1,0:T(8,128)(2,1)S(1)}, u32[]{:S(2)}, u32[]{:S(2)}) %collective-permute-start.13) | collective-permute-done | bytes 262176 | tf_op jit(solution)/shard_map/ppermute | solution.py:21
  79.0 9.5 %collective-permute-done.11.refs_1_ = bf16[1024,512]{1,0:T(8,128)(2,1)S(1)} collective-permute-done((bf16[1024,512]{1,0:T(8,128)(2,1)}, bf16[1024,512]{1,0:T(8,128)(2,1)S(1)}, u32[]{:S(2)}, u32[]{:S(2)}) %collective-permute-start.11) | collective-permute-done | bytes 1048608 | tf_op jit(solution)/shard_map/ppermute | solution.py:21
  95.2 2.1 pad_maximum_fusion.6.refs_2_
  97.3 10.0 %collective-permute-done.15.refs_1_ = bf16[512,512]{1,0:T(8,128)(2,1)S(1)} collective-permute-done((bf16[512,512]{1,0:T(8,128)(2,1)S(1)}, bf16[512,512]{1,0:T(8,128)(2,1)S(1)}, u32[]{:S(2)}, u32[]{:S(2)}) %collective-permute-start.15) | collective-permute-done | bytes 524320 | tf_op jit(solution)/shard_map/ppermute | solution.py:21
  120.9 8.4 %shard_map.226 = (bf16[256,2048]{1,0:T(8,128)(2,1)}, bf16[256,2048]{1,0:T(8,128)(2,1)}, bf16[256,256]{1,0:T(8,128)(2,1)}) custom-call(s32[3]{0:T(128)} %pad_add_fusion.refs_0_.place, bf16[256,2048]{1,0:T(8,128)(2,1)} %bitcast.46, f32[1,2048]{1,0:T(1,128)} %bitcast.68, f32[256,1]{1,0:T(8,128)} %fusion.15.refs_3_, ...), custom_call_target="tpu_custom_call" | custom-call | tf_op jit(solution)/shard_map/pallas_call | solution.py:554
  131.2 3.9 collective-permute-start.20
  135.1 8.0 %collective-permute-done.21.refs_3_.refs_1_ = bf16[256,256]{1,0:T(8,128)(2,1)S(1)} collective-permute-done((bf16[256,256]{1,0:T(8,128)(2,1)}, bf16[256,256]{1,0:T(8,128)(2,1)S(1)}, u32[]{:S(2)}, u32[]{:S(2)}) %collective-permute-start.21) | collective-permute-done | bytes 131104 | tf_op jit(solution)/shard_map/ppermute | solution.py:95
  143.1 2.6 collective-permute-done.20.refs_2_.refs_0_
  148.7 3.4 collective-permute-start.27
  156.3 15.6 %shard_map.228.refs_4_.refs_1_ = bf16[256,2048]{1,0:T(8,128)(2,1)} custom-call(s32[3]{0:T(128)} %pad_add_fusion.refs_0_.place, bf16[256,2048]{1,0:T(8,128)(2,1)} %get-tuple-element.107.query_ref, bf16[256,256]{1,0:T(8,128)(2,1)} %copy-done.77, bf16[256,256]{1,0:T(8,128)(2,1)} %copy-done.76, bf16[256,256]{1,0:T(8,128)(2,1)} %get-tuple-element.108.refs_2_, ...), custom_call_target="tpu_custom_call" | custom-call | tf_op jit(solution)/shard_map/pallas_call | solution.py:711
  178.0 8.5 %shard_map.230 = (f32[256,2048]{1,0:T(8,128)}, bf16[256,2048]{1,0:T(8,128)(2,1)}, bf16[256,2048]{1,0:T(8,128)(2,1)}) custom-call(s32[3]{0:T(128)} %pad_add_fusion.refs_0_.place, bf16[256,2048]{1,0:T(8,128)(2,1)} %shard_map.228.refs_4_.refs_1_, bf16[256,2048]{1,0:T(8,128)(2,1)} %bitcast.47, f32[1,2048]{1,0:T(1,128)} %bitcast.70, ...), custom_call_target="tpu_custom_call" | custom-call | tf_op jit(solution)/shard_map/pallas_call | solution.py:554
  192.4 19.6 %collective-permute-done.32.refs_1_ = bf16[256,2048]{1,0:T(8,128)(2,1)} collective-permute-done((bf16[256,2048]{1,0:T(8,128)(2,1)}, bf16[256,2048]{1,0:T(8,128)(2,1)}, u32[]{:S(2)}, u32[]{:S(2)}) %collective-permute-start.32) | collective-permute-done | bytes 1048608 | tf_op jit(solution)/shard_map/ppermute | solution.py:21
  216.8 11.7 %collective-permute-done.34.refs_4_.refs_2_ = bf16[128,2048]{1,0:T(8,128)(2,1)S(1)} collective-permute-done((bf16[128,2048]{1,0:T(8,128)(2,1)S(1)}, bf16[128,2048]{1,0:T(8,128)(2,1)S(1)}, u32[]{:S(2)}, u32[]{:S(2)}) %collective-permute-start.34) | collective-permute-done | bytes 524320 | tf_op jit(solution)/shard_map/ppermute | solution.py:21
  231.6 19.2 %shard_map.232 = (bf16[1024,2048]{1,0:T(8,128)(2,1)}, bf16[1024,1408]{1,0:T(8,128)(2,1)}, bf16[1024,1408]{1,0:T(8,128)(2,1)}, bf16[1024,1408]{1,0:T(8,128)(2,1)}) custom-call(bf16[256,2048]{1,0:T(8,128)(2,1)} %get-tuple-element.115.refs_0_, bf16[256,2048]{1,0:T(8,128)(2,1)} %get-tuple-element.116.refs_1_, bf16[256,2048]{1,0:T(8,128)(2,1)} %get-tuple-element.117.refs_2_, ...), custom_call_target="tpu_custom_call" | custom-call | tf_op jit(solution)/shard_map/pallas_call | solution.py:752
  250.8 2.1 collective-permute-done.36.refs_2_.refs_1_
  256.7 10.7 %convolution_convert_fusion.1 = bf16[1408,2048]{1,0:T(8,128)(2,1)} fusion(bf16[1024,1408]{1,0:T(8,128)(2,1)S(1)} %copy-done.3, bf16[1024,2048]{1,0:T(8,128)(2,1)} %shard_map.234.refs_3_), kind=kOutput, calls=%fused_computation.4 | convolution fusion | flops 5908463616 | bytes 12845056 | tf_op jit(solution)/shard_map/dot_general | solution.py:115
  275.3 10.9 %fusion.31 = f32[1024,1408]{1,0:T(8,128)S(1)} fusion(bf16[1024,2048]{1,0:T(8,128)(2,1)} %shard_map.234.refs_3_, bf16[1408,2048]{1,0:T(8,128)(2,1)} %all-gather.9.cloned.1.call-done.right_ref), kind=kOutput, calls=%fused_computation.113 | convolution fusion | flops 5905580032 | bytes 15728640 | tf_op jit(solution)/shard_map/dot_general | solution.py:111
  286.3 2.9 fusion.5
  289.2 2.9 pad_maximum_fusion.refs_0_
  292.1 9.9 %collective-permute-done.38.refs_2_.refs_4_ = bf16[128,2048]{1,0:T(8,128)(2,1)S(1)} collective-permute-done((bf16[128,2048]{1,0:T(8,128)(2,1)}, bf16[128,2048]{1,0:T(8,128)(2,1)S(1)}, u32[]{:S(2)}, u32[]{:S(2)}) %collective-permute-start.38) | collective-permute-done | bytes 524320 | tf_op jit(solution)/shard_map/ppermute | solution.py:21
  308.7 17.9 %shard_map.237 = (bf16[256,2048]{1,0:T(8,128)(2,1)}, bf16[128,2048]{1,0:T(8,128)(2,1)}, bf16[128,2048]{1,0:T(8,128)(2,1)}, bf16[128,2048]{1,0:T(8,128)(2,1)}, bf...) custom-call(bf16[1024,2816]{1,0:T(8,128)(2,1)} %shard_map.236.left_ref.refs_2_.refs_4_, ...), custom_call_target="tpu_custom_call" | custom-call | tf_op jit(solution)/shard_map/pallas_call | solution.py:795
  329.6 11.4 %shard_map.239 = (bf16[256,2048]{1,0:T(8,128)(2,1)}, bf16[128,2048]{1,0:T(8,128)(2,1)}, bf16[128,2048]{1,0:T(8,128)(2,1)}, bf16[128,2048]{1,0:T(8,128)(2,1)}, bf...) custom-call(bf16[1024,1408]{1,0:T(8,128)(2,1)} %shard_map.238.left_ref, ...), custom_call_target="tpu_custom_call" | custom-call | tf_op jit(solution)/shard_map/pallas_call | solution.py:795
  349.7 11.1 %convolution_convert_fusion.2.refs_0_ = bf16[2048,1408]{1,0:T(8,128)(2,1)} fusion(bf16[1024,2048]{1,0:T(8,128)(2,1)} %get-tuple-element.144, bf16[1024,2816]{1,0:T(8,128)(2,1)} %get-tuple-element.145.refs_0_), kind=kOutput, calls=%fused_computation.5 | convolution fusion | flops 5908463616 | bytes 12845056 | tf_op jit(solution)/shard_map/dot_general | solution.py:115
  360.8 4.0 collective-permute-done.46
  364.7 2.8 collective-permute-done.48
  371.8 9.3 %shard_map.244 = (f32[256,2048]{1,0:T(8,128)}, bf16[256,2048]{1,0:T(8,128)(2,1)}, f32[1,2048]{1,0:T(1,128)}, bf16[256,512]{1,0:T(8,128)(2,1)}, bf16[256,512]{1,0...) custom-call(s32[3]{0:T(128)} %pad_add_fusion.refs_0_.place, ...), custom_call_target="tpu_custom_call" | custom-call | tf_op jit(solution)/shard_map/pallas_call | solution.py:554
  384.6 20.8 %shard_map.245 = (bf16[256,2048]{1,0:T(8,128)(2,1)}, f32[768,256]{1,0:T(8,128)}) custom-call(s32[3]{0:T(128)} %pad_add_fusion.refs_0_.place, bf16[256,2048]{1,0:T(8,128)(2,1)} %get-tuple-element.107.query_ref, bf16[256,2048]{1,0:T(8,128)(2,1)} %get-tuple-element.148.grad_ref, bf16[256,256]{1,0:T(8,128)(2,1)} %copy-done.77, bf16[256,256]{1,0:T(8,128)(2,1)} %copy-done.76, ...), custom_call_target="tpu_custom_call" | custom-call | tf_op jit(solution)/shard_map/pallas_call | solution.py:844
  411.9 2.1 collective-permute-start.55
  413.9 11.0 %convolution_convert_fusion.refs_2_.refs_0_ = bf16[2048,1408]{1,0:T(8,128)(2,1)} fusion(bf16[1024,2048]{1,0:T(8,128)(2,1)} %get-tuple-element.144, bf16[1024,2816]{1,0:T(8,128)(2,1)} %shard_map.248), kind=kOutput, calls=%fused_computation.3 | convolution fusion | flops 5908463616 | bytes 12845056 | tf_op jit(solution)/shard_map/dot_general | solution.py:115
  425.0 5.0 collective-permute-done.55
  432.0 2.1 pad_maximum_fusion.7
  434.1 9.4 %shard_map.250 = (bf16[256,2048]{1,0:T(8,128)(2,1)}, f32[1,2048]{1,0:T(1,128)}) custom-call(s32[3]{0:T(128)} %pad_add_fusion.refs_0_.place, bf16[256,2048]{1,0:T(8,128)(2,1)} %get-tuple-element.149.refs_1_, bf16[256,256]{1,0:T(8,128)(2,1)} %get-tuple-element.160.refs_2_, bf16[256,2048]{1,0:T(8,128)(2,1)} %bitcast.48, ...), custom_call_target="tpu_custom_call" | custom-call | tf_op jit(solution)/shard_map/pallas_call | solution.py:554
  451.5 16.3 %collective-permute-done.58.refs_6_.refs_13_ = bf16[256,768]{1,0:T(8,128)(2,1)S(1)} collective-permute-done((bf16[256,768]{1,0:T(8,128)(2,1)}, bf16[256,768]{1,0:T(8,128)(2,1)S(1)}, u32[]{:S(2)}, u32[]{:S(2)}) %collective-permute-start.58) | collective-permute-done | bytes 393248 | tf_op jit(solution)/shard_map/ppermute | solution.py:21
  469.3 5.4 collective-permute-done.56.refs_4_.refs_11_
  474.7 2.3 collective-permute-done.57.refs_5_.refs_12_
  480.6 9.2 %shard_map.252.refs_19_ = bf16[1024,1408]{1,0:T(8,128)(2,1)} custom-call(s32[3]{0:T(128)} %pad_add_fusion.refs_0_.place, bf16[256,2048]{1,0:T(8,128)(2,1)} %shard_map.233.refs_0_, bf16[256,2048]{1,0:T(8,128)(2,1)} %get-tuple-element.125.refs_1_, bf16[256,2048]{1,0:T(8,128)(2,1)} %get-tuple-element.126.refs_2_, bf16[128,2048]{1,0:T(8,128)(2,1)} %copy-done.26, ...), custom_call_target="tpu_custom_call" | custom-call | tf_op jit(solution)/shard_map/pallas_call | solution.py:906
  490.0 2.8 add_convert_fusion.refs_2_
  492.7 14.9 %reduce-scatter.8.cloned.1.call-done.refs_1_ = bf16[256,1408]{1,0:T(8,128)(2,1)} async-done(((bf16[2048,1408]{1,0:T(8,128)(2,1)}), bf16[256,1408]{1,0:T(8,128)(2,1)}) %reduce-scatter.8.cloned.1.call-update) | async-done | bytes 720912 | tf_op jit(solution)/shard_map/reduce_scatter | solution.py:929
  509.8 8.7 %shard_map.253.refs_1_ = bf16[1024,1408]{1,0:T(8,128)(2,1)} custom-call(s32[3]{0:T(128)} %pad_add_fusion.refs_0_.place, bf16[256,2048]{1,0:T(8,128)(2,1)} %shard_map.233.refs_0_, bf16[256,2048]{1,0:T(8,128)(2,1)} %get-tuple-element.125.refs_1_, bf16[256,2048]{1,0:T(8,128)(2,1)} %get-tuple-element.126.refs_2_, bf16[128,2048]{1,0:T(8,128)(2,1)} %copy-done.26, ...), custom_call_target="tpu_custom_call" | custom-call | tf_op jit(solution)/shard_map/pallas_call | solution.py:906
  520.6 2.8 add_convert_fusion.4
  523.3 3.2 collective-permute-start.65
  526.6 2.0 constant_dynamic-update-slice_fusion.14
  528.6 4.0 collective-permute-done.72.refs_1_
  532.6 3.6 collective-permute-done.71.refs_0_
  541.5 2.2 collective-permute-start.64
  545.7 7.5 %collective-permute-done.73 = bf16[88,2048]{1,0:T(8,128)(2,1)S(1)} collective-permute-done((bf16[88,2048]{1,0:T(8,128)(2,1)S(1)}, bf16[88,2048]{1,0:T(8,128)(2,1)S(1)}, u32[]{:S(2)}, u32[]{:S(2)}) %collective-permute-start.73) | collective-permute-done | bytes 360480 | tf_op jit(solution)/shard_map/ppermute | solution.py:21
  556.9 3.2 collective-permute-done.74
  561.0 25.5 %collective-permute-done.66 = bf16[256,1408]{1,0:T(8,128)(2,1)S(1)} collective-permute-done((bf16[256,1408]{1,0:T(8,128)(2,1)S(1)}, bf16[256,1408]{1,0:T(8,128)(2,1)S(1)}, u32[]{:S(2)}, u32[]{:S(2)}) %collective-permute-start.66) | collective-permute-done | bytes 720928 | tf_op jit(solution)/shard_map/ppermute | solution.py:21
  588.5 3.5 bitcast_convert_fusion
  592.7 15.4 %collective-permute-done.67 = bf16[256,1152]{1,0:T(8,128)(2,1)S(1)} collective-permute-done((bf16[256,1152]{1,0:T(8,128)(2,1)S(1)}, bf16[256,1152]{1,0:T(8,128)(2,1)S(1)}, u32[]{:S(2)}, u32[]{:S(2)}) %collective-permute-start.67) | collective-permute-done | bytes 589856 | tf_op jit(solution)/shard_map/ppermute | solution.py:21
  608.3 3.0 collective-permute-start.70
  611.4 9.8 %collective-permute-done.69 = bf16[128,1152]{1,0:T(8,128)(2,1)S(1)} collective-permute-done((bf16[128,1152]{1,0:T(8,128)(2,1)S(1)}, bf16[128,1152]{1,0:T(8,128)(2,1)S(1)}, u32[]{:S(2)}, u32[]{:S(2)}) %collective-permute-start.69) | collective-permute-done | bytes 294944 | tf_op jit(solution)/shard_map/ppermute | solution.py:21
  626.8 7.7 %shard_map.257 = f32[256,5632]{1,0:T(8,128)} custom-call(s32[3]{0:T(128)} %pad_add_fusion.refs_0_.place, bf16[4,256,1408]{2,1,0:T(8,128)(2,1)} %bitcast.60), custom_call_target="tpu_custom_call" | custom-call | tf_op jit(solution)/shard_map/pallas_call | solution.py:967
  634.5 7.9 %shard_map.258 = f32[256,5632]{1,0:T(8,128)} custom-call(s32[3]{0:T(128)} %pad_add_fusion.refs_0_.place, bf16[4,256,1408]{2,1,0:T(8,128)(2,1)} %bitcast.61), custom_call_target="tpu_custom_call" | custom-call | tf_op jit(solution)/shard_map/pallas_call | solution.py:967
  (440 shorter events, 157.0 us)
Async XLA Ops:
  7.2 224.4 %all-gather.7.cloned.1.call-start = ((), (), s32[]{:S(2)}) async-start(), calls=%async_computation.3 | async-start | bytes 12976128 | tf_op jit(solution)/shard_map/all_gather | solution.py:640
  10.9 25.2 %collective-permute-start.3 = (bf16[256,2048]{1,0:T(8,128)(2,1)}, bf16[256,2048]{1,0:T(8,128)(2,1)}, u32[]{:S(2)}, u32[]{:S(2)}) collective-permute-start(bf16[256,2048]{1,0:T(8,128)(2,1)} %get-tuple-element.183), channel_id=1, source_target_pairs={{0,16},{8,24},{16,0},{24,8},{1,17},{9,25},{17,1},{25,9},{2,18},{10... | collective-permute-start | bytes 3145736 | tf_op jit(solution)/shard_map/ppermute | solution.py:21
  12.5 26.0 %collective-permute-start.2 = (bf16[256,2048]{1,0:T(8,128)(2,1)}, bf16[256,2048]{1,0:T(8,128)(2,1)}, u32[]{:S(2)}, u32[]{:S(2)}) collective-permute-start(bf16[256,2048]{1,0:T(8,128)(2,1)} %get-tuple-element.183), channel_id=1, source_target_pairs={{0,8},{8,0},{16,24},{24,16},{1,9},{9,1},{17,25},{25,17},{2,10},{10... | collective-permute-start | bytes 3145736 | tf_op jit(solution)/shard_map/ppermute | solution.py:21
  15.5 25.2 %collective-permute-start.1 = (bf16[272,768]{1,0:T(8,128)(2,1)}, bf16[272,768]{1,0:T(8,128)(2,1)S(1)}, u32[]{:S(2)}, u32[]{:S(2)}) collective-permute-start(bf16[272,768]{1,0:T(8,128)(2,1)} %pad_maximum_fusion.13), channel_id=1, source_target_pairs={{0,6},{1,7},{2,4},{3,5},{4,2},{5,3},{6,0},{7,1},{8,14},{9,15},{10,... | collective-permute-start | bytes 1253384 | tf_op jit(solution)/shard_map/ppermute | solution.py:21
  17.1 23.7 %collective-permute-start = (bf16[272,768]{1,0:T(8,128)(2,1)}, bf16[272,768]{1,0:T(8,128)(2,1)}, u32[]{:S(2)}, u32[]{:S(2)}) collective-permute-start(bf16[272,768]{1,0:T(8,128)(2,1)} %pad_maximum_fusion.13), channel_id=1, source_target_pairs={{0,2},{1,3},{2,0},{3,1},{4,6},{5,7},{6,4},{7,5},{8,10},{9,11},{10,... | collective-permute-start | bytes 1253384 | tf_op jit(solution)/shard_map/ppermute | solution.py:21
  43.1 16.9 %collective-permute-start.8 = (bf16[128,2048]{1,0:T(8,128)(2,1)S(1)}, bf16[128,2048]{1,0:T(8,128)(2,1)S(1)}, u32[]{:S(2)}, u32[]{:S(2)}) collective-permute-start(bf16[128,2048]{1,0:T(8,128)(2,1)S(1)} %slice.198), channel_id=1, source_target_pairs={{0,8},{8,0},{16,24},{24,16},{1,9},{9,1},{17,25},{25,17},{2,10},{10... | collective-permute-start | bytes 1572872 | tf_op jit(solution)/shard_map/ppermute | solution.py:21
  43.7 16.3 %collective-permute-start.7 = (bf16[128,2048]{1,0:T(8,128)(2,1)S(1)}, bf16[128,2048]{1,0:T(8,128)(2,1)S(1)}, u32[]{:S(2)}, u32[]{:S(2)}) collective-permute-start(bf16[128,2048]{1,0:T(8,128)(2,1)S(1)} %slice.197), channel_id=1, source_target_pairs={{0,16},{8,24},{16,0},{24,8},{1,17},{9,25},{17,1},{25,9},{2,18},{10... | collective-permute-start | bytes 1572872 | tf_op jit(solution)/shard_map/ppermute | solution.py:21
  61.8 213.5 %all-gather.9.cloned.1.call-start = ((), (), s32[]{:S(2)}) async-start(), calls=%async_computation.4 | async-start | bytes 6488064 | tf_op jit(solution)/shard_map/all_gather | solution.py:641
  62.6 306.8 %reduce-scatter.4.cloned.1.call-start = ((), (), s32[]{:S(2)}) async-start(), calls=%async_computation.5 | async-start | bytes 6488064 | tf_op jit(solution)/shard_map/reduce_scatter | solution.py:773
  62.6 16.3 %collective-permute-start.12 = (bf16[1024,512]{1,0:T(8,128)(2,1)}, bf16[1024,512]{1,0:T(8,128)(2,1)S(1)}, u32[]{:S(2)}, u32[]{:S(2)}) collective-permute-start(bf16[1024,512]{1,0:T(8,128)(2,1)} %get-tuple-element.101.refs_6_), channel_id=1, source_target_pairs={{0,1},{1,0},{2,3},{3,2},{4,5},{5,4},{6,7},{7,6},{8,9},{9,8},{10,11... | collective-permute-start | bytes 3145736 | tf_op jit(solution)/shard_map/ppermute | solution.py:21
  62.7 25.8 %collective-permute-start.11 = (bf16[1024,512]{1,0:T(8,128)(2,1)}, bf16[1024,512]{1,0:T(8,128)(2,1)S(1)}, u32[]{:S(2)}, u32[]{:S(2)}) collective-permute-start(bf16[1024,512]{1,0:T(8,128)(2,1)} %get-tuple-element.101.refs_6_), channel_id=1, source_target_pairs={{0,16},{8,24},{16,0},{24,8},{1,17},{9,25},{17,1},{25,9},{2,18},{10... | collective-permute-start | bytes 3145736 | tf_op jit(solution)/shard_map/ppermute | solution.py:21
  64.3 25.4 %collective-permute-start.10 = (bf16[1024,512]{1,0:T(8,128)(2,1)}, bf16[1024,512]{1,0:T(8,128)(2,1)S(1)}, u32[]{:S(2)}, u32[]{:S(2)}) collective-permute-start(bf16[1024,512]{1,0:T(8,128)(2,1)} %get-tuple-element.101.refs_6_), channel_id=1, source_target_pairs={{0,8},{8,0},{16,24},{24,16},{1,9},{9,1},{17,25},{25,17},{2,10},{10... | collective-permute-start | bytes 3145736 | tf_op jit(solution)/shard_map/ppermute | solution.py:21
  64.8 14.1 %collective-permute-start.9 = (bf16[1088,256]{1,0:T(8,128)(2,1)}, bf16[1088,256]{1,0:T(8,128)(2,1)S(1)}, u32[]{:S(2)}, u32[]{:S(2)}) collective-permute-start(bf16[1088,256]{1,0:T(8,128)(2,1)} %get-tuple-element.100), channel_id=1, source_target_pairs={{0,1},{1,0},{2,3},{3,2},{4,5},{5,4},{6,7},{7,6},{8,9},{9,8},{10,11... | collective-permute-start | bytes 1671176 | tf_op jit(solution)/shard_map/ppermute | solution.py:21
  90.7 16.9 %collective-permute-start.16 = (bf16[1024,512]{1,0:T(8,128)(2,1)}, bf16[1024,512]{1,0:T(8,128)(2,1)S(1)}, u32[]{:S(2)}, u32[]{:S(2)}) collective-permute-start(bf16[1024,512]{1,0:T(8,128)(2,1)} %get-tuple-element.103.refs_7_), channel_id=1, source_target_pairs={{0,1},{1,0},{2,3},{3,2},{4,5},{5,4},{6,7},{7,6},{8,9},{9,8},{10,11... | collective-permute-start | bytes 3145736 | tf_op jit(solution)/shard_map/ppermute | solution.py:21
  90.7 17.7 %collective-permute-start.17 = (bf16[1024,512]{1,0:T(8,128)(2,1)}, bf16[1024,512]{1,0:T(8,128)(2,1)S(1)}, u32[]{:S(2)}, u32[]{:S(2)}) collective-permute-start(bf16[1024,512]{1,0:T(8,128)(2,1)} %get-tuple-element.104.refs_8_), channel_id=1, source_target_pairs={{0,1},{1,0},{2,3},{3,2},{4,5},{5,4},{6,7},{7,6},{8,9},{9,8},{10,11... | collective-permute-start | bytes 3145736 | tf_op jit(solution)/shard_map/ppermute | solution.py:21
  110.3 35.4 %collective-permute-start.24 = (bf16[1024,512]{1,0:T(8,128)(2,1)}, bf16[1024,512]{1,0:T(8,128)(2,1)S(1)}, u32[]{:S(2)}, u32[]{:S(2)}) collective-permute-start(bf16[1024,512]{1,0:T(8,128)(2,1)} %get-tuple-element.109.refs_4_.refs_5_), channel_id=1, source_target_pairs={{0,1},{1,0},{2,3},{3,2},{4,5},{5,4},{6,7},{7,6},{8,9},{9,8},{10,11... | collective-permute-start | bytes 3145736 | tf_op jit(solution)/shard_map/ppermute | solution.py:21
  110.4 35.4 %collective-permute-start.23 = (bf16[1024,512]{1,0:T(8,128)(2,1)}, bf16[1024,512]{1,0:T(8,128)(2,1)S(1)}, u32[]{:S(2)}, u32[]{:S(2)}) collective-permute-start(bf16[1024,512]{1,0:T(8,128)(2,1)} %get-tuple-element.109.refs_4_.refs_5_), channel_id=1, source_target_pairs={{0,16},{8,24},{16,0},{24,8},{1,17},{9,25},{17,1},{25,9},{2,18},{10... | collective-permute-start | bytes 3145736 | tf_op jit(solution)/shard_map/ppermute | solution.py:21
  111.6 35.1 %collective-permute-start.22 = (bf16[1024,512]{1,0:T(8,128)(2,1)}, bf16[1024,512]{1,0:T(8,128)(2,1)S(1)}, u32[]{:S(2)}, u32[]{:S(2)}) collective-permute-start(bf16[1024,512]{1,0:T(8,128)(2,1)} %get-tuple-element.109.refs_4_.refs_5_), channel_id=1, source_target_pairs={{0,8},{8,0},{16,24},{24,16},{1,9},{9,1},{17,25},{25,17},{2,10},{10... | collective-permute-start | bytes 3145736 | tf_op jit(solution)/shard_map/ppermute | solution.py:21
  131.2 14.5 %collective-permute-start.20 = (bf16[256,256]{1,0:T(8,128)(2,1)}, bf16[256,256]{1,0:T(8,128)(2,1)S(1)}, u32[]{:S(2)}, u32[]{:S(2)}) collective-permute-start(bf16[256,256]{1,0:T(8,128)(2,1)} %get-tuple-element.108.refs_2_), channel_id=1, source_target_pairs={{0,2},{1,3},{2,4},{3,5},{4,6},{5,7},{8,10},{9,11},{10,12},{11,13},... | collective-permute-start | bytes 393224 | tf_op jit(solution)/shard_map/ppermute | solution.py:95
  148.7 23.3 %collective-permute-start.27 = (bf16[1024,512]{1,0:T(8,128)(2,1)}, bf16[1024,512]{1,0:T(8,128)(2,1)S(1)}, u32[]{:S(2)}, u32[]{:S(2)}) collective-permute-start(bf16[1024,512]{1,0:T(8,128)(2,1)} %get-tuple-element.110.refs_3_.refs_5_.refs_6_), channel_id=1, source_target_pairs={{0,1},{1,0},{2,3},{3,2},{4,5},{5,4},{6,7},{7,6},{8,9},{9,8},{10,11... | collective-permute-start | bytes 3145736 | tf_op jit(solution)/shard_map/ppermute | solution.py:21
  152.1 19.9 %collective-permute-start.28 = (bf16[1024,512]{1,0:T(8,128)(2,1)}, bf16[1024,512]{1,0:T(8,128)(2,1)S(1)}, u32[]{:S(2)}, u32[]{:S(2)}) collective-permute-start(bf16[1024,512]{1,0:T(8,128)(2,1)} %get-tuple-element.111.refs_4_.refs_6_.refs_7_), channel_id=1, source_target_pairs={{0,1},{1,0},{2,3},{3,2},{4,5},{5,4},{6,7},{7,6},{8,9},{9,8},{10,11... | collective-permute-start | bytes 3145736 | tf_op jit(solution)/shard_map/ppermute | solution.py:21
  154.3 17.7 %collective-permute-start.26 = (bf16[512,512]{1,0:T(8,128)(2,1)S(1)}, bf16[512,512]{1,0:T(8,128)(2,1)S(1)}, u32[]{:S(2)}, u32[]{:S(2)}) collective-permute-start(bf16[512,512]{1,0:T(8,128)(2,1)S(1)} %slice.208), channel_id=1, source_target_pairs={{0,8},{8,0},{16,24},{24,16},{1,9},{9,1},{17,25},{25,17},{2,10},{10... | collective-permute-start | bytes 1572872 | tf_op jit(solution)/shard_map/ppermute | solution.py:21
  155.8 16.1 %collective-permute-start.25 = (bf16[512,512]{1,0:T(8,128)(2,1)S(1)}, bf16[512,512]{1,0:T(8,128)(2,1)S(1)}, u32[]{:S(2)}, u32[]{:S(2)}) collective-permute-start(bf16[512,512]{1,0:T(8,128)(2,1)S(1)} %slice.207), channel_id=1, source_target_pairs={{0,16},{8,24},{16,0},{24,8},{1,17},{9,25},{17,1},{25,9},{2,18},{10... | collective-permute-start | bytes 1572872 | tf_op jit(solution)/shard_map/ppermute | solution.py:21
  186.4 25.6 %collective-permute-start.32 = (bf16[256,2048]{1,0:T(8,128)(2,1)}, bf16[256,2048]{1,0:T(8,128)(2,1)}, u32[]{:S(2)}, u32[]{:S(2)}) collective-permute-start(bf16[256,2048]{1,0:T(8,128)(2,1)} %get-tuple-element.115.refs_0_), channel_id=1, source_target_pairs={{0,16},{8,24},{16,0},{24,8},{1,17},{9,25},{17,1},{25,9},{2,18},{10... | collective-permute-start | bytes 3145736 | tf_op jit(solution)/shard_map/ppermute | solution.py:21
  188.2 25.2 %collective-permute-start.31 = (bf16[256,2048]{1,0:T(8,128)(2,1)}, bf16[256,2048]{1,0:T(8,128)(2,1)}, u32[]{:S(2)}, u32[]{:S(2)}) collective-permute-start(bf16[256,2048]{1,0:T(8,128)(2,1)} %get-tuple-element.115.refs_0_), channel_id=1, source_target_pairs={{0,8},{8,0},{16,24},{24,16},{1,9},{9,1},{17,25},{25,17},{2,10},{10... | collective-permute-start | bytes 3145736 | tf_op jit(solution)/shard_map/ppermute | solution.py:21
  229.5 23.5 %collective-permute-start.36 = (bf16[256,2048]{1,0:T(8,128)(2,1)}, bf16[256,2048]{1,0:T(8,128)(2,1)S(1)}, u32[]{:S(2)}, u32[]{:S(2)}) collective-permute-start(bf16[256,2048]{1,0:T(8,128)(2,1)} %shard_map.233.refs_0_), channel_id=1, source_target_pairs={{0,16},{8,24},{16,0},{24,8},{1,17},{9,25},{17,1},{25,9},{2,18},{10... | collective-permute-start | bytes 3145736 | tf_op jit(solution)/shard_map/ppermute | solution.py:21
  230.1 23.4 %collective-permute-start.35 = (bf16[256,2048]{1,0:T(8,128)(2,1)}, bf16[256,2048]{1,0:T(8,128)(2,1)S(1)}, u32[]{:S(2)}, u32[]{:S(2)}) collective-permute-start(bf16[256,2048]{1,0:T(8,128)(2,1)} %shard_map.233.refs_0_), channel_id=1, source_target_pairs={{0,8},{8,0},{16,24},{24,16},{1,9},{9,1},{17,25},{25,17},{2,10},{10... | collective-permute-start | bytes 3145736 | tf_op jit(solution)/shard_map/ppermute | solution.py:21
  267.4 176.1 %reduce-scatter.6.cloned.1.call-start = ((), (), s32[]{:S(2)}) async-start(), calls=%async_computation.6 | async-start | bytes 6488064 | tf_op jit(solution)/shard_map/reduce_scatter | solution.py:826
  267.5 34.6 %collective-permute-start.40 = (bf16[256,2048]{1,0:T(8,128)(2,1)}, bf16[256,2048]{1,0:T(8,128)(2,1)S(1)}, u32[]{:S(2)}, u32[]{:S(2)}) collective-permute-start(bf16[256,2048]{1,0:T(8,128)(2,1)} %get-tuple-element.127.refs_5_), channel_id=1, source_target_pairs={{0,16},{8,24},{16,0},{24,8},{1,17},{9,25},{17,1},{25,9},{2,18},{10... | collective-permute-start | bytes 3145736 | tf_op jit(solution)/shard_map/ppermute | solution.py:21
  268.3 33.7 %collective-permute-start.39 = (bf16[256,2048]{1,0:T(8,128)(2,1)}, bf16[256,2048]{1,0:T(8,128)(2,1)S(1)}, u32[]{:S(2)}, u32[]{:S(2)}) collective-permute-start(bf16[256,2048]{1,0:T(8,128)(2,1)} %get-tuple-element.127.refs_5_), channel_id=1, source_target_pairs={{0,8},{8,0},{16,24},{24,16},{1,9},{9,1},{17,25},{25,17},{2,10},{10... | collective-permute-start | bytes 3145736 | tf_op jit(solution)/shard_map/ppermute | solution.py:21
  273.4 28.6 %collective-permute-start.38 = (bf16[128,2048]{1,0:T(8,128)(2,1)}, bf16[128,2048]{1,0:T(8,128)(2,1)S(1)}, u32[]{:S(2)}, u32[]{:S(2)}) collective-permute-start(bf16[128,2048]{1,0:T(8,128)(2,1)} %slice.212), channel_id=1, source_target_pairs={{0,8},{8,0},{16,24},{24,16},{1,9},{9,1},{17,25},{25,17},{2,10},{10... | collective-permute-start | bytes 1572872 | tf_op jit(solution)/shard_map/ppermute | solution.py:21
  274.1 27.9 %collective-permute-start.37 = (bf16[128,2048]{1,0:T(8,128)(2,1)}, bf16[128,2048]{1,0:T(8,128)(2,1)S(1)}, u32[]{:S(2)}, u32[]{:S(2)}) collective-permute-start(bf16[128,2048]{1,0:T(8,128)(2,1)} %slice.211), channel_id=1, source_target_pairs={{0,16},{8,24},{16,0},{24,8},{1,17},{9,25},{17,1},{25,9},{2,18},{10... | collective-permute-start | bytes 1572872 | tf_op jit(solution)/shard_map/ppermute | solution.py:21
  306.6 20.1 %collective-permute-start.42 = (bf16[128,2048]{1,0:T(8,128)(2,1)S(1)}, bf16[128,2048]{1,0:T(8,128)(2,1)S(1)}, u32[]{:S(2)}, u32[]{:S(2)}) collective-permute-start(bf16[128,2048]{1,0:T(8,128)(2,1)S(1)} %slice.214), channel_id=1, source_target_pairs={{0,8},{8,0},{16,24},{24,16},{1,9},{9,1},{17,25},{25,17},{2,10},{10... | collective-permute-start | bytes 1572872 | tf_op jit(solution)/shard_map/ppermute | solution.py:21
  307.7 19.0 %collective-permute-start.41 = (bf16[128,2048]{1,0:T(8,128)(2,1)S(1)}, bf16[128,2048]{1,0:T(8,128)(2,1)S(1)}, u32[]{:S(2)}, u32[]{:S(2)}) collective-permute-start(bf16[128,2048]{1,0:T(8,128)(2,1)S(1)} %slice.213), channel_id=1, source_target_pairs={{0,16},{8,24},{16,0},{24,8},{1,17},{9,25},{17,1},{25,9},{2,18},{10... | collective-permute-start | bytes 1572872 | tf_op jit(solution)/shard_map/ppermute | solution.py:21
  344.3 16.4 %collective-permute-start.45 = (bf16[128,2048]{1,0:T(8,128)(2,1)S(1)}, bf16[128,2048]{1,0:T(8,128)(2,1)S(1)}, u32[]{:S(2)}, u32[]{:S(2)}) collective-permute-start(bf16[128,2048]{1,0:T(8,128)(2,1)S(1)} %add_convert_fusion.8), channel_id=1, source_target_pairs={{0,8},{8,0},{16,24},{24,16},{1,9},{9,1},{17,25},{25,17},{2,10},{10... | collective-permute-start | bytes 1572872 | tf_op jit(solution)/shard_map/ppermute | solution.py:21
  345.5 19.2 %collective-permute-start.46 = (bf16[128,2048]{1,0:T(8,128)(2,1)}, bf16[128,2048]{1,0:T(8,128)(2,1)S(1)}, u32[]{:S(2)}, u32[]{:S(2)}) collective-permute-start(bf16[128,2048]{1,0:T(8,128)(2,1)} %get-tuple-element.140), channel_id=1, source_target_pairs={{0,8},{8,0},{16,24},{24,16},{1,9},{9,1},{17,25},{25,17},{2,10},{10... | collective-permute-start | bytes 1572872 | tf_op jit(solution)/shard_map/ppermute | solution.py:21
  346.4 18.3 %collective-permute-start.47 = (bf16[128,2048]{1,0:T(8,128)(2,1)}, bf16[128,2048]{1,0:T(8,128)(2,1)S(1)}, u32[]{:S(2)}, u32[]{:S(2)}) collective-permute-start(bf16[128,2048]{1,0:T(8,128)(2,1)} %get-tuple-element.141), channel_id=1, source_target_pairs={{0,16},{8,24},{16,0},{24,8},{1,17},{9,25},{17,1},{25,9},{2,18},{10... | collective-permute-start | bytes 1572872 | tf_op jit(solution)/shard_map/ppermute | solution.py:21
  348.7 18.9 %collective-permute-start.48 = (bf16[128,2048]{1,0:T(8,128)(2,1)S(1)}, bf16[128,2048]{1,0:T(8,128)(2,1)S(1)}, u32[]{:S(2)}, u32[]{:S(2)}) collective-permute-start(bf16[128,2048]{1,0:T(8,128)(2,1)S(1)} %add_convert_fusion.7), channel_id=1, source_target_pairs={{0,16},{8,24},{16,0},{24,8},{1,17},{9,25},{17,1},{25,9},{2,18},{10... | collective-permute-start | bytes 1572872 | tf_op jit(solution)/shard_map/ppermute | solution.py:21
  369.4 138.2 %reduce-scatter.8.cloned.1.call-start = ((), (), s32[]{:S(2)}) async-start(), calls=%async_computation.7 | async-start | bytes 6488064 | tf_op jit(solution)/shard_map/reduce_scatter | solution.py:929
  369.7 37.7 %collective-permute-start.49 = (bf16[128,2048]{1,0:T(8,128)(2,1)}, bf16[128,2048]{1,0:T(8,128)(2,1)S(1)}, u32[]{:S(2)}, u32[]{:S(2)}) collective-permute-start(bf16[128,2048]{1,0:T(8,128)(2,1)} %shard_map.246), channel_id=1, source_target_pairs={{0,16},{8,24},{16,0},{24,8},{1,17},{9,25},{17,1},{25,9},{2,18},{10... | collective-permute-start | bytes 1572872 | tf_op jit(solution)/shard_map/ppermute | solution.py:21
  370.8 36.6 %collective-permute-start.50 = (bf16[128,2048]{1,0:T(8,128)(2,1)S(1)}, bf16[128,2048]{1,0:T(8,128)(2,1)S(1)}, u32[]{:S(2)}, u32[]{:S(2)}) collective-permute-start(bf16[128,2048]{1,0:T(8,128)(2,1)S(1)} %copy-done.54), channel_id=1, source_target_pairs={{0,8},{8,0},{16,24},{24,16},{1,9},{9,1},{17,25},{25,17},{2,10},{10... | collective-permute-start | bytes 1572872 | tf_op jit(solution)/shard_map/ppermute | solution.py:21
  381.1 26.3 %collective-permute-start.51 = (bf16[256,512]{1,0:T(8,128)(2,1)}, bf16[256,512]{1,0:T(8,128)(2,1)S(1)}, u32[]{:S(2)}, u32[]{:S(2)}) collective-permute-start(bf16[256,512]{1,0:T(8,128)(2,1)} %get-tuple-element.155), channel_id=1, source_target_pairs={{0,8},{8,0},{16,24},{24,16},{1,9},{9,1},{17,25},{25,17},{2,10},{10... | collective-permute-start | bytes 786440 | tf_op jit(solution)/shard_map/ppermute | solution.py:21
  382.2 25.2 %collective-permute-start.52 = (bf16[256,512]{1,0:T(8,128)(2,1)}, bf16[256,512]{1,0:T(8,128)(2,1)S(1)}, u32[]{:S(2)}, u32[]{:S(2)}) collective-permute-start(bf16[256,512]{1,0:T(8,128)(2,1)} %get-tuple-element.156), channel_id=1, source_target_pairs={{0,16},{8,24},{16,0},{24,8},{1,17},{9,25},{17,1},{25,9},{2,18},{10... | collective-permute-start | bytes 786440 | tf_op jit(solution)/shard_map/ppermute | solution.py:21
  383.1 24.2 %collective-permute-start.53 = (bf16[256,512]{1,0:T(8,128)(2,1)}, bf16[256,512]{1,0:T(8,128)(2,1)S(1)}, u32[]{:S(2)}, u32[]{:S(2)}) collective-permute-start(bf16[256,512]{1,0:T(8,128)(2,1)} %get-tuple-element.157), channel_id=1, source_target_pairs={{0,24},{8,16},{16,8},{24,0},{1,25},{9,17},{17,9},{25,1},{2,26},{10... | collective-permute-start | bytes 786440 | tf_op jit(solution)/shard_map/ppermute | solution.py:21
  409.9 15.1 %collective-permute-start.54 = (bf16[256,256]{1,0:T(8,128)(2,1)S(1)}, bf16[256,256]{1,0:T(8,128)(2,1)S(1)}, u32[]{:S(2)}, u32[]{:S(2)}) collective-permute-start(bf16[256,256]{1,0:T(8,128)(2,1)S(1)} %get-tuple-element.206), channel_id=1, source_target_pairs={{1,0},{2,1},{3,2},{4,3},{5,4},{6,5},{7,6},{9,8},{10,9},{11,10},{12... | collective-permute-start | bytes 393224 | tf_op jit(solution)/shard_map/ppermute | solution.py:95
  411.9 18.1 %collective-permute-start.55 = (bf16[256,256]{1,0:T(8,128)(2,1)S(1)}, bf16[256,256]{1,0:T(8,128)(2,1)S(1)}, u32[]{:S(2)}, u32[]{:S(2)}) collective-permute-start(bf16[256,256]{1,0:T(8,128)(2,1)S(1)} %get-tuple-element.207), channel_id=1, source_target_pairs={{2,0},{3,1},{4,2},{5,3},{6,4},{7,5},{10,8},{11,9},{12,10},{13,11},... | collective-permute-start | bytes 393224 | tf_op jit(solution)/shard_map/ppermute | solution.py:95
  443.6 183.1 %all-gather.11.cloned.1.call-start = ((), (), s32[]{:S(2)}) async-start(), calls=%async_computation.8 | async-start | bytes 3604480 | tf_op jit(solution)/shard_map/all_gather | solution.py:939
  444.3 32.8 %collective-permute-start.59 = (bf16[128,2048]{1,0:T(8,128)(2,1)}, bf16[128,2048]{1,0:T(8,128)(2,1)S(1)}, u32[]{:S(2)}, u32[]{:S(2)}) collective-permute-start(bf16[128,2048]{1,0:T(8,128)(2,1)} %get-tuple-element.167), channel_id=1, source_target_pairs={{0,8},{8,0},{16,24},{24,16},{1,9},{9,1},{17,25},{25,17},{2,10},{10... | collective-permute-start | bytes 1572872 | tf_op jit(solution)/shard_map/ppermute | solution.py:21
  445.1 31.9 %collective-permute-start.60 = (bf16[128,2048]{1,0:T(8,128)(2,1)}, bf16[128,2048]{1,0:T(8,128)(2,1)S(1)}, u32[]{:S(2)}, u32[]{:S(2)}) collective-permute-start(bf16[128,2048]{1,0:T(8,128)(2,1)} %get-tuple-element.168), channel_id=1, source_target_pairs={{0,16},{8,24},{16,0},{24,8},{1,17},{9,25},{17,1},{25,9},{2,18},{10... | collective-permute-start | bytes 1572872 | tf_op jit(solution)/shard_map/ppermute | solution.py:21
  445.8 22.0 %collective-permute-start.58 = (bf16[256,768]{1,0:T(8,128)(2,1)}, bf16[256,768]{1,0:T(8,128)(2,1)S(1)}, u32[]{:S(2)}, u32[]{:S(2)}) collective-permute-start(bf16[256,768]{1,0:T(8,128)(2,1)} %get-tuple-element.210.refs_21_), channel_id=1, source_target_pairs={{0,24},{8,16},{16,8},{24,0},{1,25},{9,17},{17,9},{25,1},{2,26},{10... | collective-permute-start | bytes 1179656 | tf_op jit(solution)/shard_map/ppermute | solution.py:21
  447.8 26.9 %collective-permute-start.56 = (bf16[256,768]{1,0:T(8,128)(2,1)}, bf16[256,768]{1,0:T(8,128)(2,1)S(1)}, u32[]{:S(2)}, u32[]{:S(2)}) collective-permute-start(bf16[256,768]{1,0:T(8,128)(2,1)} %get-tuple-element.211.refs_19_), channel_id=1, source_target_pairs={{0,8},{8,0},{16,24},{24,16},{1,9},{9,1},{17,25},{25,17},{2,10},{10... | collective-permute-start | bytes 1179656 | tf_op jit(solution)/shard_map/ppermute | solution.py:21
  448.6 28.4 %collective-permute-start.57 = (bf16[256,768]{1,0:T(8,128)(2,1)}, bf16[256,768]{1,0:T(8,128)(2,1)S(1)}, u32[]{:S(2)}, u32[]{:S(2)}) collective-permute-start(bf16[256,768]{1,0:T(8,128)(2,1)} %get-tuple-element.212.refs_20_), channel_id=1, source_target_pairs={{0,16},{8,24},{16,0},{24,8},{1,17},{9,25},{17,1},{25,9},{2,18},{10... | collective-permute-start | bytes 1179656 | tf_op jit(solution)/shard_map/ppermute | solution.py:21
  467.8 22.1 %collective-permute-start.62 = (bf16[128,2048]{1,0:T(8,128)(2,1)}, bf16[128,2048]{1,0:T(8,128)(2,1)}, u32[]{:S(2)}, u32[]{:S(2)}) collective-permute-start(bf16[128,2048]{1,0:T(8,128)(2,1)} %add_convert_fusion.5), channel_id=1, source_target_pairs={{0,16},{8,24},{16,0},{24,8},{1,17},{9,25},{17,1},{25,9},{2,18},{10... | collective-permute-start | bytes 1572872 | tf_op jit(solution)/shard_map/ppermute | solution.py:21
  489.8 28.7 %collective-permute-start.63 = (bf16[1024,1408]{1,0:T(8,128)(2,1)}, bf16[1024,1408]{1,0:T(8,128)(2,1)}, u32[]{:S(2)}, u32[]{:S(2)}) collective-permute-start(bf16[1024,1408]{1,0:T(8,128)(2,1)} %shard_map.252.refs_19_), channel_id=1, source_target_pairs={{0,1},{1,0},{2,3},{3,2},{4,5},{5,4},{6,7},{7,6},{8,9},{9,8},{10,11... | collective-permute-start | bytes 8650760 | tf_op jit(solution)/shard_map/ppermute | solution.py:21
  507.7 126.8 %all-gather.13.cloned.1.call-start = ((), (), s32[]{:S(2)}) async-start(), calls=%async_computation.9 | async-start | bytes 3604480 | tf_op jit(solution)/shard_map/all_gather | solution.py:940
  507.7 24.8 %collective-permute-start.72 = (bf16[176,2048]{1,0:T(8,128)(2,1)}, bf16[176,2048]{1,0:T(8,128)(2,1)}, u32[]{:S(2)}, u32[]{:S(2)}) collective-permute-start(bf16[176,2048]{1,0:T(8,128)(2,1)} %get-tuple-element.175), channel_id=1, source_target_pairs={{0,16},{8,24},{16,0},{24,8},{1,17},{9,25},{17,1},{25,9},{2,18},{10... | collective-permute-start | bytes 2162696 | tf_op jit(solution)/shard_map/ppermute | solution.py:21
  509.3 26.9 %collective-permute-start.71 = (bf16[176,2048]{1,0:T(8,128)(2,1)}, bf16[176,2048]{1,0:T(8,128)(2,1)}, u32[]{:S(2)}, u32[]{:S(2)}) collective-permute-start(bf16[176,2048]{1,0:T(8,128)(2,1)} %get-tuple-element.175), channel_id=1, source_target_pairs={{0,8},{8,0},{16,24},{24,16},{1,9},{9,1},{17,25},{25,17},{2,10},{10... | collective-permute-start | bytes 2162696 | tf_op jit(solution)/shard_map/ppermute | solution.py:21
  523.3 30.7 %collective-permute-start.65 = (bf16[256,1408]{1,0:T(8,128)(2,1)}, bf16[256,1408]{1,0:T(8,128)(2,1)}, u32[]{:S(2)}, u32[]{:S(2)}) collective-permute-start(bf16[256,1408]{1,0:T(8,128)(2,1)} %get-tuple-element.187), channel_id=1, source_target_pairs={{0,2},{1,3},{2,0},{3,1},{4,6},{5,7},{6,4},{7,5},{8,10},{9,11},{10,... | collective-permute-start | bytes 2162696 | tf_op jit(solution)/shard_map/ppermute | solution.py:21
  537.2 16.0 %collective-permute-start.73 = (bf16[88,2048]{1,0:T(8,128)(2,1)S(1)}, bf16[88,2048]{1,0:T(8,128)(2,1)S(1)}, u32[]{:S(2)}, u32[]{:S(2)}) collective-permute-start(bf16[88,2048]{1,0:T(8,128)(2,1)S(1)} %slice.247), channel_id=1, source_target_pairs={{0,16},{8,24},{16,0},{24,8},{1,17},{9,25},{17,1},{25,9},{2,18},{10... | collective-permute-start | bytes 1081352 | tf_op jit(solution)/shard_map/ppermute | solution.py:21
  541.4 18.7 %collective-permute-start.74 = (bf16[88,2048]{1,0:T(8,128)(2,1)}, bf16[88,2048]{1,0:T(8,128)(2,1)S(1)}, u32[]{:S(2)}, u32[]{:S(2)}) collective-permute-start(bf16[88,2048]{1,0:T(8,128)(2,1)} %slice.248), channel_id=1, source_target_pairs={{0,8},{8,0},{16,24},{24,16},{1,9},{9,1},{17,25},{25,17},{2,10},{10... | collective-permute-start | bytes 1081352 | tf_op jit(solution)/shard_map/ppermute | solution.py:21
  541.5 19.6 %collective-permute-start.64 = (bf16[256,1408]{1,0:T(8,128)(2,1)}, bf16[256,1408]{1,0:T(8,128)(2,1)}, u32[]{:S(2)}, u32[]{:S(2)}) collective-permute-start(bf16[256,1408]{1,0:T(8,128)(2,1)} %get-tuple-element.186), channel_id=1, source_target_pairs={{0,2},{1,3},{2,0},{3,1},{4,6},{5,7},{6,4},{7,5},{8,10},{9,11},{10,... | collective-permute-start | bytes 2162696 | tf_op jit(solution)/shard_map/ppermute | solution.py:21
  555.8 30.7 %collective-permute-start.66 = (bf16[256,1408]{1,0:T(8,128)(2,1)S(1)}, bf16[256,1408]{1,0:T(8,128)(2,1)S(1)}, u32[]{:S(2)}, u32[]{:S(2)}) collective-permute-start(bf16[256,1408]{1,0:T(8,128)(2,1)S(1)} %add_convert_fusion.1), channel_id=1, source_target_pairs={{0,6},{1,7},{2,4},{3,5},{4,2},{5,3},{6,0},{7,1},{8,14},{9,15},{10,... | collective-permute-start | bytes 2162696 | tf_op jit(solution)/shard_map/ppermute | solution.py:21
  588.4 19.8 %collective-permute-start.67 = (bf16[256,1152]{1,0:T(8,128)(2,1)S(1)}, bf16[256,1152]{1,0:T(8,128)(2,1)S(1)}, u32[]{:S(2)}, u32[]{:S(2)}) collective-permute-start(bf16[256,1152]{1,0:T(8,128)(2,1)S(1)} %get-tuple-element.204), channel_id=1, source_target_pairs={{0,8},{8,0},{16,24},{24,16},{1,9},{9,1},{17,25},{25,17},{2,10},{10... | collective-permute-start | bytes 1769480 | tf_op jit(solution)/shard_map/ppermute | solution.py:21
  588.4 19.8 %collective-permute-start.68 = (bf16[256,1152]{1,0:T(8,128)(2,1)S(1)}, bf16[256,1152]{1,0:T(8,128)(2,1)S(1)}, u32[]{:S(2)}, u32[]{:S(2)}) collective-permute-start(bf16[256,1152]{1,0:T(8,128)(2,1)S(1)} %get-tuple-element.204), channel_id=1, source_target_pairs={{0,16},{8,24},{16,0},{24,8},{1,17},{9,25},{17,1},{25,9},{2,18},{10... | collective-permute-start | bytes 1769480 | tf_op jit(solution)/shard_map/ppermute | solution.py:21
  (112 other events, 727.4 us)
Sparse Core Ops, SparseCore 0:
  61.9 115.3 all-gather.6
  179.0 58.1 all-gather.8
  267.5 68.1 reduce-scatter.3
  369.5 70.6 reduce-scatter.5
  443.7 63.8 reduce-scatter.7
  509.3 55.9 all-gather.10
  567.1 55.6 all-gather.12

commit v3 on v2

--- a/solution.py
+++ b/solution.py
@@ -499,14 +499,16 @@
         out_ref[to] = refs[m][...]
 
 
-def unshare_kernel(slots, seqs, place, part_ref, out_ref):
-    piece = part_ref.shape[2] // seqs
-    parts = []
-    for q in range(seqs):
-        for s in range(slots):
-            part = part_ref[s, :, q * piece : (q + 1) * piece]
-            parts.append(part.astype(F32))
-    out_ref[...] = jnp.concatenate(parts, axis=1)
+def unshare_kernel(slots, seqs, part_ref, gate_ref, up_ref):
+    width = part_ref.shape[2] // 2
+    piece = width // seqs
+    for n, ref in enumerate((gate_ref, up_ref)):
+        parts = [
+            part_ref[s, :, n * width + q * piece : n * width + (q + 1) * piece]
+            for q in range(seqs)
+            for s in range(slots)
+        ]
+        ref[...] = jnp.concatenate(parts, axis=1).astype(F32)
 
 
 def tie(value, *after):
@@ -779,12 +781,13 @@
     grad_gate = grad_hidden * up_out * sig_gate * (1.0 + gate_out * (1.0 - sig_gate))
     grad_up = grad_hidden * gate_out * sig_gate
     grad_gu = jnp.concatenate([grad_gate.astype(BF), grad_up.astype(BF)], axis=1)
-    grad_gu = tie(grad_gu, *normed_all[slots - 1 :], *attended_near[1:])
+    grad_gate_w = dot_tn(normed_two_all, grad_gu[:, :hidden_slot]).astype(BF)
+    grad_gu = tie(grad_gu, *normed_all[slots - 1 :], *attended_near[1:], grad_gate_w)
     half_tok = tok_count // 2
     cut_rows = [tok_count] + [half_tok] * 6 if slots == 4 else [tok_count] * slots
 
     def cut_product(left, right, transposed, late):
-        width = 256
+        width = 512
         depth = left.shape[1]
         right_spec = (
             pl.BlockSpec((width, depth), lambda j: (j, 0))
@@ -818,12 +821,11 @@
         )
     near = scatter_near(grad_parts)
     far = scatter_far(grad_parts, passed)
-    grad_gate_w = dot_tn(normed_two_all, grad_gu[:, :hidden_slot]).astype(BF)
+    grad_gate_w = tie(grad_gate_w, own_down, *passed)
+    own_gate = lax.psum_scatter(grad_gate_w, "seq", scatter_dimension=0, tiled=True)
+    grad_up_w = dot_tn(normed_two_all, grad_gu[:, hidden_slot:]).astype(BF)
     grad_normed_two = scatter_total(grad_parts, near, far)
-    grad_gate_w, own_down, down_parts[-1] = fence(
-        [grad_gate_w, own_down, down_parts[-1]], [grad_normed_two]
-    )
-    own_gate = lax.psum_scatter(grad_gate_w, "seq", scatter_dimension=0, tiled=True)
+    down_parts[-1] = tie(down_parts[-1], grad_normed_two)
     down_passed = scatter_pass(
         [*down_parts[:-2], tie(down_parts[-2], down_parts[-1]), down_parts[-1]]
     )
@@ -831,7 +833,7 @@
     grad_middle, grad_attended, grad_gain_two, *branch = call(
         functools.partial(mid_back_kernel, shape),
         (place, grad_normed_two, middle, cot_own, gain_two, *out_w),
-        (grad_gate_w,),
+        (grad_up_w, *down_passed),
         (
             shape_of(tok_count, model, F32),
             shape_of(tok_count, head_count * head_width, BF),
@@ -840,6 +842,7 @@
         + (shape_of(tok_count, out_slot, BF),) * slots,
     )
     branch_all = trade_slot(branch)
+    own_down_near = gather_near(tie(own_down, branch[0]))
 
     grad_query, grad_table = pl.pallas_call(
         functools.partial(attend_back_kernel, hop_count, 0),
@@ -856,12 +859,9 @@
         ),
         compiler_params=BIG,
     )(place, queries, grad_attended, *table, cosine, sine)
-    grad_table, down_parts[2], down_parts[3], *down_passed = fence(
-        [grad_table, down_parts[2], down_parts[3], *down_passed],
-        branch_all[1:],
-    )
-    down_near = scatter_near(down_parts)
-    grad_up_w = dot_tn(normed_two_all, tie(grad_gu, grad_table)[:, hidden_slot:]).astype(BF)
+    grad_table, *down_passed = fence([grad_table, *down_passed], branch_all[1:])
+    grad_up_w = tie(grad_up_w, own_gate, grad_table)
+    own_up = lax.psum_scatter(grad_up_w, "seq", scatter_dimension=0, tiled=True)
     own_grad = grad_table[WINDOW:] + kv_cot[0].astype(F32)
     for hop in range(1, hop_count + 1):
         lower = (hop_count - hop) * tok_count
@@ -872,8 +872,14 @@
     grad_key = own_grad[:, :head_width]
     grad_key = grad_key * cosine - jnp.roll(grad_key, head_width // 2, axis=1) * sine
     grad_kv = jnp.concatenate([grad_key, own_grad[:, head_width:]], axis=1).astype(BF)
-    grad_kv, own_down = fence([grad_kv, own_down], [grad_up_w])
-
+    grad_kv, down_parts[2], *own_down_near[1:] = fence(
+        [grad_kv, down_parts[2], *own_down_near[1:]], []
+    )
+    down_near = scatter_near(
+        [*down_parts[:3], tie(down_parts[3], down_parts[2]), *down_parts[4:]]
+        if slots == 4
+        else down_parts
+    )
     traded = [
         jnp.concatenate([grad_query[:, j * cols_slot : (j + 1) * cols_slot], grad_kv], axis=1)
         for j in range(slots)
@@ -889,10 +895,13 @@
     )
     gain_grads = jnp.concatenate([grad_gain_one, grad_gain_two], axis=0).astype(BF)
     gain_grads = jnp.pad(gain_grads.T, ((0, 0), (0, head_width - 2)))
-    gain_grads, down_parts[1], own_down = fence(
-        [gain_grads, down_parts[1], own_down], [grad_inputs, *traded[1:], *down_near]
-    )
-    own_down_near = gather_near(own_down)
+    late = [grad_inputs, *traded[1:], *down_near]
+    gain_grads, down_parts[1], *down_passed = fence(
+        [gain_grads, down_parts[1], *down_passed], late
+    )
+    own_down_near[1:] = fence(own_down_near[1:], [gain_grads])
+    down_far = scatter_far(down_parts, down_passed)
+    own_down_all = own_down_near + gather_far(own_down_near)
     width_all = traded[0].shape[1] + branch_all[0].shape[1] + head_width
     places = seqs // 2
 
@@ -921,27 +930,30 @@
             compiler_params=BIG,
         )(place, *normed_all, *attended_all, *traded, *branch_all, gain_grads, *late)
 
-    theirs = line_grads(places, ())
-    down_far = scatter_far(down_parts, down_passed)
+    mine = line_grads(0, ())
+    theirs = line_grads(places, (mine,))
     passed = swap(theirs, "seq", 1)
-    mine = line_grads(0, (theirs,))
-    grad_up_w = tie(grad_up_w, own_gate, grad_inputs)
-    own_up = lax.psum_scatter(grad_up_w, "seq", scatter_dimension=0, tiled=True)
-    passed = tie(passed, mine)
-    own_down_near[1:] = fence(own_down_near[1:], [passed])
-    own_down_all = own_down_near + gather_far(own_down_near)
     line = line_sums(mine, passed)
     first = line_first(line)
     down_total = scatter_total(down_parts, down_near, down_far)
     result = (middle + down_total * row_valid).astype(BF)
     second = line_second(line, first)
-    own_gate = tie(own_gate.astype(BF), own_up, result)
-    gate_all = lax.all_gather(own_gate, "slot", axis=0)
-    up_all = lax.all_gather(own_up.astype(BF), "slot", axis=0)
+    own_hidden = jnp.concatenate([own_gate, own_up], axis=1)
+    hidden_parts = lax.all_gather(own_hidden, "slot", axis=0)
     own = line_total(line, first, second)
     kv_end = cols_slot + 2 * head_width
     shared_out = jnp.concatenate([own[:, :cols_slot], own[:, kv_end:]], axis=1).astype(BF)
     shared_near = gather_near(shared_out)
+    row_tile = 32
+
+    gate_grad, up_grad = pl.pallas_call(
+        functools.partial(unshare_kernel, slots, seqs),
+        out_shape=(shape_of(rows_dev, hidden_all, F32),) * 2,
+        grid=(rows_dev // row_tile,),
+        in_specs=[pl.BlockSpec((slots, row_tile, 2 * hidden_slot), lambda r: (0, r, 0))],
+        out_specs=(pl.BlockSpec((row_tile, hidden_all), lambda r: (r, 0)),) * 2,
+        compiler_params=BIG,
+    )(hidden_parts)
     all_own = jnp.concatenate(shared_near + gather_far(shared_near), axis=0)
     all_own = all_own.reshape(slots, rows_dev, -1)
     all_own = jnp.stack(
@@ -961,25 +973,6 @@
     out_grad_w = slot_columns(all_own[:, :, cols_slot : cols_slot + out_slot])
     gain_total = jnp.sum(all_own[:, :, cols_slot + out_slot :][:, :, :2].astype(F32), axis=0)
     down_grad = by_slot(own_down_all).reshape(slots * piece, model).astype(F32)
-    row_tile = 32
-
-    def whole_rows(parts):
-        return pl.pallas_call(
-            functools.partial(unshare_kernel, slots, seqs),
-            out_shape=shape_of(rows_dev, hidden_all, F32),
-            grid_spec=pltpu.PrefetchScalarGridSpec(
-                num_scalar_prefetch=1,
-                grid=(rows_dev // row_tile,),
-                in_specs=[
-                    pl.BlockSpec((slots, row_tile, hidden_slot), lambda r, place: (0, r, 0))
-                ],
-                out_specs=pl.BlockSpec((row_tile, hidden_all), lambda r, place: (r, 0)),
-            ),
-            compiler_params=BIG,
-        )(place, parts)
-
-    gate_grad = whole_rows(gate_all)
-    up_grad = whole_rows(up_all)
     return (
         result[None],
         shared[None],

time: 660 us -> 630 us (0.955)
  local copies, waits for them, and re-layouts: 81.1 us -> 71.1 us
  waiting for transfers between devices: 225 us -> 215 us
  Pallas kernels: 158 us -> 150 us
    reduce_scatter x1, waiting for transfers between devices: 14.9 us -> 0.02 us  [shards(): own_up = lax.psum_scatter(grad_up_w, 'seq', scatter_dimension=0, tiled=True)]
    unnamed x200 -> x212, local copies, waits for them, and re-layouts: 45.9 us -> 37.2 us
    pallas_call x2 -> x1, Pallas kernels: 15.7 us -> 9.19 us  [shards(): pl.pallas_call(functools.partial(unshare_kernel, slots, seqs), out_shape=...]
  transfers between devices with their start and end apart: 82 -> 81, of which waited for: 35 -> 36; matrix products, arithmetic and copies ran while one was open for 20% -> 19% of each run, Pallas kernels for 23% -> 23%
where the time goes in v3:
time: 630 us; the launch traced here: 619 us
  waiting for transfers between devices  215 us (34%)
  Pallas kernels  150 us (24%)
  starting transfers between devices  87.3 us (14%)
  local copies, waits for them, and re-layouts  71.1 us (11%)
  matrix products  41.1 us (7%)
  other arithmetic  37.9 us (6%)
  between operations  16.6 us (3%)
    ppermute x71, waiting for transfers between devices, swap(): lax.ppermute(block, axis, [(i, i ^ mask) for i in range(lax.axis_size(axi...  196 us
    ppermute x71, starting transfers between devices, swap(): lax.ppermute(block, axis, [(i, i ^ mask) for i in range(lax.axis_size(axi...  76.7 us
    pallas_call x5, Pallas kernels, call(): pl.pallas_call(run, out_shape=out_shape, in_specs=[SMEM] + [VMEM] * (coun...  40.1 us
    unnamed x212, local copies, waits for them, and re-layouts  37.2 us
    dot_general x3, matrix products, dot_tn(): lax.dot_general(left, right, (((0,), (0,)), ((), ())), preferred_element_...  30.4 us
    pallas_call x2, Pallas kernels, cut_product(): pl.pallas_call(functools.partial(rows_kernel, transposed, len(late)), out...  27.6 us
    pallas_call x1, Pallas kernels, shards(): pl.pallas_call(functools.partial(attend_back_kernel, hop_count, 0), out_s...  20.8 us
    pallas_call x1, Pallas kernels, shards(): pl.pallas_call(functools.partial(gate_kernel, len(normed_two_parts)), out...  19.1 us
  transfers between devices with their start and end apart: 81, of which 36 were waited for; matrix products, arithmetic and copies ran while one was open for 19% of the time, Pallas kernels for 23%

profile of v3, /device:TPU:10, one launch (start us, length us, event | category | flops | bytes accessed | tf_op | source)
XLA Modules:
  0.0 619.0 jit_solution(8818670273554234402)
XLA Ops:
  8.1 2.8 constant_dynamic-update-slice_fusion.4
  17.1 2.5 collective-permute-start
  20.2 4.5 shard_map.220.refs_5_.refs_3_
  27.3 8.9 %collective-permute-done.3.refs_4_ = bf16[256,2048]{1,0:T(8,128)(2,1)} collective-permute-done((bf16[256,2048]{1,0:T(8,128)(2,1)}, bf16[256,2048]{1,0:T(8,128)(2,1)}, u32[]{:S(2)}, u32[]{:S(2)}) %collective-permute-start.3) | collective-permute-done | bytes 1048608 | tf_op jit(solution)/shard_map/ppermute | solution.py:21
  36.2 2.3 copy.102.refs_1_
  38.5 2.3 copy.101.refs_0_
  48.8 2.5 collective-permute-start.5
  51.3 3.1 collective-permute-done.4.refs_4_
  56.4 3.7 collective-permute-done.6.refs_5_
  64.8 6.0 collective-permute-start.13
  70.8 8.1 %collective-permute-done.13.refs_4_ = bf16[256,512]{1,0:T(8,128)(2,1)S(1)} collective-permute-done((bf16[256,512]{1,0:T(8,128)(2,1)}, bf16[256,512]{1,0:T(8,128)(2,1)S(1)}, u32[]{:S(2)}, u32[]{:S(2)}) %collective-permute-start.13) | collective-permute-done | bytes 262176 | tf_op jit(solution)/shard_map/ppermute | solution.py:21
  79.0 9.5 %collective-permute-done.11.refs_1_ = bf16[1024,512]{1,0:T(8,128)(2,1)S(1)} collective-permute-done((bf16[1024,512]{1,0:T(8,128)(2,1)}, bf16[1024,512]{1,0:T(8,128)(2,1)S(1)}, u32[]{:S(2)}, u32[]{:S(2)}) %collective-permute-start.11) | collective-permute-done | bytes 1048608 | tf_op jit(solution)/shard_map/ppermute | solution.py:21
  95.2 2.1 pad_maximum_fusion.7.refs_2_
  97.3 10.0 %collective-permute-done.15.refs_1_ = bf16[512,512]{1,0:T(8,128)(2,1)S(1)} collective-permute-done((bf16[512,512]{1,0:T(8,128)(2,1)S(1)}, bf16[512,512]{1,0:T(8,128)(2,1)S(1)}, u32[]{:S(2)}, u32[]{:S(2)}) %collective-permute-start.15) | collective-permute-done | bytes 524320 | tf_op jit(solution)/shard_map/ppermute | solution.py:21
  117.3 1.9 slice.252
  120.8 8.3 %shard_map.226 = (bf16[256,2048]{1,0:T(8,128)(2,1)}, bf16[256,2048]{1,0:T(8,128)(2,1)}, bf16[256,256]{1,0:T(8,128)(2,1)}) custom-call(s32[3]{0:T(128)} %pad_add_fusion.refs_0_.place, bf16[256,2048]{1,0:T(8,128)(2,1)} %bitcast.47, f32[1,2048]{1,0:T(1,128)} %bitcast.67, f32[256,1]{1,0:T(8,128)} %fusion.15.refs_3_, ...), custom_call_target="tpu_custom_call" | custom-call | tf_op jit(solution)/shard_map/pallas_call | solution.py:556
  129.2 2.0 collective-permute-start.21
  131.2 3.9 collective-permute-start.20
  135.0 8.0 %collective-permute-done.21.refs_3_.refs_1_ = bf16[256,256]{1,0:T(8,128)(2,1)S(1)} collective-permute-done((bf16[256,256]{1,0:T(8,128)(2,1)}, bf16[256,256]{1,0:T(8,128)(2,1)S(1)}, u32[]{:S(2)}, u32[]{:S(2)}) %collective-permute-start.21) | collective-permute-done | bytes 131104 | tf_op jit(solution)/shard_map/ppermute | solution.py:95
  143.0 2.6 collective-permute-done.20.refs_2_.refs_0_
  148.6 3.5 collective-permute-start.27
  156.4 15.6 %shard_map.228.refs_4_.refs_1_ = bf16[256,2048]{1,0:T(8,128)(2,1)} custom-call(s32[3]{0:T(128)} %pad_add_fusion.refs_0_.place, bf16[256,2048]{1,0:T(8,128)(2,1)} %get-tuple-element.107.query_ref, bf16[256,256]{1,0:T(8,128)(2,1)} %copy-done.83, bf16[256,256]{1,0:T(8,128)(2,1)} %copy-done.82, bf16[256,256]{1,0:T(8,128)(2,1)} %get-tuple-element.108.refs_2_, ...), custom_call_target="tpu_custom_call" | custom-call | tf_op jit(solution)/shard_map/pallas_call | solution.py:713
  178.0 8.4 %shard_map.230 = (f32[256,2048]{1,0:T(8,128)}, bf16[256,2048]{1,0:T(8,128)(2,1)}, bf16[256,2048]{1,0:T(8,128)(2,1)}) custom-call(s32[3]{0:T(128)} %pad_add_fusion.refs_0_.place, bf16[256,2048]{1,0:T(8,128)(2,1)} %shard_map.228.refs_4_.refs_1_, bf16[256,2048]{1,0:T(8,128)(2,1)} %bitcast.48, f32[1,2048]{1,0:T(1,128)} %bitcast.69, ...), custom_call_target="tpu_custom_call" | custom-call | tf_op jit(solution)/shard_map/pallas_call | solution.py:556
  192.4 19.6 %collective-permute-done.32.refs_1_ = bf16[256,2048]{1,0:T(8,128)(2,1)} collective-permute-done((bf16[256,2048]{1,0:T(8,128)(2,1)}, bf16[256,2048]{1,0:T(8,128)(2,1)}, u32[]{:S(2)}, u32[]{:S(2)}) %collective-permute-start.32) | collective-permute-done | bytes 1048608 | tf_op jit(solution)/shard_map/ppermute | solution.py:21
  216.8 11.7 %collective-permute-done.34.refs_4_.refs_2_ = bf16[128,2048]{1,0:T(8,128)(2,1)S(1)} collective-permute-done((bf16[128,2048]{1,0:T(8,128)(2,1)S(1)}, bf16[128,2048]{1,0:T(8,128)(2,1)S(1)}, u32[]{:S(2)}, u32[]{:S(2)}) %collective-permute-start.34) | collective-permute-done | bytes 524320 | tf_op jit(solution)/shard_map/ppermute | solution.py:21
  231.7 19.1 %shard_map.232 = (bf16[1024,2048]{1,0:T(8,128)(2,1)}, bf16[1024,1408]{1,0:T(8,128)(2,1)}, bf16[1024,1408]{1,0:T(8,128)(2,1)}, bf16[1024,1408]{1,0:T(8,128)(2,1)}) custom-call(bf16[256,2048]{1,0:T(8,128)(2,1)} %get-tuple-element.115.refs_0_, bf16[256,2048]{1,0:T(8,128)(2,1)} %get-tuple-element.116.refs_1_, bf16[256,2048]{1,0:T(8,128)(2,1)} %get-tuple-element.117.refs_2_, ...), custom_call_target="tpu_custom_call" | custom-call | tf_op jit(solution)/shard_map/pallas_call | solution.py:754
  250.8 2.1 collective-permute-done.36.refs_2_.refs_1_
  254.9 1.8 copy-done.3
  256.7 10.7 %convolution_convert_fusion = bf16[1408,2048]{1,0:T(8,128)(2,1)} fusion(bf16[1024,1408]{1,0:T(8,128)(2,1)S(1)} %copy-done.3, bf16[1024,2048]{1,0:T(8,128)(2,1)} %shard_map.234.refs_3_), kind=kOutput, calls=%fused_computation.3 | convolution fusion | flops 5908463616 | bytes 12845056 | tf_op jit(solution)/shard_map/dot_general | solution.py:115
  269.8 1.9 slice.208
  271.7 1.9 slice.209
  275.5 10.7 %fusion.31 = f32[1024,1408]{1,0:T(8,128)S(1)} fusion(bf16[1024,2048]{1,0:T(8,128)(2,1)} %shard_map.234.refs_3_, bf16[1408,2048]{1,0:T(8,128)(2,1)} %all-gather.7.cloned.1.call-done.right_ref), kind=kOutput, calls=%fused_computation.114 | convolution fusion | flops 5905580032 | bytes 15728640 | tf_op jit(solution)/shard_map/dot_general | solution.py:111
  286.3 2.9 fusion.5
  289.2 8.7 %convolution_convert_fusion.2.refs_5_.refs_0_ = bf16[2048,1408]{1,0:T(8,128)(2,1)} fusion(bf16[1024,2048]{1,0:T(8,128)(2,1)S(1)} %copy-done.97, bf16[1024,1408]{1,0:T(8,128)(2,1)S(1)} %get-tuple-element.184), kind=kOutput, calls=%fused_computation.5 | convolution fusion | flops 5908463616 | bytes 12845056 | tf_op jit(solution)/shard_map/dot_general | solution.py:115
  297.9 2.9 pad_maximum_fusion.refs_0_
  308.9 17.2 %shard_map.237 = (bf16[256,2048]{1,0:T(8,128)(2,1)}, bf16[128,2048]{1,0:T(8,128)(2,1)}, bf16[128,2048]{1,0:T(8,128)(2,1)}, bf16[128,2048]{1,0:T(8,128)(2,1)}, bf...) custom-call(bf16[1024,2816]{1,0:T(8,128)(2,1)} %shard_map.236.left_ref.refs_2_.refs_4_, ...), custom_call_target="tpu_custom_call" | custom-call | tf_op jit(solution)/shard_map/pallas_call | solution.py:798
  329.1 10.4 %shard_map.239 = (bf16[256,2048]{1,0:T(8,128)(2,1)}, bf16[128,2048]{1,0:T(8,128)(2,1)}, bf16[128,2048]{1,0:T(8,128)(2,1)}, bf16[128,2048]{1,0:T(8,128)(2,1)}, bf...) custom-call(bf16[1024,1408]{1,0:T(8,128)(2,1)} %shard_map.238.left_ref, ...), custom_call_target="tpu_custom_call" | custom-call | tf_op jit(solution)/shard_map/pallas_call | solution.py:798
  345.4 10.6 %collective-permute-done.46 = bf16[128,2048]{1,0:T(8,128)(2,1)S(1)} collective-permute-done((bf16[128,2048]{1,0:T(8,128)(2,1)}, bf16[128,2048]{1,0:T(8,128)(2,1)S(1)}, u32[]{:S(2)}, u32[]{:S(2)}) %collective-permute-start.46) | collective-permute-done | bytes 524320 | tf_op jit(solution)/shard_map/ppermute | solution.py:21
  357.2 6.7 %collective-permute-done.48 = bf16[128,2048]{1,0:T(8,128)(2,1)S(1)} collective-permute-done((bf16[128,2048]{1,0:T(8,128)(2,1)S(1)}, bf16[128,2048]{1,0:T(8,128)(2,1)S(1)}, u32[]{:S(2)}, u32[]{:S(2)}) %collective-permute-start.48) | collective-permute-done | bytes 524320 | tf_op jit(solution)/shard_map/ppermute | solution.py:21
  364.0 1.8 convert_add_fusion.refs_1_
  367.9 11.0 %convolution_convert_fusion.1.refs_15_.refs_0_ = bf16[2048,1408]{1,0:T(8,128)(2,1)} fusion(bf16[1024,2048]{1,0:T(8,128)(2,1)} %get-tuple-element.128, bf16[1024,2816]{1,0:T(8,128)(2,1)} %get-tuple-element.145), kind=kOutput, calls=%fused_computation.4 | convolution fusion | flops 5908463616 | bytes 12845056 | tf_op jit(solution)/shard_map/dot_general | solution.py:115
  379.9 9.4 %shard_map.245 = (f32[256,2048]{1,0:T(8,128)}, bf16[256,2048]{1,0:T(8,128)(2,1)}, f32[1,2048]{1,0:T(1,128)}, bf16[256,512]{1,0:T(8,128)(2,1)}, bf16[256,512]{1,0...) custom-call(s32[3]{0:T(128)} %pad_add_fusion.refs_0_.place, f32[256,2048]{1,0:T(8,128)} %convert_add_fusion.refs_1_, ...), custom_call_target="tpu_custom_call" | custom-call | tf_op jit(solution)/shard_map/pallas_call | solution.py:556
  392.9 20.8 %shard_map.246 = (bf16[256,2048]{1,0:T(8,128)(2,1)}, f32[768,256]{1,0:T(8,128)}) custom-call(s32[3]{0:T(128)} %pad_add_fusion.refs_0_.place, bf16[256,2048]{1,0:T(8,128)(2,1)} %get-tuple-element.107.query_ref, bf16[256,2048]{1,0:T(8,128)(2,1)} %get-tuple-element.148.grad_ref, bf16[256,256]{1,0:T(8,128)(2,1)} %copy-done.83, bf16[256,256]{1,0:T(8,128)(2,1)} %copy-done.82, ...), custom_call_target="tpu_custom_call" | custom-call | tf_op jit(solution)/shard_map/pallas_call | solution.py:847
  415.8 1.9 collective-permute-start.54
  417.7 2.2 collective-permute-start.55
  422.8 7.8 %collective-permute-done.55 = bf16[256,256]{1,0:T(8,128)(2,1)S(1)} collective-permute-done((bf16[256,256]{1,0:T(8,128)(2,1)S(1)}, bf16[256,256]{1,0:T(8,128)(2,1)S(1)}, u32[]{:S(2)}, u32[]{:S(2)}) %collective-permute-start.55) | collective-permute-done | bytes 131104 | tf_op jit(solution)/shard_map/ppermute | solution.py:95
  431.7 7.9 %collective-permute-done.57.refs_3_ = bf16[176,2048]{1,0:T(8,128)(2,1)S(1)} collective-permute-done((bf16[176,2048]{1,0:T(8,128)(2,1)}, bf16[176,2048]{1,0:T(8,128)(2,1)S(1)}, u32[]{:S(2)}, u32[]{:S(2)}) %collective-permute-start.57) | collective-permute-done | bytes 720928 | tf_op jit(solution)/shard_map/ppermute | solution.py:21
  443.7 2.2 pad_maximum_fusion.8
  449.5 9.4 %shard_map.250 = (bf16[256,2048]{1,0:T(8,128)(2,1)}, f32[1,2048]{1,0:T(1,128)}) custom-call(s32[3]{0:T(128)} %pad_add_fusion.refs_0_.place, bf16[256,2048]{1,0:T(8,128)(2,1)} %get-tuple-element.149.refs_1_, bf16[256,256]{1,0:T(8,128)(2,1)} %get-tuple-element.157.refs_2_, bf16[256,2048]{1,0:T(8,128)(2,1)} %bitcast.49, ...), custom_call_target="tpu_custom_call" | custom-call | tf_op jit(solution)/shard_map/pallas_call | solution.py:556
  460.9 4.4 collective-permute-done.60.refs_7_.refs_13_
  465.3 6.3 %collective-permute-done.58.refs_5_.refs_11_ = bf16[256,768]{1,0:T(8,128)(2,1)S(1)} collective-permute-done((bf16[256,768]{1,0:T(8,128)(2,1)}, bf16[256,768]{1,0:T(8,128)(2,1)S(1)}, u32[]{:S(2)}, u32[]{:S(2)}) %collective-permute-start.58) | collective-permute-done | bytes 393248 | tf_op jit(solution)/shard_map/ppermute | solution.py:21
  473.8 8.8 %shard_map.253.refs_19_ = bf16[1024,1408]{1,0:T(8,128)(2,1)} custom-call(s32[3]{0:T(128)} %pad_add_fusion.refs_0_.place, bf16[256,2048]{1,0:T(8,128)(2,1)} %shard_map.233.refs_0_, bf16[256,2048]{1,0:T(8,128)(2,1)} %get-tuple-element.125.refs_1_, bf16[256,2048]{1,0:T(8,128)(2,1)} %get-tuple-element.126.refs_2_, bf16[128,2048]{1,0:T(8,128)(2,1)} %copy-done.34, ...), custom_call_target="tpu_custom_call" | custom-call | tf_op jit(solution)/shard_map/pallas_call | solution.py:915
  482.6 8.8 %shard_map.254 = bf16[1024,1408]{1,0:T(8,128)(2,1)} custom-call(s32[3]{0:T(128)} %pad_add_fusion.refs_0_.place, bf16[256,2048]{1,0:T(8,128)(2,1)} %shard_map.233.refs_0_, bf16[256,2048]{1,0:T(8,128)(2,1)} %get-tuple-element.125.refs_1_, bf16[256,2048]{1,0:T(8,128)(2,1)} %get-tuple-element.126.refs_2_, bf16[128,2048]{1,0:T(8,128)(2,1)} %copy-done.34, ...), custom_call_target="tpu_custom_call" | custom-call | tf_op jit(solution)/shard_map/pallas_call | solution.py:915
  491.6 2.4 pad_maximum_fusion.2
  504.5 1.8 add_convert_fusion.4
  506.5 2.9 collective-permute-done.73
  509.8 15.7 %collective-permute-done.67 = bf16[256,1408]{1,0:T(8,128)(2,1)S(1)} collective-permute-done((bf16[256,1408]{1,0:T(8,128)(2,1)S(1)}, bf16[256,1408]{1,0:T(8,128)(2,1)S(1)}, u32[]{:S(2)}, u32[]{:S(2)}) %collective-permute-start.67) | collective-permute-done | bytes 720928 | tf_op jit(solution)/shard_map/ppermute | solution.py:21
  526.9 4.7 collective-permute-start.68
  532.0 3.5 bitcast_convert_fusion
  535.5 5.5 collective-permute-done.66
  541.0 19.3 %collective-permute-done.68 = bf16[256,1408]{1,0:T(8,128)(2,1)S(1)} collective-permute-done((bf16[256,1408]{1,0:T(8,128)(2,1)S(1)}, bf16[256,1408]{1,0:T(8,128)(2,1)S(1)}, u32[]{:S(2)}, u32[]{:S(2)}) %collective-permute-start.68) | collective-permute-done | bytes 720928 | tf_op jit(solution)/shard_map/ppermute | solution.py:21
  566.4 23.3 %collective-permute-done.69 = bf16[256,1152]{1,0:T(8,128)(2,1)S(1)} collective-permute-done((bf16[256,1152]{1,0:T(8,128)(2,1)S(1)}, bf16[256,1152]{1,0:T(8,128)(2,1)S(1)}, u32[]{:S(2)}, u32[]{:S(2)}) %collective-permute-start.69) | collective-permute-done | bytes 589856 | tf_op jit(solution)/shard_map/ppermute | solution.py:21
  592.3 4.8 collective-permute-done.71
  602.5 9.2 %shard_map.257 = (f32[256,5632]{1,0:T(8,128)}, f32[256,5632]{1,0:T(8,128)}) custom-call(bf16[4,256,2816]{2,1,0:T(8,128)(2,1)} %bitcast.50), custom_call_target="tpu_custom_call" | custom-call | tf_op jit(solution)/shard_map/pallas_call | solution.py:949
  (449 shorter events, 145.0 us)
Async XLA Ops:
  7.2 224.4 %all-gather.5.cloned.1.call-start = ((), (), s32[]{:S(2)}) async-start(), calls=%async_computation.3 | async-start | bytes 12976128 | tf_op jit(solution)/shard_map/all_gather | solution.py:642
  10.9 25.2 %collective-permute-start.3 = (bf16[256,2048]{1,0:T(8,128)(2,1)}, bf16[256,2048]{1,0:T(8,128)(2,1)}, u32[]{:S(2)}, u32[]{:S(2)}) collective-permute-start(bf16[256,2048]{1,0:T(8,128)(2,1)} %get-tuple-element.183), channel_id=1, source_target_pairs={{0,16},{8,24},{16,0},{24,8},{1,17},{9,25},{17,1},{25,9},{2,18},{10... | collective-permute-start | bytes 3145736 | tf_op jit(solution)/shard_map/ppermute | solution.py:21
  12.5 26.0 %collective-permute-start.2 = (bf16[256,2048]{1,0:T(8,128)(2,1)}, bf16[256,2048]{1,0:T(8,128)(2,1)}, u32[]{:S(2)}, u32[]{:S(2)}) collective-permute-start(bf16[256,2048]{1,0:T(8,128)(2,1)} %get-tuple-element.183), channel_id=1, source_target_pairs={{0,8},{8,0},{16,24},{24,16},{1,9},{9,1},{17,25},{25,17},{2,10},{10... | collective-permute-start | bytes 3145736 | tf_op jit(solution)/shard_map/ppermute | solution.py:21
  15.5 25.3 %collective-permute-start.1 = (bf16[272,768]{1,0:T(8,128)(2,1)}, bf16[272,768]{1,0:T(8,128)(2,1)S(1)}, u32[]{:S(2)}, u32[]{:S(2)}) collective-permute-start(bf16[272,768]{1,0:T(8,128)(2,1)} %pad_maximum_fusion.14), channel_id=1, source_target_pairs={{0,6},{1,7},{2,4},{3,5},{4,2},{5,3},{6,0},{7,1},{8,14},{9,15},{10,... | collective-permute-start | bytes 1253384 | tf_op jit(solution)/shard_map/ppermute | solution.py:21
  17.1 23.7 %collective-permute-start = (bf16[272,768]{1,0:T(8,128)(2,1)}, bf16[272,768]{1,0:T(8,128)(2,1)}, u32[]{:S(2)}, u32[]{:S(2)}) collective-permute-start(bf16[272,768]{1,0:T(8,128)(2,1)} %pad_maximum_fusion.14), channel_id=1, source_target_pairs={{0,2},{1,3},{2,0},{3,1},{4,6},{5,7},{6,4},{7,5},{8,10},{9,11},{10,... | collective-permute-start | bytes 1253384 | tf_op jit(solution)/shard_map/ppermute | solution.py:21
  43.1 16.9 %collective-permute-start.8 = (bf16[128,2048]{1,0:T(8,128)(2,1)S(1)}, bf16[128,2048]{1,0:T(8,128)(2,1)S(1)}, u32[]{:S(2)}, u32[]{:S(2)}) collective-permute-start(bf16[128,2048]{1,0:T(8,128)(2,1)S(1)} %slice.195), channel_id=1, source_target_pairs={{0,8},{8,0},{16,24},{24,16},{1,9},{9,1},{17,25},{25,17},{2,10},{10... | collective-permute-start | bytes 1572872 | tf_op jit(solution)/shard_map/ppermute | solution.py:21
  43.7 16.3 %collective-permute-start.7 = (bf16[128,2048]{1,0:T(8,128)(2,1)S(1)}, bf16[128,2048]{1,0:T(8,128)(2,1)S(1)}, u32[]{:S(2)}, u32[]{:S(2)}) collective-permute-start(bf16[128,2048]{1,0:T(8,128)(2,1)S(1)} %slice.194), channel_id=1, source_target_pairs={{0,16},{8,24},{16,0},{24,8},{1,17},{9,25},{17,1},{25,9},{2,18},{10... | collective-permute-start | bytes 1572872 | tf_op jit(solution)/shard_map/ppermute | solution.py:21
  61.8 213.7 %all-gather.7.cloned.1.call-start = ((), (), s32[]{:S(2)}) async-start(), calls=%async_computation.4 | async-start | bytes 6488064 | tf_op jit(solution)/shard_map/all_gather | solution.py:643
  62.6 277.9 %reduce-scatter.4.cloned.1.call-start = ((), (), s32[]{:S(2)}) async-start(), calls=%async_computation.5 | async-start | bytes 6488064 | tf_op jit(solution)/shard_map/reduce_scatter | solution.py:775
  62.6 16.3 %collective-permute-start.12 = (bf16[1024,512]{1,0:T(8,128)(2,1)}, bf16[1024,512]{1,0:T(8,128)(2,1)S(1)}, u32[]{:S(2)}, u32[]{:S(2)}) collective-permute-start(bf16[1024,512]{1,0:T(8,128)(2,1)} %get-tuple-element.101.refs_6_), channel_id=1, source_target_pairs={{0,1},{1,0},{2,3},{3,2},{4,5},{5,4},{6,7},{7,6},{8,9},{9,8},{10,11... | collective-permute-start | bytes 3145736 | tf_op jit(solution)/shard_map/ppermute | solution.py:21
  62.7 25.8 %collective-permute-start.11 = (bf16[1024,512]{1,0:T(8,128)(2,1)}, bf16[1024,512]{1,0:T(8,128)(2,1)S(1)}, u32[]{:S(2)}, u32[]{:S(2)}) collective-permute-start(bf16[1024,512]{1,0:T(8,128)(2,1)} %get-tuple-element.101.refs_6_), channel_id=1, source_target_pairs={{0,16},{8,24},{16,0},{24,8},{1,17},{9,25},{17,1},{25,9},{2,18},{10... | collective-permute-start | bytes 3145736 | tf_op jit(solution)/shard_map/ppermute | solution.py:21
  64.3 25.4 %collective-permute-start.10 = (bf16[1024,512]{1,0:T(8,128)(2,1)}, bf16[1024,512]{1,0:T(8,128)(2,1)S(1)}, u32[]{:S(2)}, u32[]{:S(2)}) collective-permute-start(bf16[1024,512]{1,0:T(8,128)(2,1)} %get-tuple-element.101.refs_6_), channel_id=1, source_target_pairs={{0,8},{8,0},{16,24},{24,16},{1,9},{9,1},{17,25},{25,17},{2,10},{10... | collective-permute-start | bytes 3145736 | tf_op jit(solution)/shard_map/ppermute | solution.py:21
  64.8 14.1 %collective-permute-start.9 = (bf16[1088,256]{1,0:T(8,128)(2,1)}, bf16[1088,256]{1,0:T(8,128)(2,1)S(1)}, u32[]{:S(2)}, u32[]{:S(2)}) collective-permute-start(bf16[1088,256]{1,0:T(8,128)(2,1)} %get-tuple-element.100), channel_id=1, source_target_pairs={{0,1},{1,0},{2,3},{3,2},{4,5},{5,4},{6,7},{7,6},{8,9},{9,8},{10,11... | collective-permute-start | bytes 1671176 | tf_op jit(solution)/shard_map/ppermute | solution.py:21
  64.8 14.1 %collective-permute-start.13 = (bf16[256,512]{1,0:T(8,128)(2,1)}, bf16[256,512]{1,0:T(8,128)(2,1)S(1)}, u32[]{:S(2)}, u32[]{:S(2)}) collective-permute-start(bf16[256,512]{1,0:T(8,128)(2,1)} %get-tuple-element.102), channel_id=1, source_target_pairs={{0,2},{1,3},{2,0},{3,1},{4,6},{5,7},{6,4},{7,5},{8,10},{9,11},{10,... | collective-permute-start | bytes 786440 | tf_op jit(solution)/shard_map/ppermute | solution.py:21
  90.7 16.9 %collective-permute-start.16 = (bf16[1024,512]{1,0:T(8,128)(2,1)}, bf16[1024,512]{1,0:T(8,128)(2,1)S(1)}, u32[]{:S(2)}, u32[]{:S(2)}) collective-permute-start(bf16[1024,512]{1,0:T(8,128)(2,1)} %get-tuple-element.103.refs_7_), channel_id=1, source_target_pairs={{0,1},{1,0},{2,3},{3,2},{4,5},{5,4},{6,7},{7,6},{8,9},{9,8},{10,11... | collective-permute-start | bytes 3145736 | tf_op jit(solution)/shard_map/ppermute | solution.py:21
  90.7 17.7 %collective-permute-start.17 = (bf16[1024,512]{1,0:T(8,128)(2,1)}, bf16[1024,512]{1,0:T(8,128)(2,1)S(1)}, u32[]{:S(2)}, u32[]{:S(2)}) collective-permute-start(bf16[1024,512]{1,0:T(8,128)(2,1)} %get-tuple-element.104.refs_8_), channel_id=1, source_target_pairs={{0,1},{1,0},{2,3},{3,2},{4,5},{5,4},{6,7},{7,6},{8,9},{9,8},{10,11... | collective-permute-start | bytes 3145736 | tf_op jit(solution)/shard_map/ppermute | solution.py:21
  93.4 13.9 %collective-permute-start.15 = (bf16[512,512]{1,0:T(8,128)(2,1)S(1)}, bf16[512,512]{1,0:T(8,128)(2,1)S(1)}, u32[]{:S(2)}, u32[]{:S(2)}) collective-permute-start(bf16[512,512]{1,0:T(8,128)(2,1)S(1)} %slice.200), channel_id=1, source_target_pairs={{0,8},{8,0},{16,24},{24,16},{1,9},{9,1},{17,25},{25,17},{2,10},{10... | collective-permute-start | bytes 1572872 | tf_op jit(solution)/shard_map/ppermute | solution.py:21
  94.0 13.6 %collective-permute-start.14 = (bf16[512,512]{1,0:T(8,128)(2,1)S(1)}, bf16[512,512]{1,0:T(8,128)(2,1)S(1)}, u32[]{:S(2)}, u32[]{:S(2)}) collective-permute-start(bf16[512,512]{1,0:T(8,128)(2,1)S(1)} %slice.199), channel_id=1, source_target_pairs={{0,16},{8,24},{16,0},{24,8},{1,17},{9,25},{17,1},{25,9},{2,18},{10... | collective-permute-start | bytes 1572872 | tf_op jit(solution)/shard_map/ppermute | solution.py:21
  110.4 35.3 %collective-permute-start.24 = (bf16[1024,512]{1,0:T(8,128)(2,1)}, bf16[1024,512]{1,0:T(8,128)(2,1)S(1)}, u32[]{:S(2)}, u32[]{:S(2)}) collective-permute-start(bf16[1024,512]{1,0:T(8,128)(2,1)} %get-tuple-element.109.refs_4_.refs_5_), channel_id=1, source_target_pairs={{0,1},{1,0},{2,3},{3,2},{4,5},{5,4},{6,7},{7,6},{8,9},{9,8},{10,11... | collective-permute-start | bytes 3145736 | tf_op jit(solution)/shard_map/ppermute | solution.py:21
  110.4 35.3 %collective-permute-start.23 = (bf16[1024,512]{1,0:T(8,128)(2,1)}, bf16[1024,512]{1,0:T(8,128)(2,1)S(1)}, u32[]{:S(2)}, u32[]{:S(2)}) collective-permute-start(bf16[1024,512]{1,0:T(8,128)(2,1)} %get-tuple-element.109.refs_4_.refs_5_), channel_id=1, source_target_pairs={{0,16},{8,24},{16,0},{24,8},{1,17},{9,25},{17,1},{25,9},{2,18},{10... | collective-permute-start | bytes 3145736 | tf_op jit(solution)/shard_map/ppermute | solution.py:21
  111.6 35.0 %collective-permute-start.22 = (bf16[1024,512]{1,0:T(8,128)(2,1)}, bf16[1024,512]{1,0:T(8,128)(2,1)S(1)}, u32[]{:S(2)}, u32[]{:S(2)}) collective-permute-start(bf16[1024,512]{1,0:T(8,128)(2,1)} %get-tuple-element.109.refs_4_.refs_5_), channel_id=1, source_target_pairs={{0,8},{8,0},{16,24},{24,16},{1,9},{9,1},{17,25},{25,17},{2,10},{10... | collective-permute-start | bytes 3145736 | tf_op jit(solution)/shard_map/ppermute | solution.py:21
  129.2 13.8 %collective-permute-start.21 = (bf16[256,256]{1,0:T(8,128)(2,1)}, bf16[256,256]{1,0:T(8,128)(2,1)S(1)}, u32[]{:S(2)}, u32[]{:S(2)}) collective-permute-start(bf16[256,256]{1,0:T(8,128)(2,1)} %get-tuple-element.108.refs_2_), channel_id=1, source_target_pairs={{0,1},{1,2},{2,3},{3,4},{4,5},{5,6},{6,7},{8,9},{9,10},{10,11},{11... | collective-permute-start | bytes 393224 | tf_op jit(solution)/shard_map/ppermute | solution.py:95
  131.2 14.5 %collective-permute-start.20 = (bf16[256,256]{1,0:T(8,128)(2,1)}, bf16[256,256]{1,0:T(8,128)(2,1)S(1)}, u32[]{:S(2)}, u32[]{:S(2)}) collective-permute-start(bf16[256,256]{1,0:T(8,128)(2,1)} %get-tuple-element.108.refs_2_), channel_id=1, source_target_pairs={{0,2},{1,3},{2,4},{3,5},{4,6},{5,7},{8,10},{9,11},{10,12},{11,13},... | collective-permute-start | bytes 393224 | tf_op jit(solution)/shard_map/ppermute | solution.py:95
  148.6 23.4 %collective-permute-start.27 = (bf16[1024,512]{1,0:T(8,128)(2,1)}, bf16[1024,512]{1,0:T(8,128)(2,1)S(1)}, u32[]{:S(2)}, u32[]{:S(2)}) collective-permute-start(bf16[1024,512]{1,0:T(8,128)(2,1)} %get-tuple-element.110.refs_3_.refs_5_.refs_6_), channel_id=1, source_target_pairs={{0,1},{1,0},{2,3},{3,2},{4,5},{5,4},{6,7},{7,6},{8,9},{9,8},{10,11... | collective-permute-start | bytes 3145736 | tf_op jit(solution)/shard_map/ppermute | solution.py:21
  152.1 19.9 %collective-permute-start.28 = (bf16[1024,512]{1,0:T(8,128)(2,1)}, bf16[1024,512]{1,0:T(8,128)(2,1)S(1)}, u32[]{:S(2)}, u32[]{:S(2)}) collective-permute-start(bf16[1024,512]{1,0:T(8,128)(2,1)} %get-tuple-element.111.refs_4_.refs_6_.refs_7_), channel_id=1, source_target_pairs={{0,1},{1,0},{2,3},{3,2},{4,5},{5,4},{6,7},{7,6},{8,9},{9,8},{10,11... | collective-permute-start | bytes 3145736 | tf_op jit(solution)/shard_map/ppermute | solution.py:21
  154.3 17.7 %collective-permute-start.26 = (bf16[512,512]{1,0:T(8,128)(2,1)S(1)}, bf16[512,512]{1,0:T(8,128)(2,1)S(1)}, u32[]{:S(2)}, u32[]{:S(2)}) collective-permute-start(bf16[512,512]{1,0:T(8,128)(2,1)S(1)} %slice.205), channel_id=1, source_target_pairs={{0,8},{8,0},{16,24},{24,16},{1,9},{9,1},{17,25},{25,17},{2,10},{10... | collective-permute-start | bytes 1572872 | tf_op jit(solution)/shard_map/ppermute | solution.py:21
  155.9 16.2 %collective-permute-start.25 = (bf16[512,512]{1,0:T(8,128)(2,1)S(1)}, bf16[512,512]{1,0:T(8,128)(2,1)S(1)}, u32[]{:S(2)}, u32[]{:S(2)}) collective-permute-start(bf16[512,512]{1,0:T(8,128)(2,1)S(1)} %slice.204), channel_id=1, source_target_pairs={{0,16},{8,24},{16,0},{24,8},{1,17},{9,25},{17,1},{25,9},{2,18},{10... | collective-permute-start | bytes 1572872 | tf_op jit(solution)/shard_map/ppermute | solution.py:21
  186.5 25.6 %collective-permute-start.32 = (bf16[256,2048]{1,0:T(8,128)(2,1)}, bf16[256,2048]{1,0:T(8,128)(2,1)}, u32[]{:S(2)}, u32[]{:S(2)}) collective-permute-start(bf16[256,2048]{1,0:T(8,128)(2,1)} %get-tuple-element.115.refs_0_), channel_id=1, source_target_pairs={{0,16},{8,24},{16,0},{24,8},{1,17},{9,25},{17,1},{25,9},{2,18},{10... | collective-permute-start | bytes 3145736 | tf_op jit(solution)/shard_map/ppermute | solution.py:21
  188.2 25.2 %collective-permute-start.31 = (bf16[256,2048]{1,0:T(8,128)(2,1)}, bf16[256,2048]{1,0:T(8,128)(2,1)}, u32[]{:S(2)}, u32[]{:S(2)}) collective-permute-start(bf16[256,2048]{1,0:T(8,128)(2,1)} %get-tuple-element.115.refs_0_), channel_id=1, source_target_pairs={{0,8},{8,0},{16,24},{24,16},{1,9},{9,1},{17,25},{25,17},{2,10},{10... | collective-permute-start | bytes 3145736 | tf_op jit(solution)/shard_map/ppermute | solution.py:21
  229.5 23.5 %collective-permute-start.36 = (bf16[256,2048]{1,0:T(8,128)(2,1)}, bf16[256,2048]{1,0:T(8,128)(2,1)S(1)}, u32[]{:S(2)}, u32[]{:S(2)}) collective-permute-start(bf16[256,2048]{1,0:T(8,128)(2,1)} %shard_map.233.refs_0_), channel_id=1, source_target_pairs={{0,16},{8,24},{16,0},{24,8},{1,17},{9,25},{17,1},{25,9},{2,18},{10... | collective-permute-start | bytes 3145736 | tf_op jit(solution)/shard_map/ppermute | solution.py:21
  230.1 23.4 %collective-permute-start.35 = (bf16[256,2048]{1,0:T(8,128)(2,1)}, bf16[256,2048]{1,0:T(8,128)(2,1)S(1)}, u32[]{:S(2)}, u32[]{:S(2)}) collective-permute-start(bf16[256,2048]{1,0:T(8,128)(2,1)} %shard_map.233.refs_0_), channel_id=1, source_target_pairs={{0,8},{8,0},{16,24},{24,16},{1,9},{9,1},{17,25},{25,17},{2,10},{10... | collective-permute-start | bytes 3145736 | tf_op jit(solution)/shard_map/ppermute | solution.py:21
  267.4 147.1 %reduce-scatter.6.cloned.1.call-start = ((), (), s32[]{:S(2)}) async-start(), calls=%async_computation.6 | async-start | bytes 6488064 | tf_op jit(solution)/shard_map/reduce_scatter | solution.py:825
  267.7 34.5 %collective-permute-start.40 = (bf16[256,2048]{1,0:T(8,128)(2,1)}, bf16[256,2048]{1,0:T(8,128)(2,1)S(1)}, u32[]{:S(2)}, u32[]{:S(2)}) collective-permute-start(bf16[256,2048]{1,0:T(8,128)(2,1)} %get-tuple-element.127.refs_5_), channel_id=1, source_target_pairs={{0,16},{8,24},{16,0},{24,8},{1,17},{9,25},{17,1},{25,9},{2,18},{10... | collective-permute-start | bytes 3145736 | tf_op jit(solution)/shard_map/ppermute | solution.py:21
  268.5 33.7 %collective-permute-start.39 = (bf16[256,2048]{1,0:T(8,128)(2,1)}, bf16[256,2048]{1,0:T(8,128)(2,1)S(1)}, u32[]{:S(2)}, u32[]{:S(2)}) collective-permute-start(bf16[256,2048]{1,0:T(8,128)(2,1)} %get-tuple-element.127.refs_5_), channel_id=1, source_target_pairs={{0,8},{8,0},{16,24},{24,16},{1,9},{9,1},{17,25},{25,17},{2,10},{10... | collective-permute-start | bytes 3145736 | tf_op jit(solution)/shard_map/ppermute | solution.py:21
  273.6 28.6 %collective-permute-start.38 = (bf16[128,2048]{1,0:T(8,128)(2,1)}, bf16[128,2048]{1,0:T(8,128)(2,1)S(1)}, u32[]{:S(2)}, u32[]{:S(2)}) collective-permute-start(bf16[128,2048]{1,0:T(8,128)(2,1)} %slice.209), channel_id=1, source_target_pairs={{0,8},{8,0},{16,24},{24,16},{1,9},{9,1},{17,25},{25,17},{2,10},{10... | collective-permute-start | bytes 1572872 | tf_op jit(solution)/shard_map/ppermute | solution.py:21
  274.3 27.9 %collective-permute-start.37 = (bf16[128,2048]{1,0:T(8,128)(2,1)}, bf16[128,2048]{1,0:T(8,128)(2,1)S(1)}, u32[]{:S(2)}, u32[]{:S(2)}) collective-permute-start(bf16[128,2048]{1,0:T(8,128)(2,1)} %slice.208), channel_id=1, source_target_pairs={{0,16},{8,24},{16,0},{24,8},{1,17},{9,25},{17,1},{25,9},{2,18},{10... | collective-permute-start | bytes 1572872 | tf_op jit(solution)/shard_map/ppermute | solution.py:21
  306.7 19.3 %collective-permute-start.42 = (bf16[128,2048]{1,0:T(8,128)(2,1)S(1)}, bf16[128,2048]{1,0:T(8,128)(2,1)S(1)}, u32[]{:S(2)}, u32[]{:S(2)}) collective-permute-start(bf16[128,2048]{1,0:T(8,128)(2,1)S(1)} %slice.211), channel_id=1, source_target_pairs={{0,8},{8,0},{16,24},{24,16},{1,9},{9,1},{17,25},{25,17},{2,10},{10... | collective-permute-start | bytes 1572872 | tf_op jit(solution)/shard_map/ppermute | solution.py:21
  307.8 18.3 %collective-permute-start.41 = (bf16[128,2048]{1,0:T(8,128)(2,1)S(1)}, bf16[128,2048]{1,0:T(8,128)(2,1)S(1)}, u32[]{:S(2)}, u32[]{:S(2)}) collective-permute-start(bf16[128,2048]{1,0:T(8,128)(2,1)S(1)} %slice.210), channel_id=1, source_target_pairs={{0,16},{8,24},{16,0},{24,8},{1,17},{9,25},{17,1},{25,9},{2,18},{10... | collective-permute-start | bytes 1572872 | tf_op jit(solution)/shard_map/ppermute | solution.py:21
  340.6 151.0 %reduce-scatter.8.cloned.1.call-start = ((), (), s32[]{:S(2)}) async-start(), calls=%async_computation.7 | async-start | bytes 6488064 | tf_op jit(solution)/shard_map/reduce_scatter | solution.py:864
  340.8 15.1 %collective-permute-start.46 = (bf16[128,2048]{1,0:T(8,128)(2,1)}, bf16[128,2048]{1,0:T(8,128)(2,1)S(1)}, u32[]{:S(2)}, u32[]{:S(2)}) collective-permute-start(bf16[128,2048]{1,0:T(8,128)(2,1)} %get-tuple-element.141), channel_id=1, source_target_pairs={{0,8},{8,0},{16,24},{24,16},{1,9},{9,1},{17,25},{25,17},{2,10},{10... | collective-permute-start | bytes 1572872 | tf_op jit(solution)/shard_map/ppermute | solution.py:21
  342.3 14.9 %collective-permute-start.47 = (bf16[128,2048]{1,0:T(8,128)(2,1)S(1)}, bf16[128,2048]{1,0:T(8,128)(2,1)S(1)}, u32[]{:S(2)}, u32[]{:S(2)}) collective-permute-start(bf16[128,2048]{1,0:T(8,128)(2,1)S(1)} %copy-done.92), channel_id=1, source_target_pairs={{0,16},{8,24},{16,0},{24,8},{1,17},{9,25},{17,1},{25,9},{2,18},{10... | collective-permute-start | bytes 1572872 | tf_op jit(solution)/shard_map/ppermute | solution.py:21
  343.5 20.5 %collective-permute-start.48 = (bf16[128,2048]{1,0:T(8,128)(2,1)S(1)}, bf16[128,2048]{1,0:T(8,128)(2,1)S(1)}, u32[]{:S(2)}, u32[]{:S(2)}) collective-permute-start(bf16[128,2048]{1,0:T(8,128)(2,1)S(1)} %add_convert_fusion.7), channel_id=1, source_target_pairs={{0,16},{8,24},{16,0},{24,8},{1,17},{9,25},{17,1},{25,9},{2,18},{10... | collective-permute-start | bytes 1572872 | tf_op jit(solution)/shard_map/ppermute | solution.py:21
  344.4 19.6 %collective-permute-start.45 = (bf16[128,2048]{1,0:T(8,128)(2,1)S(1)}, bf16[128,2048]{1,0:T(8,128)(2,1)S(1)}, u32[]{:S(2)}, u32[]{:S(2)}) collective-permute-start(bf16[128,2048]{1,0:T(8,128)(2,1)S(1)} %add_convert_fusion.8), channel_id=1, source_target_pairs={{0,8},{8,0},{16,24},{24,16},{1,9},{9,1},{17,25},{25,17},{2,10},{10... | collective-permute-start | bytes 1572872 | tf_op jit(solution)/shard_map/ppermute | solution.py:21
  365.8 13.1 %collective-permute-start.50 = (bf16[128,2048]{1,0:T(8,128)(2,1)}, bf16[128,2048]{1,0:T(8,128)(2,1)S(1)}, u32[]{:S(2)}, u32[]{:S(2)}) collective-permute-start(bf16[128,2048]{1,0:T(8,128)(2,1)} %shard_map.243.refs_1_), channel_id=1, source_target_pairs={{0,8},{8,0},{16,24},{24,16},{1,9},{9,1},{17,25},{25,17},{2,10},{10... | collective-permute-start | bytes 1572872 | tf_op jit(solution)/shard_map/ppermute | solution.py:21
  389.3 24.3 %collective-permute-start.51 = (bf16[256,512]{1,0:T(8,128)(2,1)}, bf16[256,512]{1,0:T(8,128)(2,1)S(1)}, u32[]{:S(2)}, u32[]{:S(2)}) collective-permute-start(bf16[256,512]{1,0:T(8,128)(2,1)} %get-tuple-element.151), channel_id=1, source_target_pairs={{0,8},{8,0},{16,24},{24,16},{1,9},{9,1},{17,25},{25,17},{2,10},{10... | collective-permute-start | bytes 786440 | tf_op jit(solution)/shard_map/ppermute | solution.py:21
  390.8 22.9 %collective-permute-start.52 = (bf16[256,512]{1,0:T(8,128)(2,1)}, bf16[256,512]{1,0:T(8,128)(2,1)S(1)}, u32[]{:S(2)}, u32[]{:S(2)}) collective-permute-start(bf16[256,512]{1,0:T(8,128)(2,1)} %get-tuple-element.152), channel_id=1, source_target_pairs={{0,16},{8,24},{16,0},{24,8},{1,17},{9,25},{17,1},{25,9},{2,18},{10... | collective-permute-start | bytes 786440 | tf_op jit(solution)/shard_map/ppermute | solution.py:21
  391.3 22.4 %collective-permute-start.53 = (bf16[256,512]{1,0:T(8,128)(2,1)}, bf16[256,512]{1,0:T(8,128)(2,1)S(1)}, u32[]{:S(2)}, u32[]{:S(2)}) collective-permute-start(bf16[256,512]{1,0:T(8,128)(2,1)} %get-tuple-element.153), channel_id=1, source_target_pairs={{0,24},{8,16},{16,8},{24,0},{1,25},{9,17},{17,9},{25,1},{2,26},{10... | collective-permute-start | bytes 786440 | tf_op jit(solution)/shard_map/ppermute | solution.py:21
  414.6 187.9 %all-gather.9.cloned.1.call-start = ((), (), s32[]{:S(2)}) async-start(), calls=%async_computation.8 | async-start | bytes 7208960 | tf_op jit(solution)/shard_map/all_gather | solution.py:942
  417.7 12.9 %collective-permute-start.55 = (bf16[256,256]{1,0:T(8,128)(2,1)S(1)}, bf16[256,256]{1,0:T(8,128)(2,1)S(1)}, u32[]{:S(2)}, u32[]{:S(2)}) collective-permute-start(bf16[256,256]{1,0:T(8,128)(2,1)S(1)} %get-tuple-element.207), channel_id=1, source_target_pairs={{2,0},{3,1},{4,2},{5,3},{6,4},{7,5},{10,8},{11,9},{12,10},{13,11},... | collective-permute-start | bytes 393224 | tf_op jit(solution)/shard_map/ppermute | solution.py:95
  420.9 18.8 %collective-permute-start.57 = (bf16[176,2048]{1,0:T(8,128)(2,1)}, bf16[176,2048]{1,0:T(8,128)(2,1)S(1)}, u32[]{:S(2)}, u32[]{:S(2)}) collective-permute-start(bf16[176,2048]{1,0:T(8,128)(2,1)} %shard_map.248), channel_id=1, source_target_pairs={{0,16},{8,24},{16,0},{24,8},{1,17},{9,25},{17,1},{25,9},{2,18},{10... | collective-permute-start | bytes 2162696 | tf_op jit(solution)/shard_map/ppermute | solution.py:21
  421.5 18.5 %collective-permute-start.56 = (bf16[176,2048]{1,0:T(8,128)(2,1)}, bf16[176,2048]{1,0:T(8,128)(2,1)S(1)}, u32[]{:S(2)}, u32[]{:S(2)}) collective-permute-start(bf16[176,2048]{1,0:T(8,128)(2,1)} %shard_map.248), channel_id=1, source_target_pairs={{0,8},{8,0},{16,24},{24,16},{1,9},{9,1},{17,25},{25,17},{2,10},{10... | collective-permute-start | bytes 2162696 | tf_op jit(solution)/shard_map/ppermute | solution.py:21
  440.9 31.9 %collective-permute-start.61 = (bf16[128,2048]{1,0:T(8,128)(2,1)}, bf16[128,2048]{1,0:T(8,128)(2,1)S(1)}, u32[]{:S(2)}, u32[]{:S(2)}) collective-permute-start(bf16[128,2048]{1,0:T(8,128)(2,1)} %get-tuple-element.165.refs_1_), channel_id=1, source_target_pairs={{0,8},{8,0},{16,24},{24,16},{1,9},{9,1},{17,25},{25,17},{2,10},{10... | collective-permute-start | bytes 1572872 | tf_op jit(solution)/shard_map/ppermute | solution.py:21
  442.3 30.4 %collective-permute-start.62 = (bf16[128,2048]{1,0:T(8,128)(2,1)}, bf16[128,2048]{1,0:T(8,128)(2,1)S(1)}, u32[]{:S(2)}, u32[]{:S(2)}) collective-permute-start(bf16[128,2048]{1,0:T(8,128)(2,1)} %shard_map.251), channel_id=1, source_target_pairs={{0,16},{8,24},{16,0},{24,8},{1,17},{9,25},{17,1},{25,9},{2,18},{10... | collective-permute-start | bytes 1572872 | tf_op jit(solution)/shard_map/ppermute | solution.py:21
  446.0 19.3 %collective-permute-start.60 = (bf16[256,768]{1,0:T(8,128)(2,1)}, bf16[256,768]{1,0:T(8,128)(2,1)S(1)}, u32[]{:S(2)}, u32[]{:S(2)}) collective-permute-start(bf16[256,768]{1,0:T(8,128)(2,1)} %get-tuple-element.210.refs_21_), channel_id=1, source_target_pairs={{0,24},{8,16},{16,8},{24,0},{1,25},{9,17},{17,9},{25,1},{2,26},{10... | collective-permute-start | bytes 1179656 | tf_op jit(solution)/shard_map/ppermute | solution.py:21
  446.6 25.0 %collective-permute-start.58 = (bf16[256,768]{1,0:T(8,128)(2,1)}, bf16[256,768]{1,0:T(8,128)(2,1)S(1)}, u32[]{:S(2)}, u32[]{:S(2)}) collective-permute-start(bf16[256,768]{1,0:T(8,128)(2,1)} %get-tuple-element.211.refs_19_), channel_id=1, source_target_pairs={{0,8},{8,0},{16,24},{24,16},{1,9},{9,1},{17,25},{25,17},{2,10},{10... | collective-permute-start | bytes 1179656 | tf_op jit(solution)/shard_map/ppermute | solution.py:21
  448.0 24.7 %collective-permute-start.59 = (bf16[256,768]{1,0:T(8,128)(2,1)S(1)}, bf16[256,768]{1,0:T(8,128)(2,1)S(1)}, u32[]{:S(2)}, u32[]{:S(2)}) collective-permute-start(bf16[256,768]{1,0:T(8,128)(2,1)S(1)} %get-tuple-element.212.refs_20_), channel_id=1, source_target_pairs={{0,16},{8,24},{16,0},{24,8},{1,17},{9,25},{17,1},{25,9},{2,18},{10... | collective-permute-start | bytes 1179656 | tf_op jit(solution)/shard_map/ppermute | solution.py:21
  491.5 13.0 %collective-permute-start.65 = (bf16[1024,1408]{1,0:T(8,128)(2,1)}, bf16[1024,1408]{1,0:T(8,128)(2,1)}, u32[]{:S(2)}, u32[]{:S(2)}) collective-permute-start(bf16[1024,1408]{1,0:T(8,128)(2,1)} %shard_map.254), channel_id=1, source_target_pairs={{0,1},{1,0},{2,3},{3,2},{4,5},{5,4},{6,7},{7,6},{8,9},{9,8},{10,11... | collective-permute-start | bytes 8650760 | tf_op jit(solution)/shard_map/ppermute | solution.py:21
  500.7 63.3 %collective-permute-start.63 = (bf16[128,2048]{1,0:T(8,128)(2,1)S(1)}, bf16[128,2048]{1,0:T(8,128)(2,1)S(1)}, u32[]{:S(2)}, u32[]{:S(2)}) collective-permute-start(bf16[128,2048]{1,0:T(8,128)(2,1)S(1)} %add_convert_fusion.6), channel_id=1, source_target_pairs={{0,8},{8,0},{16,24},{24,16},{1,9},{9,1},{17,25},{25,17},{2,10},{10... | collective-permute-start | bytes 1572872 | tf_op jit(solution)/shard_map/ppermute | solution.py:21
  503.4 60.6 %collective-permute-start.64 = (bf16[128,2048]{1,0:T(8,128)(2,1)S(1)}, bf16[128,2048]{1,0:T(8,128)(2,1)S(1)}, u32[]{:S(2)}, u32[]{:S(2)}) collective-permute-start(bf16[128,2048]{1,0:T(8,128)(2,1)S(1)} %add_convert_fusion.5), channel_id=1, source_target_pairs={{0,16},{8,24},{16,0},{24,8},{1,17},{9,25},{17,1},{25,9},{2,18},{10... | collective-permute-start | bytes 1572872 | tf_op jit(solution)/shard_map/ppermute | solution.py:21
  506.4 19.1 %collective-permute-start.67 = (bf16[256,1408]{1,0:T(8,128)(2,1)S(1)}, bf16[256,1408]{1,0:T(8,128)(2,1)S(1)}, u32[]{:S(2)}, u32[]{:S(2)}) collective-permute-start(bf16[256,1408]{1,0:T(8,128)(2,1)S(1)} %get-tuple-element.187), channel_id=1, source_target_pairs={{0,2},{1,3},{2,0},{3,1},{4,6},{5,7},{6,4},{7,5},{8,10},{9,11},{10,... | collective-permute-start | bytes 2162696 | tf_op jit(solution)/shard_map/ppermute | solution.py:21
  509.8 31.2 %collective-permute-start.66 = (bf16[256,1408]{1,0:T(8,128)(2,1)S(1)}, bf16[256,1408]{1,0:T(8,128)(2,1)S(1)}, u32[]{:S(2)}, u32[]{:S(2)}) collective-permute-start(bf16[256,1408]{1,0:T(8,128)(2,1)S(1)} %get-tuple-element.186), channel_id=1, source_target_pairs={{0,2},{1,3},{2,0},{3,1},{4,6},{5,7},{6,4},{7,5},{8,10},{9,11},{10,... | collective-permute-start | bytes 2162696 | tf_op jit(solution)/shard_map/ppermute | solution.py:21
  526.9 33.4 %collective-permute-start.68 = (bf16[256,1408]{1,0:T(8,128)(2,1)S(1)}, bf16[256,1408]{1,0:T(8,128)(2,1)S(1)}, u32[]{:S(2)}, u32[]{:S(2)}) collective-permute-start(bf16[256,1408]{1,0:T(8,128)(2,1)S(1)} %add_convert_fusion.1), channel_id=1, source_target_pairs={{0,6},{1,7},{2,4},{3,5},{4,2},{5,3},{6,0},{7,1},{8,14},{9,15},{10,... | collective-permute-start | bytes 2162696 | tf_op jit(solution)/shard_map/ppermute | solution.py:21
  561.9 27.7 %collective-permute-start.69 = (bf16[256,1152]{1,0:T(8,128)(2,1)S(1)}, bf16[256,1152]{1,0:T(8,128)(2,1)S(1)}, u32[]{:S(2)}, u32[]{:S(2)}) collective-permute-start(bf16[256,1152]{1,0:T(8,128)(2,1)S(1)} %get-tuple-element.204), channel_id=1, source_target_pairs={{0,8},{8,0},{16,24},{24,16},{1,9},{9,1},{17,25},{25,17},{2,10},{10... | collective-permute-start | bytes 1769480 | tf_op jit(solution)/shard_map/ppermute | solution.py:21
  563.1 28.1 %collective-permute-start.70 = (bf16[256,1152]{1,0:T(8,128)(2,1)S(1)}, bf16[256,1152]{1,0:T(8,128)(2,1)S(1)}, u32[]{:S(2)}, u32[]{:S(2)}) collective-permute-start(bf16[256,1152]{1,0:T(8,128)(2,1)S(1)} %get-tuple-element.204), channel_id=1, source_target_pairs={{0,16},{8,24},{16,0},{24,8},{1,17},{9,25},{17,1},{25,9},{2,18},{10... | collective-permute-start | bytes 1769480 | tf_op jit(solution)/shard_map/ppermute | solution.py:21
  (117 other events, 761.6 us)
Sparse Core Ops, SparseCore 0:
  61.9 115.3 all-gather.4
  179.0 58.0 all-gather.6
  267.6 68.1 reduce-scatter.3
  340.7 68.0 reduce-scatter.5
  414.7 65.2 reduce-scatter.7
  494.2 98.7 all-gather.8

commit v4 on v3

--- a/solution.py
+++ b/solution.py
@@ -824,6 +824,8 @@
     grad_gate_w = tie(grad_gate_w, own_down, *passed)
     own_gate = lax.psum_scatter(grad_gate_w, "seq", scatter_dimension=0, tiled=True)
     grad_up_w = dot_tn(normed_two_all, grad_gu[:, hidden_slot:]).astype(BF)
+    if slots == 4:
+        near[0], near[1], far[0], far[1] = fence([*near, *far], [grad_up_w])
     grad_normed_two = scatter_total(grad_parts, near, far)
     down_parts[-1] = tie(down_parts[-1], grad_normed_two)
     down_passed = scatter_pass(
@@ -833,7 +835,7 @@
     grad_middle, grad_attended, grad_gain_two, *branch = call(
         functools.partial(mid_back_kernel, shape),
         (place, grad_normed_two, middle, cot_own, gain_two, *out_w),
-        (grad_up_w, *down_passed),
+        (grad_up_w,),
         (
             shape_of(tok_count, model, F32),
             shape_of(tok_count, head_count * head_width, BF),

time: 630 us -> 622 us (0.987)
  waiting for transfers between devices: 215 us -> 205 us
    ppermute x4, waiting for transfers between devices: 18.4 us -> 11.5 us  [shifted(): return lax.ppermute(block, axis, route)]
    unnamed x212 -> x218, local copies, waits for them, and re-layouts: 37.2 us -> 38.2 us
  transfers between devices with their start and end apart: 81 -> 81, of which waited for: 36 -> 35; matrix products, arithmetic and copies ran while one was open for 19% -> 20% of each run, Pallas kernels for 23% -> 23%
where the time goes in v4:
time: 622 us; the launch traced here: 610 us
  waiting for transfers between devices  205 us (33%)
  Pallas kernels  150 us (24%)
  starting transfers between devices  86.3 us (14%)
  local copies, waits for them, and re-layouts  72 us (12%)
  matrix products  41 us (7%)
  other arithmetic  39.5 us (6%)
  between operations  16.6 us (3%)
    ppermute x71, waiting for transfers between devices, swap(): lax.ppermute(block, axis, [(i, i ^ mask) for i in range(lax.axis_size(axi...  190 us
    ppermute x71, starting transfers between devices, swap(): lax.ppermute(block, axis, [(i, i ^ mask) for i in range(lax.axis_size(axi...  73.1 us
    pallas_call x5, Pallas kernels, call(): pl.pallas_call(run, out_shape=out_shape, in_specs=[SMEM] + [VMEM] * (coun...  40.2 us
    unnamed x218, local copies, waits for them, and re-layouts  38.2 us
    dot_general x3, matrix products, dot_tn(): lax.dot_general(left, right, (((0,), (0,)), ((), ())), preferred_element_...  30.3 us
    pallas_call x2, Pallas kernels, cut_product(): pl.pallas_call(functools.partial(rows_kernel, transposed, len(late)), out...  27.6 us
    pallas_call x1, Pallas kernels, shards(): pl.pallas_call(functools.partial(attend_back_kernel, hop_count, 0), out_s...  20.8 us
    pallas_call x1, Pallas kernels, shards(): pl.pallas_call(functools.partial(gate_kernel, len(normed_two_parts)), out...  19.2 us
  transfers between devices with their start and end apart: 81, of which 35 were waited for; matrix products, arithmetic and copies ran while one was open for 20% of the time, Pallas kernels for 23%

profile of v4, /device:TPU:10, one launch (start us, length us, event | category | flops | bytes accessed | tf_op | source)
XLA Modules:
  0.0 610.3 jit_solution(13961665686564454741)
XLA Ops:
  8.1 2.8 constant_dynamic-update-slice_fusion.4
  17.1 2.5 collective-permute-start
  20.2 4.5 shard_map.220.refs_5_.refs_3_
  27.3 8.8 %collective-permute-done.3.refs_4_ = bf16[256,2048]{1,0:T(8,128)(2,1)} collective-permute-done((bf16[256,2048]{1,0:T(8,128)(2,1)}, bf16[256,2048]{1,0:T(8,128)(2,1)}, u32[]{:S(2)}, u32[]{:S(2)}) %collective-permute-start.3) | collective-permute-done | bytes 1048608 | tf_op jit(solution)/shard_map/ppermute | solution.py:21
  36.2 2.3 copy.106.refs_1_
  38.5 2.3 copy.105.refs_0_
  48.8 2.5 collective-permute-start.5
  51.3 3.1 collective-permute-done.4.refs_4_
  56.4 3.7 collective-permute-done.6.refs_5_
  64.9 6.0 collective-permute-start.13
  70.9 8.1 %collective-permute-done.13.refs_4_ = bf16[256,512]{1,0:T(8,128)(2,1)S(1)} collective-permute-done((bf16[256,512]{1,0:T(8,128)(2,1)}, bf16[256,512]{1,0:T(8,128)(2,1)S(1)}, u32[]{:S(2)}, u32[]{:S(2)}) %collective-permute-start.13) | collective-permute-done | bytes 262176 | tf_op jit(solution)/shard_map/ppermute | solution.py:21
  79.0 9.5 %collective-permute-done.11.refs_1_ = bf16[1024,512]{1,0:T(8,128)(2,1)S(1)} collective-permute-done((bf16[1024,512]{1,0:T(8,128)(2,1)}, bf16[1024,512]{1,0:T(8,128)(2,1)S(1)}, u32[]{:S(2)}, u32[]{:S(2)}) %collective-permute-start.11) | collective-permute-done | bytes 1048608 | tf_op jit(solution)/shard_map/ppermute | solution.py:21
  95.3 2.1 pad_maximum_fusion.7.refs_2_
  97.4 9.9 %collective-permute-done.15.refs_1_ = bf16[512,512]{1,0:T(8,128)(2,1)S(1)} collective-permute-done((bf16[512,512]{1,0:T(8,128)(2,1)S(1)}, bf16[512,512]{1,0:T(8,128)(2,1)S(1)}, u32[]{:S(2)}, u32[]{:S(2)}) %collective-permute-start.15) | collective-permute-done | bytes 524320 | tf_op jit(solution)/shard_map/ppermute | solution.py:21
  117.4 1.9 slice.252
  120.9 8.3 %shard_map.226 = (bf16[256,2048]{1,0:T(8,128)(2,1)}, bf16[256,2048]{1,0:T(8,128)(2,1)}, bf16[256,256]{1,0:T(8,128)(2,1)}) custom-call(s32[3]{0:T(128)} %pad_add_fusion.refs_0_.place, bf16[256,2048]{1,0:T(8,128)(2,1)} %bitcast.47, f32[1,2048]{1,0:T(1,128)} %bitcast.67, f32[256,1]{1,0:T(8,128)} %fusion.15.refs_3_, ...), custom_call_target="tpu_custom_call" | custom-call | tf_op jit(solution)/shard_map/pallas_call | solution.py:556
  129.2 2.0 collective-permute-start.21
  131.2 3.9 collective-permute-start.20
  135.1 8.0 %collective-permute-done.21.refs_3_.refs_1_ = bf16[256,256]{1,0:T(8,128)(2,1)S(1)} collective-permute-done((bf16[256,256]{1,0:T(8,128)(2,1)}, bf16[256,256]{1,0:T(8,128)(2,1)S(1)}, u32[]{:S(2)}, u32[]{:S(2)}) %collective-permute-start.21) | collective-permute-done | bytes 131104 | tf_op jit(solution)/shard_map/ppermute | solution.py:95
  143.1 2.6 collective-permute-done.20.refs_2_.refs_0_
  148.6 3.5 collective-permute-start.27
  156.4 15.6 %shard_map.228.refs_4_.refs_1_ = bf16[256,2048]{1,0:T(8,128)(2,1)} custom-call(s32[3]{0:T(128)} %pad_add_fusion.refs_0_.place, bf16[256,2048]{1,0:T(8,128)(2,1)} %get-tuple-element.111.query_ref, bf16[256,256]{1,0:T(8,128)(2,1)} %copy-done.87, bf16[256,256]{1,0:T(8,128)(2,1)} %copy-done.86, bf16[256,256]{1,0:T(8,128)(2,1)} %get-tuple-element.112.refs_2_, ...), custom_call_target="tpu_custom_call" | custom-call | tf_op jit(solution)/shard_map/pallas_call | solution.py:713
  178.1 8.5 %shard_map.230 = (f32[256,2048]{1,0:T(8,128)}, bf16[256,2048]{1,0:T(8,128)(2,1)}, bf16[256,2048]{1,0:T(8,128)(2,1)}) custom-call(s32[3]{0:T(128)} %pad_add_fusion.refs_0_.place, bf16[256,2048]{1,0:T(8,128)(2,1)} %shard_map.228.refs_4_.refs_1_, bf16[256,2048]{1,0:T(8,128)(2,1)} %bitcast.48, f32[1,2048]{1,0:T(1,128)} %bitcast.69, ...), custom_call_target="tpu_custom_call" | custom-call | tf_op jit(solution)/shard_map/pallas_call | solution.py:556
  192.5 19.6 %collective-permute-done.32.refs_1_ = bf16[256,2048]{1,0:T(8,128)(2,1)} collective-permute-done((bf16[256,2048]{1,0:T(8,128)(2,1)}, bf16[256,2048]{1,0:T(8,128)(2,1)}, u32[]{:S(2)}, u32[]{:S(2)}) %collective-permute-start.32) | collective-permute-done | bytes 1048608 | tf_op jit(solution)/shard_map/ppermute | solution.py:21
  216.9 11.9 %collective-permute-done.34.refs_4_.refs_2_ = bf16[128,2048]{1,0:T(8,128)(2,1)S(1)} collective-permute-done((bf16[128,2048]{1,0:T(8,128)(2,1)S(1)}, bf16[128,2048]{1,0:T(8,128)(2,1)S(1)}, u32[]{:S(2)}, u32[]{:S(2)}) %collective-permute-start.34) | collective-permute-done | bytes 524320 | tf_op jit(solution)/shard_map/ppermute | solution.py:21
  231.9 19.2 %shard_map.232 = (bf16[1024,2048]{1,0:T(8,128)(2,1)}, bf16[1024,1408]{1,0:T(8,128)(2,1)}, bf16[1024,1408]{1,0:T(8,128)(2,1)}, bf16[1024,1408]{1,0:T(8,128)(2,1)}) custom-call(bf16[256,2048]{1,0:T(8,128)(2,1)} %get-tuple-element.119.refs_0_, bf16[256,2048]{1,0:T(8,128)(2,1)} %get-tuple-element.120.refs_1_, bf16[256,2048]{1,0:T(8,128)(2,1)} %get-tuple-element.121.refs_2_, ...), custom_call_target="tpu_custom_call" | custom-call | tf_op jit(solution)/shard_map/pallas_call | solution.py:754
  251.1 2.2 collective-permute-done.36.refs_2_.refs_1_
  255.2 1.8 copy-done.3
  257.0 10.7 %convolution_convert_fusion = bf16[1408,2048]{1,0:T(8,128)(2,1)} fusion(bf16[1024,1408]{1,0:T(8,128)(2,1)S(1)} %copy-done.3, bf16[1024,2048]{1,0:T(8,128)(2,1)} %shard_map.234.refs_3_), kind=kOutput, calls=%fused_computation.3 | convolution fusion | flops 5908463616 | bytes 12845056 | tf_op jit(solution)/shard_map/dot_general | solution.py:115
  270.1 1.9 slice.208
  272.0 1.9 slice.209
  275.9 10.7 %fusion.31 = f32[1024,1408]{1,0:T(8,128)S(1)} fusion(bf16[1024,2048]{1,0:T(8,128)(2,1)} %shard_map.234.refs_3_, bf16[1408,2048]{1,0:T(8,128)(2,1)} %all-gather.7.cloned.1.call-done.right_ref), kind=kOutput, calls=%fused_computation.114 | convolution fusion | flops 5905580032 | bytes 15728640 | tf_op jit(solution)/shard_map/dot_general | solution.py:111
  286.6 2.9 fusion.5
  289.5 8.7 %convolution_convert_fusion.2.refs_5_.refs_0_ = bf16[2048,1408]{1,0:T(8,128)(2,1)} fusion(bf16[1024,2048]{1,0:T(8,128)(2,1)S(1)} %copy-done.100, bf16[1024,1408]{1,0:T(8,128)(2,1)S(1)} %get-tuple-element.192), kind=kOutput, calls=%fused_computation.5 | convolution fusion | flops 5908463616 | bytes 12845056 | tf_op jit(solution)/shard_map/dot_general | solution.py:115
  298.2 2.9 pad_maximum_fusion.refs_0_
  309.2 17.2 %shard_map.237 = (bf16[256,2048]{1,0:T(8,128)(2,1)}, bf16[128,2048]{1,0:T(8,128)(2,1)}, bf16[128,2048]{1,0:T(8,128)(2,1)}, bf16[128,2048]{1,0:T(8,128)(2,1)}, bf...) custom-call(bf16[1024,2816]{1,0:T(8,128)(2,1)} %shard_map.236.left_ref.refs_2_.refs_4_, ...), custom_call_target="tpu_custom_call" | custom-call | tf_op jit(solution)/shard_map/pallas_call | solution.py:798
  329.4 10.4 %shard_map.239 = (bf16[256,2048]{1,0:T(8,128)(2,1)}, bf16[128,2048]{1,0:T(8,128)(2,1)}, bf16[128,2048]{1,0:T(8,128)(2,1)}, bf16[128,2048]{1,0:T(8,128)(2,1)}, bf...) custom-call(bf16[1024,1408]{1,0:T(8,128)(2,1)} %shard_map.238.left_ref, ...), custom_call_target="tpu_custom_call" | custom-call | tf_op jit(solution)/shard_map/pallas_call | solution.py:798
  345.7 11.0 %convolution_convert_fusion.1.refs_4_.refs_15_.refs_0_ = bf16[2048,1408]{1,0:T(8,128)(2,1)} fusion(bf16[1024,2048]{1,0:T(8,128)(2,1)} %get-tuple-element.132, bf16[1024,2816]{1,0:T(8,128)(2,1)} %get-tuple-element.149), kind=kOutput, calls=%fused_computation.4 | convolution fusion | flops 5908463616 | bytes 12845056 | tf_op jit(solution)/shard_map/dot_general | solution.py:115
  357.3 5.9 collective-permute-done.48.refs_3_
  364.8 3.3 convert_add_fusion.refs_1_
  371.1 9.4 %shard_map.244 = (f32[256,2048]{1,0:T(8,128)}, bf16[256,2048]{1,0:T(8,128)(2,1)}, f32[1,2048]{1,0:T(1,128)}, bf16[256,512]{1,0:T(8,128)(2,1)}, bf16[256,512]{1,0...) custom-call(s32[3]{0:T(128)} %pad_add_fusion.refs_0_.place, f32[256,2048]{1,0:T(8,128)} %convert_add_fusion.refs_1_, ...), custom_call_target="tpu_custom_call" | custom-call | tf_op jit(solution)/shard_map/pallas_call | solution.py:556
  381.7 2.4 collective-permute-start.53
  384.1 20.8 %shard_map.245 = (bf16[256,2048]{1,0:T(8,128)(2,1)}, f32[768,256]{1,0:T(8,128)}) custom-call(s32[3]{0:T(128)} %pad_add_fusion.refs_0_.place, bf16[256,2048]{1,0:T(8,128)(2,1)} %get-tuple-element.111.query_ref, bf16[256,2048]{1,0:T(8,128)(2,1)} %get-tuple-element.154.grad_ref, bf16[256,256]{1,0:T(8,128)(2,1)} %copy-done.87, bf16[256,256]{1,0:T(8,128)(2,1)} %copy-done.86, ...), custom_call_target="tpu_custom_call" | custom-call | tf_op jit(solution)/shard_map/pallas_call | solution.py:849
  406.2 2.7 reduce-scatter.6.cloned.1.call-done.refs_1_
  410.1 2.5 collective-permute-start.54
  412.6 4.3 collective-permute-start.55
  422.0 15.1 %collective-permute-done.57.refs_3_ = bf16[176,2048]{1,0:T(8,128)(2,1)S(1)} collective-permute-done((bf16[176,2048]{1,0:T(8,128)(2,1)}, bf16[176,2048]{1,0:T(8,128)(2,1)S(1)}, u32[]{:S(2)}, u32[]{:S(2)}) %collective-permute-start.57) | collective-permute-done | bytes 720928 | tf_op jit(solution)/shard_map/ppermute | solution.py:21
  440.3 2.2 pad_maximum_fusion.8
  442.5 2.3 collective-permute-start.60
  446.0 9.5 %shard_map.251 = (bf16[256,2048]{1,0:T(8,128)(2,1)}, f32[1,2048]{1,0:T(1,128)}) custom-call(s32[3]{0:T(128)} %pad_add_fusion.refs_0_.place, bf16[256,2048]{1,0:T(8,128)(2,1)} %get-tuple-element.155.refs_1_, bf16[256,256]{1,0:T(8,128)(2,1)} %get-tuple-element.165.refs_2_, bf16[256,2048]{1,0:T(8,128)(2,1)} %bitcast.49, ...), custom_call_target="tpu_custom_call" | custom-call | tf_op jit(solution)/shard_map/pallas_call | solution.py:556
  457.4 5.2 collective-permute-done.60.refs_7_.refs_13_
  462.6 7.4 %collective-permute-done.58.refs_5_.refs_11_ = bf16[256,768]{1,0:T(8,128)(2,1)S(1)} collective-permute-done((bf16[256,768]{1,0:T(8,128)(2,1)}, bf16[256,768]{1,0:T(8,128)(2,1)S(1)}, u32[]{:S(2)}, u32[]{:S(2)}) %collective-permute-start.58) | collective-permute-done | bytes 393248 | tf_op jit(solution)/shard_map/ppermute | solution.py:21
  471.3 8.7 %shard_map.254.refs_19_ = bf16[1024,1408]{1,0:T(8,128)(2,1)} custom-call(s32[3]{0:T(128)} %pad_add_fusion.refs_0_.place, bf16[256,2048]{1,0:T(8,128)(2,1)} %shard_map.233.refs_0_, bf16[256,2048]{1,0:T(8,128)(2,1)} %get-tuple-element.129.refs_1_, bf16[256,2048]{1,0:T(8,128)(2,1)} %get-tuple-element.130.refs_2_, bf16[128,2048]{1,0:T(8,128)(2,1)} %copy-done.31, ...), custom_call_target="tpu_custom_call" | custom-call | tf_op jit(solution)/shard_map/pallas_call | solution.py:917
  480.0 8.8 %shard_map.255 = bf16[1024,1408]{1,0:T(8,128)(2,1)} custom-call(s32[3]{0:T(128)} %pad_add_fusion.refs_0_.place, bf16[256,2048]{1,0:T(8,128)(2,1)} %shard_map.233.refs_0_, bf16[256,2048]{1,0:T(8,128)(2,1)} %get-tuple-element.129.refs_1_, bf16[256,2048]{1,0:T(8,128)(2,1)} %get-tuple-element.130.refs_2_, bf16[128,2048]{1,0:T(8,128)(2,1)} %copy-done.31, ...), custom_call_target="tpu_custom_call" | custom-call | tf_op jit(solution)/shard_map/pallas_call | solution.py:917
  489.0 2.4 pad_maximum_fusion.2
  503.8 9.9 %collective-permute-done.73 = bf16[88,2048]{1,0:T(8,128)(2,1)S(1)} collective-permute-done((bf16[88,2048]{1,0:T(8,128)(2,1)S(1)}, bf16[88,2048]{1,0:T(8,128)(2,1)S(1)}, u32[]{:S(2)}, u32[]{:S(2)}) %collective-permute-start.73) | collective-permute-done | bytes 360480 | tf_op jit(solution)/shard_map/ppermute | solution.py:21
  514.3 8.6 %collective-permute-done.67 = bf16[256,1408]{1,0:T(8,128)(2,1)S(1)} collective-permute-done((bf16[256,1408]{1,0:T(8,128)(2,1)S(1)}, bf16[256,1408]{1,0:T(8,128)(2,1)S(1)}, u32[]{:S(2)}, u32[]{:S(2)}) %collective-permute-start.67) | collective-permute-done | bytes 720928 | tf_op jit(solution)/shard_map/ppermute | solution.py:21
  524.8 3.5 bitcast_convert_fusion
  528.3 21.6 %collective-permute-done.66 = bf16[256,1408]{1,0:T(8,128)(2,1)S(1)} collective-permute-done((bf16[256,1408]{1,0:T(8,128)(2,1)S(1)}, bf16[256,1408]{1,0:T(8,128)(2,1)S(1)}, u32[]{:S(2)}, u32[]{:S(2)}) %collective-permute-start.66) | collective-permute-done | bytes 720928 | tf_op jit(solution)/shard_map/ppermute | solution.py:21
  549.9 4.7 collective-permute-done.68
  558.5 1.7 fusion.9
  560.9 20.0 %collective-permute-done.69 = bf16[256,1152]{1,0:T(8,128)(2,1)S(1)} collective-permute-done((bf16[256,1152]{1,0:T(8,128)(2,1)S(1)}, bf16[256,1152]{1,0:T(8,128)(2,1)S(1)}, u32[]{:S(2)}, u32[]{:S(2)}) %collective-permute-start.69) | collective-permute-done | bytes 589856 | tf_op jit(solution)/shard_map/ppermute | solution.py:21
  584.4 3.8 collective-permute-done.71
  593.8 9.2 %shard_map.258 = (f32[256,5632]{1,0:T(8,128)}, f32[256,5632]{1,0:T(8,128)}) custom-call(bf16[4,256,2816]{2,1,0:T(8,128)(2,1)} %bitcast.50), custom_call_target="tpu_custom_call" | custom-call | tf_op jit(solution)/shard_map/pallas_call | solution.py:951
  (456 shorter events, 142.3 us)
Async XLA Ops:
  7.2 224.7 %all-gather.5.cloned.1.call-start = ((), (), s32[]{:S(2)}) async-start(), calls=%async_computation.3 | async-start | bytes 12976128 | tf_op jit(solution)/shard_map/all_gather | solution.py:642
  10.9 25.2 %collective-permute-start.3 = (bf16[256,2048]{1,0:T(8,128)(2,1)}, bf16[256,2048]{1,0:T(8,128)(2,1)}, u32[]{:S(2)}, u32[]{:S(2)}) collective-permute-start(bf16[256,2048]{1,0:T(8,128)(2,1)} %get-tuple-element.191), channel_id=1, source_target_pairs={{0,16},{8,24},{16,0},{24,8},{1,17},{9,25},{17,1},{25,9},{2,18},{10... | collective-permute-start | bytes 3145736 | tf_op jit(solution)/shard_map/ppermute | solution.py:21
  12.5 26.0 %collective-permute-start.2 = (bf16[256,2048]{1,0:T(8,128)(2,1)}, bf16[256,2048]{1,0:T(8,128)(2,1)}, u32[]{:S(2)}, u32[]{:S(2)}) collective-permute-start(bf16[256,2048]{1,0:T(8,128)(2,1)} %get-tuple-element.191), channel_id=1, source_target_pairs={{0,8},{8,0},{16,24},{24,16},{1,9},{9,1},{17,25},{25,17},{2,10},{10... | collective-permute-start | bytes 3145736 | tf_op jit(solution)/shard_map/ppermute | solution.py:21
  15.5 25.3 %collective-permute-start.1 = (bf16[272,768]{1,0:T(8,128)(2,1)}, bf16[272,768]{1,0:T(8,128)(2,1)S(1)}, u32[]{:S(2)}, u32[]{:S(2)}) collective-permute-start(bf16[272,768]{1,0:T(8,128)(2,1)} %pad_maximum_fusion.14), channel_id=1, source_target_pairs={{0,6},{1,7},{2,4},{3,5},{4,2},{5,3},{6,0},{7,1},{8,14},{9,15},{10,... | collective-permute-start | bytes 1253384 | tf_op jit(solution)/shard_map/ppermute | solution.py:21
  17.1 23.7 %collective-permute-start = (bf16[272,768]{1,0:T(8,128)(2,1)}, bf16[272,768]{1,0:T(8,128)(2,1)}, u32[]{:S(2)}, u32[]{:S(2)}) collective-permute-start(bf16[272,768]{1,0:T(8,128)(2,1)} %pad_maximum_fusion.14), channel_id=1, source_target_pairs={{0,2},{1,3},{2,0},{3,1},{4,6},{5,7},{6,4},{7,5},{8,10},{9,11},{10,... | collective-permute-start | bytes 1253384 | tf_op jit(solution)/shard_map/ppermute | solution.py:21
  43.1 16.9 %collective-permute-start.8 = (bf16[128,2048]{1,0:T(8,128)(2,1)S(1)}, bf16[128,2048]{1,0:T(8,128)(2,1)S(1)}, u32[]{:S(2)}, u32[]{:S(2)}) collective-permute-start(bf16[128,2048]{1,0:T(8,128)(2,1)S(1)} %slice.195), channel_id=1, source_target_pairs={{0,8},{8,0},{16,24},{24,16},{1,9},{9,1},{17,25},{25,17},{2,10},{10... | collective-permute-start | bytes 1572872 | tf_op jit(solution)/shard_map/ppermute | solution.py:21
  43.7 16.3 %collective-permute-start.7 = (bf16[128,2048]{1,0:T(8,128)(2,1)S(1)}, bf16[128,2048]{1,0:T(8,128)(2,1)S(1)}, u32[]{:S(2)}, u32[]{:S(2)}) collective-permute-start(bf16[128,2048]{1,0:T(8,128)(2,1)S(1)} %slice.194), channel_id=1, source_target_pairs={{0,16},{8,24},{16,0},{24,8},{1,17},{9,25},{17,1},{25,9},{2,18},{10... | collective-permute-start | bytes 1572872 | tf_op jit(solution)/shard_map/ppermute | solution.py:21
  61.8 214.0 %all-gather.7.cloned.1.call-start = ((), (), s32[]{:S(2)}) async-start(), calls=%async_computation.4 | async-start | bytes 6488064 | tf_op jit(solution)/shard_map/all_gather | solution.py:643
  62.6 278.2 %reduce-scatter.4.cloned.1.call-start = ((), (), s32[]{:S(2)}) async-start(), calls=%async_computation.5 | async-start | bytes 6488064 | tf_op jit(solution)/shard_map/reduce_scatter | solution.py:775
  62.6 16.3 %collective-permute-start.12 = (bf16[1024,512]{1,0:T(8,128)(2,1)}, bf16[1024,512]{1,0:T(8,128)(2,1)S(1)}, u32[]{:S(2)}, u32[]{:S(2)}) collective-permute-start(bf16[1024,512]{1,0:T(8,128)(2,1)} %get-tuple-element.105.refs_6_), channel_id=1, source_target_pairs={{0,1},{1,0},{2,3},{3,2},{4,5},{5,4},{6,7},{7,6},{8,9},{9,8},{10,11... | collective-permute-start | bytes 3145736 | tf_op jit(solution)/shard_map/ppermute | solution.py:21
  62.7 25.8 %collective-permute-start.11 = (bf16[1024,512]{1,0:T(8,128)(2,1)}, bf16[1024,512]{1,0:T(8,128)(2,1)S(1)}, u32[]{:S(2)}, u32[]{:S(2)}) collective-permute-start(bf16[1024,512]{1,0:T(8,128)(2,1)} %get-tuple-element.105.refs_6_), channel_id=1, source_target_pairs={{0,16},{8,24},{16,0},{24,8},{1,17},{9,25},{17,1},{25,9},{2,18},{10... | collective-permute-start | bytes 3145736 | tf_op jit(solution)/shard_map/ppermute | solution.py:21
  64.3 25.4 %collective-permute-start.10 = (bf16[1024,512]{1,0:T(8,128)(2,1)}, bf16[1024,512]{1,0:T(8,128)(2,1)S(1)}, u32[]{:S(2)}, u32[]{:S(2)}) collective-permute-start(bf16[1024,512]{1,0:T(8,128)(2,1)} %get-tuple-element.105.refs_6_), channel_id=1, source_target_pairs={{0,8},{8,0},{16,24},{24,16},{1,9},{9,1},{17,25},{25,17},{2,10},{10... | collective-permute-start | bytes 3145736 | tf_op jit(solution)/shard_map/ppermute | solution.py:21
  64.8 14.1 %collective-permute-start.9 = (bf16[1088,256]{1,0:T(8,128)(2,1)}, bf16[1088,256]{1,0:T(8,128)(2,1)S(1)}, u32[]{:S(2)}, u32[]{:S(2)}) collective-permute-start(bf16[1088,256]{1,0:T(8,128)(2,1)} %get-tuple-element.104), channel_id=1, source_target_pairs={{0,1},{1,0},{2,3},{3,2},{4,5},{5,4},{6,7},{7,6},{8,9},{9,8},{10,11... | collective-permute-start | bytes 1671176 | tf_op jit(solution)/shard_map/ppermute | solution.py:21
  64.9 14.1 %collective-permute-start.13 = (bf16[256,512]{1,0:T(8,128)(2,1)}, bf16[256,512]{1,0:T(8,128)(2,1)S(1)}, u32[]{:S(2)}, u32[]{:S(2)}) collective-permute-start(bf16[256,512]{1,0:T(8,128)(2,1)} %get-tuple-element.106), channel_id=1, source_target_pairs={{0,2},{1,3},{2,0},{3,1},{4,6},{5,7},{6,4},{7,5},{8,10},{9,11},{10,... | collective-permute-start | bytes 786440 | tf_op jit(solution)/shard_map/ppermute | solution.py:21
  90.7 16.9 %collective-permute-start.16 = (bf16[1024,512]{1,0:T(8,128)(2,1)}, bf16[1024,512]{1,0:T(8,128)(2,1)S(1)}, u32[]{:S(2)}, u32[]{:S(2)}) collective-permute-start(bf16[1024,512]{1,0:T(8,128)(2,1)} %get-tuple-element.107.refs_7_), channel_id=1, source_target_pairs={{0,1},{1,0},{2,3},{3,2},{4,5},{5,4},{6,7},{7,6},{8,9},{9,8},{10,11... | collective-permute-start | bytes 3145736 | tf_op jit(solution)/shard_map/ppermute | solution.py:21
  90.7 17.7 %collective-permute-start.17 = (bf16[1024,512]{1,0:T(8,128)(2,1)}, bf16[1024,512]{1,0:T(8,128)(2,1)S(1)}, u32[]{:S(2)}, u32[]{:S(2)}) collective-permute-start(bf16[1024,512]{1,0:T(8,128)(2,1)} %get-tuple-element.108.refs_8_), channel_id=1, source_target_pairs={{0,1},{1,0},{2,3},{3,2},{4,5},{5,4},{6,7},{7,6},{8,9},{9,8},{10,11... | collective-permute-start | bytes 3145736 | tf_op jit(solution)/shard_map/ppermute | solution.py:21
  93.4 13.9 %collective-permute-start.15 = (bf16[512,512]{1,0:T(8,128)(2,1)S(1)}, bf16[512,512]{1,0:T(8,128)(2,1)S(1)}, u32[]{:S(2)}, u32[]{:S(2)}) collective-permute-start(bf16[512,512]{1,0:T(8,128)(2,1)S(1)} %slice.200), channel_id=1, source_target_pairs={{0,8},{8,0},{16,24},{24,16},{1,9},{9,1},{17,25},{25,17},{2,10},{10... | collective-permute-start | bytes 1572872 | tf_op jit(solution)/shard_map/ppermute | solution.py:21
  110.4 35.3 %collective-permute-start.24 = (bf16[1024,512]{1,0:T(8,128)(2,1)}, bf16[1024,512]{1,0:T(8,128)(2,1)S(1)}, u32[]{:S(2)}, u32[]{:S(2)}) collective-permute-start(bf16[1024,512]{1,0:T(8,128)(2,1)} %get-tuple-element.113.refs_4_.refs_5_), channel_id=1, source_target_pairs={{0,1},{1,0},{2,3},{3,2},{4,5},{5,4},{6,7},{7,6},{8,9},{9,8},{10,11... | collective-permute-start | bytes 3145736 | tf_op jit(solution)/shard_map/ppermute | solution.py:21
  110.4 35.3 %collective-permute-start.23 = (bf16[1024,512]{1,0:T(8,128)(2,1)}, bf16[1024,512]{1,0:T(8,128)(2,1)S(1)}, u32[]{:S(2)}, u32[]{:S(2)}) collective-permute-start(bf16[1024,512]{1,0:T(8,128)(2,1)} %get-tuple-element.113.refs_4_.refs_5_), channel_id=1, source_target_pairs={{0,16},{8,24},{16,0},{24,8},{1,17},{9,25},{17,1},{25,9},{2,18},{10... | collective-permute-start | bytes 3145736 | tf_op jit(solution)/shard_map/ppermute | solution.py:21
  111.7 35.0 %collective-permute-start.22 = (bf16[1024,512]{1,0:T(8,128)(2,1)}, bf16[1024,512]{1,0:T(8,128)(2,1)S(1)}, u32[]{:S(2)}, u32[]{:S(2)}) collective-permute-start(bf16[1024,512]{1,0:T(8,128)(2,1)} %get-tuple-element.113.refs_4_.refs_5_), channel_id=1, source_target_pairs={{0,8},{8,0},{16,24},{24,16},{1,9},{9,1},{17,25},{25,17},{2,10},{10... | collective-permute-start | bytes 3145736 | tf_op jit(solution)/shard_map/ppermute | solution.py:21
  129.2 13.8 %collective-permute-start.21 = (bf16[256,256]{1,0:T(8,128)(2,1)}, bf16[256,256]{1,0:T(8,128)(2,1)S(1)}, u32[]{:S(2)}, u32[]{:S(2)}) collective-permute-start(bf16[256,256]{1,0:T(8,128)(2,1)} %get-tuple-element.112.refs_2_), channel_id=1, source_target_pairs={{0,1},{1,2},{2,3},{3,4},{4,5},{5,6},{6,7},{8,9},{9,10},{10,11},{11... | collective-permute-start | bytes 393224 | tf_op jit(solution)/shard_map/ppermute | solution.py:95
  131.2 14.5 %collective-permute-start.20 = (bf16[256,256]{1,0:T(8,128)(2,1)}, bf16[256,256]{1,0:T(8,128)(2,1)S(1)}, u32[]{:S(2)}, u32[]{:S(2)}) collective-permute-start(bf16[256,256]{1,0:T(8,128)(2,1)} %get-tuple-element.112.refs_2_), channel_id=1, source_target_pairs={{0,2},{1,3},{2,4},{3,5},{4,6},{5,7},{8,10},{9,11},{10,12},{11,13},... | collective-permute-start | bytes 393224 | tf_op jit(solution)/shard_map/ppermute | solution.py:95
  148.6 23.4 %collective-permute-start.27 = (bf16[1024,512]{1,0:T(8,128)(2,1)}, bf16[1024,512]{1,0:T(8,128)(2,1)S(1)}, u32[]{:S(2)}, u32[]{:S(2)}) collective-permute-start(bf16[1024,512]{1,0:T(8,128)(2,1)} %get-tuple-element.114.refs_3_.refs_5_.refs_6_), channel_id=1, source_target_pairs={{0,1},{1,0},{2,3},{3,2},{4,5},{5,4},{6,7},{7,6},{8,9},{9,8},{10,11... | collective-permute-start | bytes 3145736 | tf_op jit(solution)/shard_map/ppermute | solution.py:21
  152.1 19.9 %collective-permute-start.28 = (bf16[1024,512]{1,0:T(8,128)(2,1)}, bf16[1024,512]{1,0:T(8,128)(2,1)S(1)}, u32[]{:S(2)}, u32[]{:S(2)}) collective-permute-start(bf16[1024,512]{1,0:T(8,128)(2,1)} %get-tuple-element.115.refs_4_.refs_6_.refs_7_), channel_id=1, source_target_pairs={{0,1},{1,0},{2,3},{3,2},{4,5},{5,4},{6,7},{7,6},{8,9},{9,8},{10,11... | collective-permute-start | bytes 3145736 | tf_op jit(solution)/shard_map/ppermute | solution.py:21
  154.3 17.7 %collective-permute-start.26 = (bf16[512,512]{1,0:T(8,128)(2,1)S(1)}, bf16[512,512]{1,0:T(8,128)(2,1)S(1)}, u32[]{:S(2)}, u32[]{:S(2)}) collective-permute-start(bf16[512,512]{1,0:T(8,128)(2,1)S(1)} %slice.205), channel_id=1, source_target_pairs={{0,8},{8,0},{16,24},{24,16},{1,9},{9,1},{17,25},{25,17},{2,10},{10... | collective-permute-start | bytes 1572872 | tf_op jit(solution)/shard_map/ppermute | solution.py:21
  155.8 16.2 %collective-permute-start.25 = (bf16[512,512]{1,0:T(8,128)(2,1)S(1)}, bf16[512,512]{1,0:T(8,128)(2,1)S(1)}, u32[]{:S(2)}, u32[]{:S(2)}) collective-permute-start(bf16[512,512]{1,0:T(8,128)(2,1)S(1)} %slice.204), channel_id=1, source_target_pairs={{0,16},{8,24},{16,0},{24,8},{1,17},{9,25},{17,1},{25,9},{2,18},{10... | collective-permute-start | bytes 1572872 | tf_op jit(solution)/shard_map/ppermute | solution.py:21
  186.6 25.6 %collective-permute-start.32 = (bf16[256,2048]{1,0:T(8,128)(2,1)}, bf16[256,2048]{1,0:T(8,128)(2,1)}, u32[]{:S(2)}, u32[]{:S(2)}) collective-permute-start(bf16[256,2048]{1,0:T(8,128)(2,1)} %get-tuple-element.119.refs_0_), channel_id=1, source_target_pairs={{0,16},{8,24},{16,0},{24,8},{1,17},{9,25},{17,1},{25,9},{2,18},{10... | collective-permute-start | bytes 3145736 | tf_op jit(solution)/shard_map/ppermute | solution.py:21
  188.2 25.3 %collective-permute-start.31 = (bf16[256,2048]{1,0:T(8,128)(2,1)}, bf16[256,2048]{1,0:T(8,128)(2,1)}, u32[]{:S(2)}, u32[]{:S(2)}) collective-permute-start(bf16[256,2048]{1,0:T(8,128)(2,1)} %get-tuple-element.119.refs_0_), channel_id=1, source_target_pairs={{0,8},{8,0},{16,24},{24,16},{1,9},{9,1},{17,25},{25,17},{2,10},{10... | collective-permute-start | bytes 3145736 | tf_op jit(solution)/shard_map/ppermute | solution.py:21
  229.7 23.6 %collective-permute-start.36 = (bf16[256,2048]{1,0:T(8,128)(2,1)}, bf16[256,2048]{1,0:T(8,128)(2,1)S(1)}, u32[]{:S(2)}, u32[]{:S(2)}) collective-permute-start(bf16[256,2048]{1,0:T(8,128)(2,1)} %shard_map.233.refs_0_), channel_id=1, source_target_pairs={{0,16},{8,24},{16,0},{24,8},{1,17},{9,25},{17,1},{25,9},{2,18},{10... | collective-permute-start | bytes 3145736 | tf_op jit(solution)/shard_map/ppermute | solution.py:21
  230.3 23.5 %collective-permute-start.35 = (bf16[256,2048]{1,0:T(8,128)(2,1)}, bf16[256,2048]{1,0:T(8,128)(2,1)S(1)}, u32[]{:S(2)}, u32[]{:S(2)}) collective-permute-start(bf16[256,2048]{1,0:T(8,128)(2,1)} %shard_map.233.refs_0_), channel_id=1, source_target_pairs={{0,8},{8,0},{16,24},{24,16},{1,9},{9,1},{17,25},{25,17},{2,10},{10... | collective-permute-start | bytes 3145736 | tf_op jit(solution)/shard_map/ppermute | solution.py:21
  267.7 141.2 %reduce-scatter.6.cloned.1.call-start = ((), (), s32[]{:S(2)}) async-start(), calls=%async_computation.6 | async-start | bytes 6488064 | tf_op jit(solution)/shard_map/reduce_scatter | solution.py:825
  268.0 34.6 %collective-permute-start.40 = (bf16[256,2048]{1,0:T(8,128)(2,1)}, bf16[256,2048]{1,0:T(8,128)(2,1)S(1)}, u32[]{:S(2)}, u32[]{:S(2)}) collective-permute-start(bf16[256,2048]{1,0:T(8,128)(2,1)} %get-tuple-element.131.refs_5_), channel_id=1, source_target_pairs={{0,16},{8,24},{16,0},{24,8},{1,17},{9,25},{17,1},{25,9},{2,18},{10... | collective-permute-start | bytes 3145736 | tf_op jit(solution)/shard_map/ppermute | solution.py:21
  268.8 33.8 %collective-permute-start.39 = (bf16[256,2048]{1,0:T(8,128)(2,1)}, bf16[256,2048]{1,0:T(8,128)(2,1)S(1)}, u32[]{:S(2)}, u32[]{:S(2)}) collective-permute-start(bf16[256,2048]{1,0:T(8,128)(2,1)} %get-tuple-element.131.refs_5_), channel_id=1, source_target_pairs={{0,8},{8,0},{16,24},{24,16},{1,9},{9,1},{17,25},{25,17},{2,10},{10... | collective-permute-start | bytes 3145736 | tf_op jit(solution)/shard_map/ppermute | solution.py:21
  273.9 28.7 %collective-permute-start.38 = (bf16[128,2048]{1,0:T(8,128)(2,1)}, bf16[128,2048]{1,0:T(8,128)(2,1)S(1)}, u32[]{:S(2)}, u32[]{:S(2)}) collective-permute-start(bf16[128,2048]{1,0:T(8,128)(2,1)} %slice.209), channel_id=1, source_target_pairs={{0,8},{8,0},{16,24},{24,16},{1,9},{9,1},{17,25},{25,17},{2,10},{10... | collective-permute-start | bytes 1572872 | tf_op jit(solution)/shard_map/ppermute | solution.py:21
  274.6 28.0 %collective-permute-start.37 = (bf16[128,2048]{1,0:T(8,128)(2,1)}, bf16[128,2048]{1,0:T(8,128)(2,1)S(1)}, u32[]{:S(2)}, u32[]{:S(2)}) collective-permute-start(bf16[128,2048]{1,0:T(8,128)(2,1)} %slice.208), channel_id=1, source_target_pairs={{0,16},{8,24},{16,0},{24,8},{1,17},{9,25},{17,1},{25,9},{2,18},{10... | collective-permute-start | bytes 1572872 | tf_op jit(solution)/shard_map/ppermute | solution.py:21
  307.1 19.2 %collective-permute-start.42 = (bf16[128,2048]{1,0:T(8,128)(2,1)S(1)}, bf16[128,2048]{1,0:T(8,128)(2,1)S(1)}, u32[]{:S(2)}, u32[]{:S(2)}) collective-permute-start(bf16[128,2048]{1,0:T(8,128)(2,1)S(1)} %slice.211), channel_id=1, source_target_pairs={{0,8},{8,0},{16,24},{24,16},{1,9},{9,1},{17,25},{25,17},{2,10},{10... | collective-permute-start | bytes 1572872 | tf_op jit(solution)/shard_map/ppermute | solution.py:21
  308.2 18.2 %collective-permute-start.41 = (bf16[128,2048]{1,0:T(8,128)(2,1)S(1)}, bf16[128,2048]{1,0:T(8,128)(2,1)S(1)}, u32[]{:S(2)}, u32[]{:S(2)}) collective-permute-start(bf16[128,2048]{1,0:T(8,128)(2,1)S(1)} %slice.210), channel_id=1, source_target_pairs={{0,16},{8,24},{16,0},{24,8},{1,17},{9,25},{17,1},{25,9},{2,18},{10... | collective-permute-start | bytes 1572872 | tf_op jit(solution)/shard_map/ppermute | solution.py:21
  340.9 148.1 %reduce-scatter.8.cloned.1.call-start = ((), (), s32[]{:S(2)}) async-start(), calls=%async_computation.7 | async-start | bytes 6488064 | tf_op jit(solution)/shard_map/reduce_scatter | solution.py:866
  341.1 15.5 %collective-permute-start.45 = (bf16[128,2048]{1,0:T(8,128)(2,1)}, bf16[128,2048]{1,0:T(8,128)(2,1)S(1)}, u32[]{:S(2)}, u32[]{:S(2)}) collective-permute-start(bf16[128,2048]{1,0:T(8,128)(2,1)} %get-tuple-element.143), channel_id=1, source_target_pairs={{0,8},{8,0},{16,24},{24,16},{1,9},{9,1},{17,25},{25,17},{2,10},{10... | collective-permute-start | bytes 1572872 | tf_op jit(solution)/shard_map/ppermute | solution.py:21
  342.2 15.1 %collective-permute-start.46 = (bf16[128,2048]{1,0:T(8,128)(2,1)}, bf16[128,2048]{1,0:T(8,128)(2,1)S(1)}, u32[]{:S(2)}, u32[]{:S(2)}) collective-permute-start(bf16[128,2048]{1,0:T(8,128)(2,1)} %get-tuple-element.144), channel_id=1, source_target_pairs={{0,16},{8,24},{16,0},{24,8},{1,17},{9,25},{17,1},{25,9},{2,18},{10... | collective-permute-start | bytes 1572872 | tf_op jit(solution)/shard_map/ppermute | solution.py:21
  343.4 19.8 %collective-permute-start.48 = (bf16[128,2048]{1,0:T(8,128)(2,1)S(1)}, bf16[128,2048]{1,0:T(8,128)(2,1)S(1)}, u32[]{:S(2)}, u32[]{:S(2)}) collective-permute-start(bf16[128,2048]{1,0:T(8,128)(2,1)S(1)} %add_convert_fusion.7), channel_id=1, source_target_pairs={{0,16},{8,24},{16,0},{24,8},{1,17},{9,25},{17,1},{25,9},{2,18},{10... | collective-permute-start | bytes 1572872 | tf_op jit(solution)/shard_map/ppermute | solution.py:21
  344.6 18.6 %collective-permute-start.47 = (bf16[128,2048]{1,0:T(8,128)(2,1)S(1)}, bf16[128,2048]{1,0:T(8,128)(2,1)S(1)}, u32[]{:S(2)}, u32[]{:S(2)}) collective-permute-start(bf16[128,2048]{1,0:T(8,128)(2,1)S(1)} %add_convert_fusion.8), channel_id=1, source_target_pairs={{0,8},{8,0},{16,24},{24,16},{1,9},{9,1},{17,25},{25,17},{2,10},{10... | collective-permute-start | bytes 1572872 | tf_op jit(solution)/shard_map/ppermute | solution.py:21
  368.1 36.9 %collective-permute-start.49 = (bf16[128,2048]{1,0:T(8,128)(2,1)}, bf16[128,2048]{1,0:T(8,128)(2,1)S(1)}, u32[]{:S(2)}, u32[]{:S(2)}) collective-permute-start(bf16[128,2048]{1,0:T(8,128)(2,1)} %shard_map.247), channel_id=1, source_target_pairs={{0,16},{8,24},{16,0},{24,8},{1,17},{9,25},{17,1},{25,9},{2,18},{10... | collective-permute-start | bytes 1572872 | tf_op jit(solution)/shard_map/ppermute | solution.py:21
  369.6 35.4 %collective-permute-start.50 = (bf16[128,2048]{1,0:T(8,128)(2,1)}, bf16[128,2048]{1,0:T(8,128)(2,1)S(1)}, u32[]{:S(2)}, u32[]{:S(2)}) collective-permute-start(bf16[128,2048]{1,0:T(8,128)(2,1)} %shard_map.246.refs_1_), channel_id=1, source_target_pairs={{0,8},{8,0},{16,24},{24,16},{1,9},{9,1},{17,25},{25,17},{2,10},{10... | collective-permute-start | bytes 1572872 | tf_op jit(solution)/shard_map/ppermute | solution.py:21
  380.6 24.4 %collective-permute-start.51 = (bf16[256,512]{1,0:T(8,128)(2,1)}, bf16[256,512]{1,0:T(8,128)(2,1)S(1)}, u32[]{:S(2)}, u32[]{:S(2)}) collective-permute-start(bf16[256,512]{1,0:T(8,128)(2,1)} %get-tuple-element.159), channel_id=1, source_target_pairs={{0,8},{8,0},{16,24},{24,16},{1,9},{9,1},{17,25},{25,17},{2,10},{10... | collective-permute-start | bytes 786440 | tf_op jit(solution)/shard_map/ppermute | solution.py:21
  381.1 23.8 %collective-permute-start.52 = (bf16[256,512]{1,0:T(8,128)(2,1)}, bf16[256,512]{1,0:T(8,128)(2,1)S(1)}, u32[]{:S(2)}, u32[]{:S(2)}) collective-permute-start(bf16[256,512]{1,0:T(8,128)(2,1)} %get-tuple-element.160), channel_id=1, source_target_pairs={{0,16},{8,24},{16,0},{24,8},{1,17},{9,25},{17,1},{25,9},{2,18},{10... | collective-permute-start | bytes 786440 | tf_op jit(solution)/shard_map/ppermute | solution.py:21
  381.7 23.3 %collective-permute-start.53 = (bf16[256,512]{1,0:T(8,128)(2,1)}, bf16[256,512]{1,0:T(8,128)(2,1)S(1)}, u32[]{:S(2)}, u32[]{:S(2)}) collective-permute-start(bf16[256,512]{1,0:T(8,128)(2,1)} %get-tuple-element.161), channel_id=1, source_target_pairs={{0,24},{8,16},{16,8},{24,0},{1,25},{9,17},{17,9},{25,1},{2,26},{10... | collective-permute-start | bytes 786440 | tf_op jit(solution)/shard_map/ppermute | solution.py:21
  408.9 184.9 %all-gather.9.cloned.1.call-start = ((), (), s32[]{:S(2)}) async-start(), calls=%async_computation.8 | async-start | bytes 7208960 | tf_op jit(solution)/shard_map/all_gather | solution.py:944
  417.9 19.1 %collective-permute-start.57 = (bf16[176,2048]{1,0:T(8,128)(2,1)}, bf16[176,2048]{1,0:T(8,128)(2,1)S(1)}, u32[]{:S(2)}, u32[]{:S(2)}) collective-permute-start(bf16[176,2048]{1,0:T(8,128)(2,1)} %shard_map.249), channel_id=1, source_target_pairs={{0,16},{8,24},{16,0},{24,8},{1,17},{9,25},{17,1},{25,9},{2,18},{10... | collective-permute-start | bytes 2162696 | tf_op jit(solution)/shard_map/ppermute | solution.py:21
  419.4 18.8 %collective-permute-start.56 = (bf16[176,2048]{1,0:T(8,128)(2,1)}, bf16[176,2048]{1,0:T(8,128)(2,1)S(1)}, u32[]{:S(2)}, u32[]{:S(2)}) collective-permute-start(bf16[176,2048]{1,0:T(8,128)(2,1)} %shard_map.249), channel_id=1, source_target_pairs={{0,8},{8,0},{16,24},{24,16},{1,9},{9,1},{17,25},{25,17},{2,10},{10... | collective-permute-start | bytes 2162696 | tf_op jit(solution)/shard_map/ppermute | solution.py:21
  439.1 31.1 %collective-permute-start.61 = (bf16[128,2048]{1,0:T(8,128)(2,1)}, bf16[128,2048]{1,0:T(8,128)(2,1)S(1)}, u32[]{:S(2)}, u32[]{:S(2)}) collective-permute-start(bf16[128,2048]{1,0:T(8,128)(2,1)} %get-tuple-element.173.refs_1_), channel_id=1, source_target_pairs={{0,8},{8,0},{16,24},{24,16},{1,9},{9,1},{17,25},{25,17},{2,10},{10... | collective-permute-start | bytes 1572872 | tf_op jit(solution)/shard_map/ppermute | solution.py:21
  439.7 30.5 %collective-permute-start.62 = (bf16[128,2048]{1,0:T(8,128)(2,1)}, bf16[128,2048]{1,0:T(8,128)(2,1)S(1)}, u32[]{:S(2)}, u32[]{:S(2)}) collective-permute-start(bf16[128,2048]{1,0:T(8,128)(2,1)} %shard_map.252), channel_id=1, source_target_pairs={{0,16},{8,24},{16,0},{24,8},{1,17},{9,25},{17,1},{25,9},{2,18},{10... | collective-permute-start | bytes 1572872 | tf_op jit(solution)/shard_map/ppermute | solution.py:21
  442.5 20.1 %collective-permute-start.60 = (bf16[256,768]{1,0:T(8,128)(2,1)}, bf16[256,768]{1,0:T(8,128)(2,1)S(1)}, u32[]{:S(2)}, u32[]{:S(2)}) collective-permute-start(bf16[256,768]{1,0:T(8,128)(2,1)} %get-tuple-element.218.refs_21_), channel_id=1, source_target_pairs={{0,24},{8,16},{16,8},{24,0},{1,25},{9,17},{17,9},{25,1},{2,26},{10... | collective-permute-start | bytes 1179656 | tf_op jit(solution)/shard_map/ppermute | solution.py:21
  444.8 25.1 %collective-permute-start.58 = (bf16[256,768]{1,0:T(8,128)(2,1)}, bf16[256,768]{1,0:T(8,128)(2,1)S(1)}, u32[]{:S(2)}, u32[]{:S(2)}) collective-permute-start(bf16[256,768]{1,0:T(8,128)(2,1)} %get-tuple-element.219.refs_19_), channel_id=1, source_target_pairs={{0,8},{8,0},{16,24},{24,16},{1,9},{9,1},{17,25},{25,17},{2,10},{10... | collective-permute-start | bytes 1179656 | tf_op jit(solution)/shard_map/ppermute | solution.py:21
  445.4 24.8 %collective-permute-start.59 = (bf16[256,768]{1,0:T(8,128)(2,1)S(1)}, bf16[256,768]{1,0:T(8,128)(2,1)S(1)}, u32[]{:S(2)}, u32[]{:S(2)}) collective-permute-start(bf16[256,768]{1,0:T(8,128)(2,1)S(1)} %get-tuple-element.220.refs_20_), channel_id=1, source_target_pairs={{0,16},{8,24},{16,0},{24,8},{1,17},{9,25},{17,1},{25,9},{2,18},{10... | collective-permute-start | bytes 1179656 | tf_op jit(solution)/shard_map/ppermute | solution.py:21
  494.9 18.9 %collective-permute-start.74 = (bf16[88,2048]{1,0:T(8,128)(2,1)S(1)}, bf16[88,2048]{1,0:T(8,128)(2,1)S(1)}, u32[]{:S(2)}, u32[]{:S(2)}) collective-permute-start(bf16[88,2048]{1,0:T(8,128)(2,1)S(1)} %slice.244), channel_id=1, source_target_pairs={{0,8},{8,0},{16,24},{24,16},{1,9},{9,1},{17,25},{25,17},{2,10},{10... | collective-permute-start | bytes 1081352 | tf_op jit(solution)/shard_map/ppermute | solution.py:21
  496.4 17.3 %collective-permute-start.73 = (bf16[88,2048]{1,0:T(8,128)(2,1)S(1)}, bf16[88,2048]{1,0:T(8,128)(2,1)S(1)}, u32[]{:S(2)}, u32[]{:S(2)}) collective-permute-start(bf16[88,2048]{1,0:T(8,128)(2,1)S(1)} %slice.243), channel_id=1, source_target_pairs={{0,16},{8,24},{16,0},{24,8},{1,17},{9,25},{17,1},{25,9},{2,18},{10... | collective-permute-start | bytes 1081352 | tf_op jit(solution)/shard_map/ppermute | solution.py:21
  498.6 59.9 %collective-permute-start.63 = (bf16[128,2048]{1,0:T(8,128)(2,1)S(1)}, bf16[128,2048]{1,0:T(8,128)(2,1)S(1)}, u32[]{:S(2)}, u32[]{:S(2)}) collective-permute-start(bf16[128,2048]{1,0:T(8,128)(2,1)S(1)} %add_convert_fusion.6), channel_id=1, source_target_pairs={{0,8},{8,0},{16,24},{24,16},{1,9},{9,1},{17,25},{25,17},{2,10},{10... | collective-permute-start | bytes 1572872 | tf_op jit(solution)/shard_map/ppermute | solution.py:21
  500.6 57.9 %collective-permute-start.64 = (bf16[128,2048]{1,0:T(8,128)(2,1)S(1)}, bf16[128,2048]{1,0:T(8,128)(2,1)S(1)}, u32[]{:S(2)}, u32[]{:S(2)}) collective-permute-start(bf16[128,2048]{1,0:T(8,128)(2,1)S(1)} %add_convert_fusion.5), channel_id=1, source_target_pairs={{0,16},{8,24},{16,0},{24,8},{1,17},{9,25},{17,1},{25,9},{2,18},{10... | collective-permute-start | bytes 1572872 | tf_op jit(solution)/shard_map/ppermute | solution.py:21
  503.7 19.1 %collective-permute-start.67 = (bf16[256,1408]{1,0:T(8,128)(2,1)S(1)}, bf16[256,1408]{1,0:T(8,128)(2,1)S(1)}, u32[]{:S(2)}, u32[]{:S(2)}) collective-permute-start(bf16[256,1408]{1,0:T(8,128)(2,1)S(1)} %get-tuple-element.195), channel_id=1, source_target_pairs={{0,2},{1,3},{2,0},{3,1},{4,6},{5,7},{6,4},{7,5},{8,10},{9,11},{10,... | collective-permute-start | bytes 2162696 | tf_op jit(solution)/shard_map/ppermute | solution.py:21
  514.2 35.7 %collective-permute-start.66 = (bf16[256,1408]{1,0:T(8,128)(2,1)S(1)}, bf16[256,1408]{1,0:T(8,128)(2,1)S(1)}, u32[]{:S(2)}, u32[]{:S(2)}) collective-permute-start(bf16[256,1408]{1,0:T(8,128)(2,1)S(1)} %get-tuple-element.194), channel_id=1, source_target_pairs={{0,2},{1,3},{2,0},{3,1},{4,6},{5,7},{6,4},{7,5},{8,10},{9,11},{10,... | collective-permute-start | bytes 2162696 | tf_op jit(solution)/shard_map/ppermute | solution.py:21
  524.3 30.3 %collective-permute-start.68 = (bf16[256,1408]{1,0:T(8,128)(2,1)S(1)}, bf16[256,1408]{1,0:T(8,128)(2,1)S(1)}, u32[]{:S(2)}, u32[]{:S(2)}) collective-permute-start(bf16[256,1408]{1,0:T(8,128)(2,1)S(1)} %add_convert_fusion.1), channel_id=1, source_target_pairs={{0,6},{1,7},{2,4},{3,5},{4,2},{5,3},{6,0},{7,1},{8,14},{9,15},{10,... | collective-permute-start | bytes 2162696 | tf_op jit(solution)/shard_map/ppermute | solution.py:21
  556.2 24.8 %collective-permute-start.69 = (bf16[256,1152]{1,0:T(8,128)(2,1)S(1)}, bf16[256,1152]{1,0:T(8,128)(2,1)S(1)}, u32[]{:S(2)}, u32[]{:S(2)}) collective-permute-start(bf16[256,1152]{1,0:T(8,128)(2,1)S(1)} %get-tuple-element.212), channel_id=1, source_target_pairs={{0,8},{8,0},{16,24},{24,16},{1,9},{9,1},{17,25},{25,17},{2,10},{10... | collective-permute-start | bytes 1769480 | tf_op jit(solution)/shard_map/ppermute | solution.py:21
  557.5 25.1 %collective-permute-start.70 = (bf16[256,1152]{1,0:T(8,128)(2,1)S(1)}, bf16[256,1152]{1,0:T(8,128)(2,1)S(1)}, u32[]{:S(2)}, u32[]{:S(2)}) collective-permute-start(bf16[256,1152]{1,0:T(8,128)(2,1)S(1)} %get-tuple-element.212), channel_id=1, source_target_pairs={{0,16},{8,24},{16,0},{24,8},{1,17},{9,25},{17,1},{25,9},{2,18},{10... | collective-permute-start | bytes 1769480 | tf_op jit(solution)/shard_map/ppermute | solution.py:21
  (120 other events, 771.2 us)
Sparse Core Ops, SparseCore 0:
  62.0 115.4 all-gather.4
  179.1 58.0 all-gather.6
  267.9 68.0 reduce-scatter.3
  341.0 67.8 reduce-scatter.5
  411.6 64.1 reduce-scatter.7
  491.6 89.4 all-gather.8
